TPU v7x, 32 devices: a whole 2x2x4 slice. The times are simulated.
32 devices in a mesh: dp: 8 (over y, x, core), etp: 4 (over z).
Axes of the slice: x: 2, y: 2, z: 4, core: 2. Of those that a mesh axis runs over, the one named last changes fastest.
Arguments:
- tokens: bfloat16 [4096, 3072], P(('dp', 'etp')), may hold values from -6 to 6
- out_grad: bfloat16 [4096, 3072], P(('dp', 'etp')), may hold values from -4 to 4
- route_ids: int32 [4096, 2], P(('dp', 'etp')), may hold values from 0 to 7, as said below
- route_prob: bfloat16 [4096], P(('dp', 'etp')), may hold values from 0.19921875 to 1
- w_gate: bfloat16 [3072, 8192], P(None, 'etp'), may hold values from -0.109375 to 0.109375
- w_up: bfloat16 [3072, 8192], P(None, 'etp'), may hold values from -0.109375 to 0.109375
- w_down: bfloat16 [8192, 3072], P('etp'), may hold values from -0.0625 to 0.0625
Outputs:
- grad_tokens: bfloat16 [4096, 3072], P(('dp', 'etp'))
- grad_prob: float32 [4096], P(('dp', 'etp'))
- grad_gate: bfloat16 [3072, 8192], P('dp', 'etp')
- grad_up: bfloat16 [3072, 8192], P('dp', 'etp')
- grad_down: bfloat16 [8192, 3072], P('etp', 'dp')
Inputs may be any that keep to these rules, and one draw needn't show every extreme that they name: `route_ids`: each row names two different experts. In each aligned block of 128 rows (the rows of one device) between 24 and 32 rows name expert 0, and in some block exactly 32 rows do.
All inputs are finite; a program needn't handle non-finite values.
Results may differ from a plain program's by a relative error of at most 0.023.
Values may be sent and summed in bfloat16 or wider, within the bound.
No kernel may reach another device: no remote copies, remote signals or barrier semaphores. Data moves between devices by JAX's collectives and lax.ppermute only.
A program may use at most 256 MiB of HBM per device.

v0:
```python
import jax
import jax.numpy as jnp
from jax import lax
from jax.sharding import PartitionSpec as P

LOC_CAP = 32


def contract_rows(left, right):
    return lax.dot_general(
        left, right, (((0,), (0,)), ((), ())), preferred_element_type=jnp.float32
    )


def contract_cols(left, right):
    return lax.dot_general(
        left, right, (((1,), (1,)), ((), ())), preferred_element_type=jnp.float32
    )


def shards(tokens, out_grad, route_ids, route_prob, w_gate, w_up, w_down):
    tok_rows = tokens.shape[0]
    hidden_width = w_gate.shape[1]
    data_ways = lax.axis_size("dp")
    routed = jnp.logical_or(route_ids[:, 0] == 0, route_ids[:, 1] == 0)
    positions = jnp.arange(tok_rows, dtype=jnp.int32)
    sort_keys = jnp.where(routed, positions, positions + tok_rows)
    packed_order = jnp.argsort(sort_keys)[:LOC_CAP]
    matches = packed_order[:, None] == positions[None, :]
    selector = matches.astype(jnp.bfloat16)
    x_pack = jnp.dot(selector, tokens, preferred_element_type=jnp.float32).astype(jnp.bfloat16)
    dy_pack = jnp.dot(selector, out_grad, preferred_element_type=jnp.float32).astype(jnp.bfloat16)
    row_weight = jnp.where(routed, route_prob, jnp.zeros_like(route_prob))
    w_pack = row_weight[packed_order]
    x_all, dy_all, w_all = (
        lax.all_gather(x_pack, "etp", axis=0, tiled=True),
        lax.all_gather(dy_pack, "etp", axis=0, tiled=True),
        lax.all_gather(w_pack, "etp", axis=0, tiled=True),
    )
    gate_pre = jnp.dot(x_all, w_gate, preferred_element_type=jnp.float32)
    up_pre = jnp.dot(x_all, w_up, preferred_element_type=jnp.float32)
    sig_gate = jax.nn.sigmoid(gate_pre)
    act_gate = gate_pre * sig_gate
    hidden = (act_gate * up_pre).astype(jnp.bfloat16)
    row_scale = w_all.astype(jnp.float32)[:, None]
    scaled = (row_scale * hidden.astype(jnp.float32)).astype(jnp.bfloat16)
    hidden_raw = contract_cols(dy_all, w_down)
    expert_out = jnp.dot(hidden, w_down, preferred_element_type=jnp.float32)
    prob_part = jnp.sum(expert_out * dy_all.astype(jnp.float32), axis=1)
    prob_share = lax.psum_scatter(prob_part, "etp", scatter_dimension=0, tiled=True)
    grad_hidden = row_scale * hidden_raw
    grad_gate_pre = (grad_hidden * up_pre * sig_gate * (1.0 + gate_pre * (1.0 - sig_gate))).astype(
        jnp.bfloat16
    )
    grad_up_pre = (grad_hidden * act_gate).astype(jnp.bfloat16)
    token_share = lax.psum_scatter(
        (contract_cols(grad_gate_pre, w_gate) + contract_cols(grad_up_pre, w_up)).astype(
            jnp.bfloat16
        ),
        "etp",
        scatter_dimension=0,
        tiled=True,
    )
    grad_tokens = contract_rows(selector, token_share).astype(jnp.bfloat16)
    spread_prob = jnp.where(matches, prob_share[:, None], jnp.zeros_like(prob_share)[:, None])
    grad_prob = jnp.sum(spread_prob, axis=0) * routed.astype(jnp.float32)
    gate_up = jnp.concatenate([grad_gate_pre, grad_up_pre], axis=1)
    shares = lax.psum_scatter(
        jnp.concatenate(
            [contract_rows(x_all, gate_up), contract_rows(dy_all, scaled)], axis=1
        ).astype(jnp.bfloat16),
        "dp",
        scatter_dimension=0,
        tiled=True,
    ).astype(jnp.float32)
    shares = shares / data_ways
    grad_gate = shares[:, :hidden_width].astype(jnp.bfloat16)
    grad_up = shares[:, hidden_width : 2 * hidden_width].astype(jnp.bfloat16)
    grad_down = jnp.transpose(shares[:, 2 * hidden_width :]).astype(jnp.bfloat16)
    return (grad_tokens, grad_prob, grad_gate, grad_up, grad_down)


def solution(mesh):
    placed = (
        P(("dp", "etp"), None),
        P(("dp", "etp"), None),
        P(("dp", "etp"), None),
        P(("dp", "etp")),
        P(None, "etp"),
        P(None, "etp"),
        P("etp", None),
    )
    return jax.shard_map(
        shards,
        mesh=mesh,
        in_specs=placed,
        out_specs=(
            P(("dp", "etp"), None),
            P(("dp", "etp")),
            P("dp", "etp"),
            P("dp", "etp"),
            P("etp", "dp"),
        ),
        check_vma=False,
    )
```

profile of v0, /device:TPU:0, one launch (start us, length us, event | category | flops | bytes accessed | tf_op | source)
XLA Modules:
  0.0 387.6 jit_solution(5824851129722296258)
XLA Ops:
  7.2 0.0 reduce-scatter.3.cloned.1.call-start
  7.2 0.8 bitcast_select_fusion.1
  8.0 2.5 sort.17
  10.6 1.3 fusion.11
  12.6 0.7 gather_fusion
  13.3 0.2 dynamic-update-slice
  13.5 13.4 %all-reduce = bf16[128]{0:T(256)(128)(2,1)S(1)} all-reduce(bf16[128]{0:T(256)(128)(2,1)S(1)} %dynamic-update-slice), channel_id=2, replica_groups=mesh['dp'=8,'etp'=4] {'etp'}, use_global_device_ids=true, to_apply=%add | all-reduce | flops 128 | bytes 512
  27.0 0.3 convolution_convert_fusion.3
  27.3 1.4 convolution_convert_fusion.4
  28.7 16.6 %all_gather.10 = bf16[128,3072]{1,0:T(8,128)(2,1)S(1)} all-gather(bf16[32,3072]{1,0:T(8,128)(2,1)S(1)} %convolution_convert_fusion.4), channel_id=1, replica_groups=mesh['dp'=8,'etp'=4] {'etp'}, dimensions={0}, use_global_device_ids=true | all-gather | bytes 983040 | tf_op jit(solution)/shard_map/all_gather | solution.py:37
  45.3 16.3 %all_gather.11 = bf16[128,3072]{1,0:T(8,128)(2,1)S(1)} all-gather(bf16[32,3072]{1,0:T(8,128)(2,1)S(1)} %convolution_convert_fusion.3), channel_id=1, replica_groups=mesh['dp'=8,'etp'=4] {'etp'}, dimensions={0}, use_global_device_ids=true | all-gather | bytes 983040 | tf_op jit(solution)/shard_map/all_gather | solution.py:36
  61.7 6.4 %fusion.12 = f32[128,2048]{1,0:T(8,128)S(1)} fusion(bf16[128,3072]{1,0:T(8,128)(2,1)S(1)} %all_gather.11, bf16[3072,2048]{1,0:T(8,128)(2,1)} %param.11), kind=kOutput, calls=%fused_computation.37 | convolution fusion | flops 1610612736 | bytes 14417920 | tf_op jit(solution)/shard_map/dot_general | solution.py:40
  68.1 10.0 %convolution_multiply_fusion.1 = f32[128,2048]{1,0:T(8,128)} fusion(bf16[128,3072]{1,0:T(8,128)(2,1)S(1)} %all_gather.10, bf16[2048,3072]{1,0:T(8,128)(2,1)} %param.13, f32[128]{0:T(128)S(1)} %convert_element_type.45), kind=kOutput, calls=%fused_computation.11 | convolution fusion | flops 1610874880 | bytes 14418432 | tf_op jit(solution)/shard_map/dot_general | solution.py:16
  78.0 8.4 %multiply_convert_fusion.2 = (bf16[128,2048]{1,0:T(8,128)(2,1)}, bf16[128,2048]{1,0:T(8,128)(2,1)}, bf16[128,2048]{1,0:T(8,128)(2,1)}) fusion(f32[128,2048]{1,0:T(8,128)S(1)} %fusion.12, f32[128,2048]{1,0:T(8,128)} %convolution_multiply_fusion.1, bf16[128,3072]{1,0:T(8,128)(2,1)S(1)} %all_gather.11, bf16[3072,2048]{1,0:T(8,128)(2,1)} %param.12), kind=kOutput, calls=%fused_computation.18 | convolution fusion | flops 1614544896 | bytes 17039360 | tf_op jit(solution)/shard_map/dot_general | solution.py:41
  86.4 5.3 %fusion.13 = f32[128,3072]{1,0:T(8,128)S(1)} fusion(bf16[128,2048]{1,0:T(8,128)(2,1)} %get-tuple-element.33, bf16[3072,2048]{1,0:T(8,128)(2,1)S(1)} %bitcast.26), kind=kOutput, calls=%fused_computation.38 | convolution fusion | flops 1610612736 | bytes 14680064 | tf_op jit(solution)/shard_map/dot_general | solution.py:16
  91.7 10.1 %fusion = bf16[128,3072]{1,0:T(8,128)(2,1)} fusion(f32[128,3072]{1,0:T(8,128)S(1)} %fusion.13, bf16[128,2048]{1,0:T(8,128)(2,1)} %get-tuple-element.34, bf16[3072,2048]{1,0:T(8,128)(2,1)} %param.12), kind=kOutput, calls=%fused_computation.7 | convolution fusion | flops 1611399168 | bytes 15466496 | tf_op jit(solution)/shard_map/dot_general | solution.py:16
  101.8 0.0 reduce-scatter.3.cloned.1.call-update
  101.9 0.0 reduce-scatter.5.cloned.1.call-start
  101.9 13.0 %convolution_convert_fusion = bf16[3072,4096]{1,0:T(8,128)(2,1)} fusion(bf16[128,3072]{1,0:T(8,128)(2,1)S(1)} %all_gather.11, bf16[128,2048]{1,0:T(8,128)(2,1)} %get-tuple-element.34, bf16[128,2048]{1,0:T(8,128)(2,1)} %get-tuple-element.33), kind=kOutput, calls=%fused_computation.2 | convolution fusion | flops 3235905536 | bytes 27000832 | tf_op jit(solution)/shard_map/dot_general | solution.py:10
  114.9 6.6 %convolution_convert_fusion.1 = bf16[3072,2048]{1,0:T(8,128)(2,1)} fusion(bf16[128,3072]{1,0:T(8,128)(2,1)S(1)} %all_gather.10, bf16[128,2048]{1,0:T(8,128)(2,1)S(1)} %copy-done.2, f32[128]{0:T(128)S(1)} %convert_element_type.45), kind=kOutput, calls=%fused_computation.3 | convolution fusion | flops 1617690624 | bytes 13894144 | tf_op jit(solution)/shard_map/dot_general | solution.py:10
  121.5 25.7 %pad_maximum_fusion = bf16[3072,6144]{1,0:T(8,128)(2,1)} fusion(bf16[3072,2048]{1,0:T(8,128)(2,1)} %convolution_convert_fusion.1, bf16[3072,4096]{1,0:T(8,128)(2,1)} %convolution_convert_fusion), kind=kLoop, calls=%fused_computation.1 | loop fusion | flops 75497472 | bytes 75497472 | tf_op jit(solution)/shard_map/concatenate | solution.py:69
  147.1 0.0 reduce-scatter.5.cloned.1.call-update
  147.8 6.5 %fusion.1 = f32[128]{0:T(128)S(1)} fusion(bf16[128,3072]{1,0:T(8,128)(2,1)S(1)} %all_gather.10, bf16[128,2048]{1,0:T(8,128)(2,1)S(1)} %copy-done.2, bf16[2048,3072]{1,0:T(8,128)(2,1)} %param.13), kind=kOutput, calls=%fused_computation.13 | convolution fusion | flops 1611792256 | bytes 13894144 | tf_op jit(solution)/shard_map/dot_general | solution.py:48
  154.4 11.9 %all-reduce.1 = f32[128]{0:T(128)S(1)} all-reduce(f32[128]{0:T(128)S(1)} %fusion.1), channel_id=4, replica_groups=mesh['dp'=8,'etp'=4] {'etp'}, use_global_device_ids=true, to_apply=%region_3.4.clone | all-reduce | flops 128 | bytes 1024
  166.3 0.1 dynamic-slice.2
  166.4 0.1 select_reduce_fusion
  166.5 0.5 bitcast_select_fusion
  167.0 2.3 convolution_convert_fusion.2
  169.3 204.4 %reduce-scatter.5.cloned.1.call-done = bf16[384,6144]{1,0:T(8,128)(2,1)} async-done(((bf16[3072,6144]{1,0:T(8,128)(2,1)}), bf16[384,6144]{1,0:T(8,128)(2,1)}) %reduce-scatter.5.cloned.1.call-update) | async-done | bytes 4718608 | tf_op jit(solution)/shard_map/reduce_scatter | solution.py:68
  373.8 3.3 multiply_convert_fusion
  377.1 2.1 slice_bitcast_fusion
  379.2 1.6 copy.19
  (20 shorter events, 0.1 us)
Async XLA Ops:
  7.2 19.8 %copy-start = (bf16[128,3072]{1,0:T(8,128)(2,1)S(1)}, bf16[128,3072]{1,0:T(8,128)(2,1)}, u32[]{:S(2)}) copy-start(bf16[128,3072]{1,0:T(8,128)(2,1)} %param.7) | copy-start | bytes 2359300
  7.2 159.8 %reduce-scatter.3.cloned.1.call-start = ((), (), s32[]{:S(2)}) async-start(), calls=%async_computation.2 | async-start | bytes 983040 | tf_op jit(solution)/shard_map/reduce_scatter | solution.py:56
  68.0 18.4 %slice-start = ((s8[12582912]{0:T(1024)(128)(4,1)}), s8[4194304]{0:T(1024)(128)(4,1)S(1)}, s32[]{:S(2)}) async-start(s8[12582912]{0:T(1024)(128)(4,1)} %bitcast.25), calls=%async_computation.4 | async-start | bytes 8388608
  68.0 18.4 %slice-start.1 = ((s8[12582912]{0:T(1024)(128)(4,1)}), s8[4194304]{0:T(1024)(128)(4,1)S(1)}, s32[]{:S(2)}) async-start(s8[12582912]{0:T(1024)(128)(4,1)} %bitcast.25), calls=%async_computation.5 | async-start | bytes 8388608
  78.0 8.4 %slice-start.2 = ((s8[12582912]{0:T(1024)(128)(4,1)}), s8[4194304]{0:T(1024)(128)(4,1)S(1)}, s32[]{:S(2)}) async-start(s8[12582912]{0:T(1024)(128)(4,1)} %bitcast.25), calls=%async_computation.6 | async-start | bytes 8388608
  101.9 13.1 %copy-start.2 = (bf16[128,2048]{1,0:T(8,128)(2,1)S(1)}, bf16[128,2048]{1,0:T(8,128)(2,1)}, u32[]{:S(2)}) copy-start(bf16[128,2048]{1,0:T(8,128)(2,1)} %get-tuple-element.32) | copy-start | bytes 1572868
  101.9 271.9 %reduce-scatter.5.cloned.1.call-start = ((), (), s32[]{:S(2)}) async-start(), calls=%async_computation.3 | async-start | bytes 42467328 | tf_op jit(solution)/shard_map/reduce_scatter | solution.py:68
  147.8 233.0 %copy-start.1 = (bf16[128,3072]{1,0:T(8,128)(2,1)S(1)}, bf16[128,3072]{1,0:T(8,128)(2,1)}, u32[]{:S(2)}) copy-start(bf16[128,3072]{1,0:T(8,128)(2,1)} %param.7) | copy-start | bytes 2359300
Sparse Core Ops, SparseCore 0:
  102.0 24.5 reduce-scatter.2
  147.3 226.4 reduce-scatter.4
where the time goes:
time: 388 us
  waiting for transfers between devices  204 us (53%)
  matrix products  70.2 us (18%)
  blocking collectives  58.4 us (15%)
  other arithmetic  33 us (9%)
  between operations  15.5 us (4%)
  local copies, waits for them, and re-layouts  6.06 us (2%)
    reduce_scatter x1, waiting for transfers between devices, shards(): lax.psum_scatter(jnp.concatenate([contract_rows(x_all, gate_up), contract...  204 us
    concatenate x1, other arithmetic, shards(): jnp.concatenate([contract_rows(x_all, gate_up), contract_rows(dy_all, sca...  25.7 us
    unnamed x2, blocking collectives  25.4 us
    dot_general x3, matrix products, contract_cols(): lax.dot_general(left, right, (((1,), (1,)), ((), ())), preferred_element_...  25.3 us
    dot_general x3, matrix products, contract_rows(): lax.dot_general(left, right, (((0,), (0,)), ((), ())), preferred_element_...  21.9 us
    all_gather x1, blocking collectives, shards(): lax.all_gather(dy_pack, 'etp', axis=0, tiled=True)  16.6 us
    all_gather x1, blocking collectives, shards(): lax.all_gather(x_pack, 'etp', axis=0, tiled=True)  16.3 us
    dot_general x1, matrix products, shards(): up_pre = jnp.dot(x_all, w_up, preferred_element_type=jnp.float32)  8.41 us
  transfers between devices with their start and end apart: 2, of which 1 were waited for; matrix products, arithmetic and copies ran while one was open for 14% of the time, Pallas kernels for 0%

commit v1 on v0

v1 whole, which is shorter than its diff:
```python
import jax
import jax.numpy as jnp
from jax import lax
from jax.sharding import PartitionSpec as P

LOC_CAP = 32
LANES = 128


def contract_rows(left, right):
    return lax.dot_general(
        left, right, (((0,), (0,)), ((), ())), preferred_element_type=jnp.float32
    )


def contract_cols(left, right):
    return lax.dot_general(
        left, right, (((1,), (1,)), ((), ())), preferred_element_type=jnp.float32
    )


def shift(block, step):
    ways = lax.axis_size("etp")
    return lax.ppermute(block, "etp", [(i, (i + step) % ways) for i in range(ways)])


def exchange(block, bit):
    ways = lax.axis_size("dp")
    return lax.ppermute(block, "dp", [(i, i ^ bit) for i in range(ways)])


def ring_blocks(block):
    ways = lax.axis_size("etp")
    return [block] + [shift(block, step) for step in range(1, ways)]


def dp_gather(block):
    ways = lax.axis_size("dp")
    bits = [1 << k for k in range(ways.bit_length() - 1)]
    half = block.shape[1] // 2
    halves = []
    for part, order in (
        (block[:, :half], bits[1:] + bits[:1]),
        (block[:, half:], bits[:0:-1] + bits[:1]),
    ):
        held = {0: part}
        for bit in order:
            keys = sorted(held)
            sent = jnp.concatenate([held[key] for key in keys], axis=0)
            got = exchange(sent, bit)
            rows = part.shape[0]
            for at, key in enumerate(keys):
                held[key ^ bit] = got[at * rows : (at + 1) * rows]
        halves.append(jnp.concatenate([held[key] for key in range(ways)], axis=0))
    return halves


def dp_slices(rows):
    ways = lax.axis_size("dp")
    me = lax.axis_index("dp")
    every = lax.all_to_all(rows, "dp", split_axis=1, concat_axis=0, tiled=True)
    every = every.reshape(ways, rows.shape[0], -1)
    return jnp.concatenate(
        [lax.dynamic_index_in_dim(every, me ^ k, 0, keepdims=False) for k in range(ways)], axis=0
    )


def shards(tokens, out_grad, route_ids, route_prob, w_gate, w_up, w_down):
    tok_rows = tokens.shape[0]
    width = tokens.shape[1]
    data_ways = lax.axis_size("dp")
    etp_ways = lax.axis_size("etp")
    routed = jnp.logical_or(route_ids[:, 0] == 0, route_ids[:, 1] == 0)
    positions = jnp.arange(tok_rows, dtype=jnp.int32)
    before = (positions[:, None] <= positions[None, :]) & routed[:, None]
    slot = jnp.sum(before.astype(jnp.int32), axis=0) - 1
    matches = (slot[None, :] == jnp.arange(LOC_CAP, dtype=jnp.int32)[:, None]) & routed[None, :]
    selector = matches.astype(jnp.bfloat16)
    x_pack = jnp.dot(selector, tokens, preferred_element_type=jnp.float32).astype(jnp.bfloat16)
    dy_pack = jnp.dot(selector, out_grad, preferred_element_type=jnp.float32).astype(jnp.bfloat16)
    w_pack = jnp.sum(
        jnp.where(matches, route_prob.astype(jnp.float32)[None, :], 0.0), axis=1
    ).astype(jnp.bfloat16)
    x_ext = jnp.concatenate(
        [x_pack, jnp.broadcast_to(w_pack[:, None], (LOC_CAP, LANES))], axis=1
    )
    x_ext = jnp.concatenate(ring_blocks(x_ext), axis=0)
    dy_all = jnp.concatenate(ring_blocks(dy_pack), axis=0)
    x_all = x_ext[:, :width]
    row_scale = x_ext[:, width : width + 1].astype(jnp.float32)

    gate_pre = jnp.dot(x_all, w_gate, preferred_element_type=jnp.float32)
    up_pre = jnp.dot(x_all, w_up, preferred_element_type=jnp.float32)
    sig_gate = jax.nn.sigmoid(gate_pre)
    act_gate = gate_pre * sig_gate
    hidden = (act_gate * up_pre).astype(jnp.bfloat16)
    scaled = (row_scale * hidden.astype(jnp.float32)).astype(jnp.bfloat16)
    scaled_all = dp_gather(scaled)
    x_slice = dp_slices(x_all)

    hidden_raw = contract_cols(dy_all, w_down)
    grad_hidden = row_scale * hidden_raw
    grad_gate_pre = (grad_hidden * up_pre * sig_gate * (1.0 + gate_pre * (1.0 - sig_gate))).astype(
        jnp.bfloat16
    )
    grad_up_pre = (grad_hidden * act_gate).astype(jnp.bfloat16)
    gate_all = dp_gather(grad_gate_pre)
    up_all = dp_gather(grad_up_pre)
    dy_slice = dp_slices(dy_all)

    prob_part = jnp.sum(hidden.astype(jnp.float32) * hidden_raw, axis=1, keepdims=True)
    prob_hi = prob_part.astype(jnp.bfloat16)
    prob_rest = prob_part - prob_hi.astype(jnp.float32)
    prob_mid = prob_rest.astype(jnp.bfloat16)
    prob_lo = (prob_rest - prob_mid.astype(jnp.float32)).astype(jnp.bfloat16)
    token_part = (
        contract_cols(grad_gate_pre, w_gate) + contract_cols(grad_up_pre, w_up)
    ).astype(jnp.bfloat16)
    token_ext = jnp.concatenate(
        [token_part, prob_hi, prob_mid, prob_lo, jnp.zeros((token_part.shape[0], LANES - 3), jnp.bfloat16)],
        axis=1,
    )
    share = token_ext[:LOC_CAP].astype(jnp.float32)
    for step in range(1, etp_ways):
        share = share + shift(token_ext[step * LOC_CAP : (step + 1) * LOC_CAP], -step).astype(jnp.float32)
    token_share = share[:, :width].astype(jnp.bfloat16)
    prob_share = share[:, width] + share[:, width + 1] + share[:, width + 2]
    spread_prob = jnp.where(matches, prob_share[:, None], jnp.zeros_like(prob_share)[:, None])
    grad_prob = jnp.sum(spread_prob, axis=0)
    grad_tokens = contract_rows(selector, token_share).astype(jnp.bfloat16)

    inv = 1.0 / data_ways
    grad_down = jnp.concatenate(
        [(contract_rows(part, dy_slice) * inv).astype(jnp.bfloat16) for part in scaled_all], axis=0
    )
    grad_gate, grad_up = (
        jnp.concatenate(
            [(contract_rows(x_slice, part) * inv).astype(jnp.bfloat16) for part in parts], axis=1
        )
        for parts in (gate_all, up_all)
    )
    return (grad_tokens, grad_prob, grad_gate, grad_up, grad_down)


def solution(mesh):
    placed = (
        P(("dp", "etp"), None),
        P(("dp", "etp"), None),
        P(("dp", "etp"), None),
        P(("dp", "etp")),
        P(None, "etp"),
        P(None, "etp"),
        P("etp", None),
    )
    return jax.shard_map(
        shards,
        mesh=mesh,
        in_specs=placed,
        out_specs=(
            P(("dp", "etp"), None),
            P(("dp", "etp")),
            P("dp", "etp"),
            P("dp", "etp"),
            P("etp", "dp"),
        ),
        check_vma=False,
    )
```

time: 388 us -> 183 us (0.47)
  the two profiles are of different devices: /device:TPU:0 before, /device:TPU:25 now
where the time goes in v1:
time: 183 us; the launch traced here: 182 us
  starting transfers between devices  48.7 us (27%)
  waiting for transfers between devices  44 us (24%)
  matrix products  40.6 us (22%)
  other arithmetic  24.6 us (13%)
  local copies, waits for them, and re-layouts  22.9 us (13%)
    dot_general x3, matrix products, contract_cols(): lax.dot_general(left, right, (((1,), (1,)), ((), ())), preferred_element_...  25.8 us
    ppermute x18, waiting for transfers between devices, exchange(): return lax.ppermute(block, 'dp', [(i, i ^ bit) for i in range(ways)])  25.3 us
    all_to_all x2, starting transfers between devices, dp_slices(): every = lax.all_to_all(rows, 'dp', split_axis=1, concat_axis=0, tiled=True)  18.9 us
    ppermute x9, waiting for transfers between devices, shift(): lax.ppermute(block, 'etp', [(i, (i + step) % ways) for i in range(ways)])  18.7 us
    ppermute x18, starting transfers between devices, exchange(): return lax.ppermute(block, 'dp', [(i, i ^ bit) for i in range(ways)])  16 us
    concatenate x12, other arithmetic, dp_gather(): sent = jnp.concatenate([held[key] for key in keys], axis=0)  14.4 us
    ppermute x9, starting transfers between devices, shift(): lax.ppermute(block, 'etp', [(i, (i + step) % ways) for i in range(ways)])  13.8 us
    unnamed x111, local copies, waits for them, and re-layouts  12.7 us
  transfers between devices with their start and end apart: 29, of which 6 were waited for; matrix products, arithmetic and copies ran while one was open for 44% of the time, Pallas kernels for 0%

profile of v1, /device:TPU:25, one launch (start us, length us, event | category | flops | bytes accessed | tf_op | source)
XLA Modules:
  0.0 182.3 jit_solution(1127567117484136803)
XLA Ops:
  2.3 3.1 %collective-permute-start.3 = (bf16[32,3072]{1,0:T(8,128)(2,1)S(1)}, bf16[32,3072]{1,0:T(8,128)(2,1)S(1)}, u32[]{:S(2)}, u32[]{:S(2)}) collective-permute-start(bf16[32,3072]{1,0:T(8,128)(2,1)S(1)} %convolution_convert_fusion.1), channel_id=1, source_target_pairs={{0,1},{1,2},{2,3},{3,0},{4,5},{5,6},{6,7},{7,4},{8,9},{9,10},{10,1... | collective-permute-start | bytes 589832 | tf_op jit(solution)/shard_map/ppermute | solution.py:24
  6.1 1.4 convolution_convert_fusion.2
  9.8 2.3 %collective-permute-start = (bf16[32,3200]{1,0:T(8,128)(2,1)}, bf16[32,3200]{1,0:T(8,128)(2,1)}, u32[]{:S(2)}, u32[]{:S(2)}) collective-permute-start(bf16[32,3200]{1,0:T(8,128)(2,1)} %pad_maximum_fusion.20), channel_id=1, source_target_pairs={{0,1},{1,2},{2,3},{3,0},{4,5},{5,6},{6,7},{7,4},{8,9},{9,10},{10,1... | collective-permute-start | bytes 614408 | tf_op jit(solution)/shard_map/ppermute | solution.py:24
  12.1 5.6 %collective-permute-done.4 = bf16[32,3072]{1,0:T(8,128)(2,1)S(1)} collective-permute-done((bf16[32,3072]{1,0:T(8,128)(2,1)S(1)}, bf16[32,3072]{1,0:T(8,128)(2,1)S(1)}, u32[]{:S(2)}, u32[]{:S(2)}) %collective-permute-start.4) | collective-permute-done | bytes 196640 | tf_op jit(solution)/shard_map/ppermute | solution.py:24
  18.8 13.7 %all-to-all-start.1 = ((bf16[128,8,384]{2,0,1:T(8,128)(2,1)}), bf16[128,8,384]{2,0,1:T(8,128)(2,1)S(1)}, u32[]{:S(2)}, u32[]{:S(2)}) async-start(bf16[128,8,384]{2,0,1:T(8,128)(2,1)} %bitcast.76), calls=%async_computation.1 | async-start | bytes 1572864 | tf_op jit(solution)/shard_map/all_to_all | solution.py:61
  32.4 10.3 %fusion.17 = f32[128,2048]{1,0:T(8,128)} fusion(bf16[2048,3072]{1,0:T(8,128)(2,1)} %param.13, bf16[32,3072]{1,0:T(8,128)(2,1)} %copy-done.23, bf16[32,3072]{1,0:T(8,128)(2,1)} %copy-done.24, bf16[32,3072]{1,0:T(8,128)(2,1)} %copy-done.25, bf16[32,3072]{1,0:T(8,128)(2,1)} %copy-done.20), kind=kOutput, calls=%fused_computation.132 | convolution fusion | flops 1613758464 | bytes 14417920 | tf_op jit(solution)/shard_map/dot_general | solution.py:17
  44.1 1.8 fusion.25
  45.8 1.6 convert_reduce_fusion
  48.1 3.5 %fusion.2 = (bf16[128,2048]{1,0:T(8,128)(2,1)}, bf16[128,2048]{1,0:T(8,128)(2,1)S(1)}, bf16[128,2048]{1,0:T(8,128)(2,1)S(1)}, bf16[128,2048]{1,0:T(8,128)(2,1)S(1)}) fusion(f32[128]{0:T(128)S(1)} %convert_reduce_fusion, f32[128,2048]{1,0:T(8,128)S(1)} %fusion.25, f32[128,2048]{1,0:T(8,128)S(1)} %copy-done.19, bf16[128,3072]{1,0:T(8,128)(2,1)S(1)} %pad_maximum_fusion.9, ...), kind=kOutput, calls=%fused_computation.17 | convolution fusion | flops 1615593472 | bytes 17564160 | tf_op jit(solution)/shard_map/dot_general | solution.py:93
  51.9 5.4 %fusion.26 = f32[128,3072]{1,0:T(8,128)} fusion(bf16[128,2048]{1,0:T(8,128)(2,1)S(1)} %get-tuple-element.7, bf16[3072,2048]{1,0:T(8,128)(2,1)S(1)} %copy-done.2), kind=kOutput, calls=%fused_computation.141 | convolution fusion | flops 1610612736 | bytes 14680064 | tf_op jit(solution)/shard_map/dot_general | solution.py:17
  59.3 10.1 %fusion = bf16[128,3072]{1,0:T(8,128)(2,1)} fusion(f32[128,3072]{1,0:T(8,128)S(1)} %copy-done.3, bf16[128,2048]{1,0:T(8,128)(2,1)} %copy-done.18, bf16[3072,2048]{1,0:T(8,128)(2,1)} %param.12), kind=kOutput, calls=%fused_computation.1 | convolution fusion | flops 1611399168 | bytes 15466496 | tf_op jit(solution)/shard_map/dot_general | solution.py:17
  71.2 6.7 %collective-permute-start.7 = (bf16[32,3200]{1,0:T(8,128)(2,1)S(1)}, bf16[32,3200]{1,0:T(8,128)(2,1)S(1)}, u32[]{:S(2)}, u32[]{:S(2)}) collective-permute-start(bf16[32,3200]{1,0:T(8,128)(2,1)S(1)} %get-tuple-element.11), channel_id=1, source_target_pairs={{0,2},{1,3},{2,0},{3,1},{4,6},{5,7},{6,4},{7,5},{8,10},{9,11},{10,... | collective-permute-start | bytes 614408 | tf_op jit(solution)/shard_map/ppermute | solution.py:24
  78.8 1.4 collective-permute-start.12
  83.2 13.0 %collective-permute-done.7 = bf16[32,3200]{1,0:T(8,128)(2,1)S(1)} collective-permute-done((bf16[32,3200]{1,0:T(8,128)(2,1)S(1)}, bf16[32,3200]{1,0:T(8,128)(2,1)S(1)}, u32[]{:S(2)}, u32[]{:S(2)}) %collective-permute-start.7) | collective-permute-done | bytes 204832 | tf_op jit(solution)/shard_map/ppermute | solution.py:24
  98.5 1.3 convolution_convert_fusion
  100.6 5.2 %all-to-all-start = ((bf16[128,8,384]{2,0,1:T(8,128)(2,1)}), bf16[128,8,384]{2,0,1:T(8,128)(2,1)S(1)}, u32[]{:S(2)}, u32[]{:S(2)}) async-start(bf16[128,8,384]{2,0,1:T(8,128)(2,1)} %bitcast.77), calls=%async_computation | async-start | bytes 1572864 | tf_op jit(solution)/shard_map/all_to_all | solution.py:61
  105.8 1.5 collective-permute-start.21
  107.3 1.8 pad_maximum_fusion.15
  109.2 1.8 pad_maximum_fusion.14
  111.0 1.4 collective-permute-start.10
  112.4 1.8 pad_maximum_fusion.17
  115.4 1.8 pad_maximum_fusion.16
  117.4 1.8 pad_maximum_fusion.19
  119.2 3.2 %collective-permute-done.21 = bf16[128,1024]{1,0:T(8,128)(2,1)S(1)} collective-permute-done((bf16[128,1024]{1,0:T(8,128)(2,1)}, bf16[128,1024]{1,0:T(8,128)(2,1)S(1)}, u32[]{:S(2)}, u32[]{:S(2)}) %collective-permute-start.21) | collective-permute-done | bytes 262176 | tf_op jit(solution)/shard_map/ppermute | solution.py:29
  124.1 9.6 %collective-permute-done.13 = bf16[256,1024]{1,0:T(8,128)(2,1)} collective-permute-done((bf16[256,1024]{1,0:T(8,128)(2,1)}, bf16[256,1024]{1,0:T(8,128)(2,1)}, u32[]{:S(2)}, u32[]{:S(2)}) %collective-permute-start.13) | collective-permute-done | bytes 524320 | tf_op jit(solution)/shard_map/ppermute | solution.py:29
  136.1 1.7 collective-permute-start.14
  138.9 6.0 %collective-permute-done.19 = bf16[256,1024]{1,0:T(8,128)(2,1)} collective-permute-done((bf16[256,1024]{1,0:T(8,128)(2,1)}, bf16[256,1024]{1,0:T(8,128)(2,1)}, u32[]{:S(2)}, u32[]{:S(2)}) %collective-permute-start.19) | collective-permute-done | bytes 524320 | tf_op jit(solution)/shard_map/ppermute | solution.py:29
  144.9 1.3 collective-permute-start.11
  149.6 6.5 %collective-permute-done.25 = bf16[256,1024]{1,0:T(8,128)(2,1)} collective-permute-done((bf16[256,1024]{1,0:T(8,128)(2,1)}, bf16[256,1024]{1,0:T(8,128)(2,1)}, u32[]{:S(2)}, u32[]{:S(2)}) %collective-permute-start.25) | collective-permute-done | bytes 524320 | tf_op jit(solution)/shard_map/ppermute | solution.py:29
  175.5 1.3 multiply_convert_fusion
  177.2 1.3 multiply_convert_fusion.1
  181.0 1.3 pad_maximum_fusion.2
  (205 shorter events, 50.5 us)
Async XLA Ops:
  2.0 16.7 %copy-start.20 = (bf16[32,3072]{1,0:T(8,128)(2,1)}, bf16[32,3072]{1,0:T(8,128)(2,1)S(1)}, u32[]{:S(2)}) copy-start(bf16[32,3072]{1,0:T(8,128)(2,1)S(1)} %convolution_convert_fusion.1) | copy-start | bytes 589828
  2.0 7.8 %collective-permute-start.5 = (bf16[32,3072]{1,0:T(8,128)(2,1)S(1)}, bf16[32,3072]{1,0:T(8,128)(2,1)S(1)}, u32[]{:S(2)}, u32[]{:S(2)}) collective-permute-start(bf16[32,3072]{1,0:T(8,128)(2,1)S(1)} %convolution_convert_fusion.1), channel_id=1, source_target_pairs={{0,3},{1,0},{2,1},{3,2},{4,7},{5,4},{6,5},{7,6},{8,11},{9,8},{10,9... | collective-permute-start | bytes 589832 | tf_op jit(solution)/shard_map/ppermute | solution.py:24
  2.3 15.5 %collective-permute-start.4 = (bf16[32,3072]{1,0:T(8,128)(2,1)S(1)}, bf16[32,3072]{1,0:T(8,128)(2,1)S(1)}, u32[]{:S(2)}, u32[]{:S(2)}) collective-permute-start(bf16[32,3072]{1,0:T(8,128)(2,1)S(1)} %convolution_convert_fusion.1), channel_id=1, source_target_pairs={{0,2},{1,3},{2,0},{3,1},{4,6},{5,7},{6,4},{7,5},{8,10},{9,11},{10,... | collective-permute-start | bytes 589832 | tf_op jit(solution)/shard_map/ppermute | solution.py:24
  2.3 15.5 %collective-permute-start.3 = (bf16[32,3072]{1,0:T(8,128)(2,1)S(1)}, bf16[32,3072]{1,0:T(8,128)(2,1)S(1)}, u32[]{:S(2)}, u32[]{:S(2)}) collective-permute-start(bf16[32,3072]{1,0:T(8,128)(2,1)S(1)} %convolution_convert_fusion.1), channel_id=1, source_target_pairs={{0,1},{1,2},{2,3},{3,0},{4,5},{5,6},{6,7},{7,4},{8,9},{9,10},{10,1... | collective-permute-start | bytes 589832 | tf_op jit(solution)/shard_map/ppermute | solution.py:24
  8.3 34.5 %collective-permute-start.2 = (bf16[32,3200]{1,0:T(8,128)(2,1)}, bf16[32,3200]{1,0:T(8,128)(2,1)S(1)}, u32[]{:S(2)}, u32[]{:S(2)}) collective-permute-start(bf16[32,3200]{1,0:T(8,128)(2,1)} %pad_maximum_fusion.20), channel_id=1, source_target_pairs={{0,3},{1,0},{2,1},{3,2},{4,7},{5,4},{6,5},{7,6},{8,11},{9,8},{10,9... | collective-permute-start | bytes 614408 | tf_op jit(solution)/shard_map/ppermute | solution.py:24
  8.6 34.2 %collective-permute-start.1 = (bf16[32,3200]{1,0:T(8,128)(2,1)}, bf16[32,3200]{1,0:T(8,128)(2,1)}, u32[]{:S(2)}, u32[]{:S(2)}) collective-permute-start(bf16[32,3200]{1,0:T(8,128)(2,1)} %pad_maximum_fusion.20), channel_id=1, source_target_pairs={{0,2},{1,3},{2,0},{3,1},{4,6},{5,7},{6,4},{7,5},{8,10},{9,11},{10,... | collective-permute-start | bytes 614408 | tf_op jit(solution)/shard_map/ppermute | solution.py:24
  9.8 32.9 %collective-permute-start = (bf16[32,3200]{1,0:T(8,128)(2,1)}, bf16[32,3200]{1,0:T(8,128)(2,1)}, u32[]{:S(2)}, u32[]{:S(2)}) collective-permute-start(bf16[32,3200]{1,0:T(8,128)(2,1)} %pad_maximum_fusion.20), channel_id=1, source_target_pairs={{0,1},{1,2},{2,3},{3,0},{4,5},{5,6},{6,7},{7,4},{8,9},{9,10},{10,1... | collective-permute-start | bytes 614408 | tf_op jit(solution)/shard_map/ppermute | solution.py:24
  18.8 81.9 %all-to-all-start.1 = ((bf16[128,8,384]{2,0,1:T(8,128)(2,1)}), bf16[128,8,384]{2,0,1:T(8,128)(2,1)S(1)}, u32[]{:S(2)}, u32[]{:S(2)}) async-start(bf16[128,8,384]{2,0,1:T(8,128)(2,1)} %bitcast.76), calls=%async_computation.1 | async-start | bytes 1572864 | tf_op jit(solution)/shard_map/all_to_all | solution.py:61
  58.2 20.6 %copy-start.16 = (bf16[128,1024]{1,0:T(8,128)(2,1)}, bf16[128,1024]{1,0:T(8,128)(2,1)S(1)}, u32[]{:S(2)}) copy-start(bf16[128,1024]{1,0:T(8,128)(2,1)S(1)} %get-tuple-element.27) | copy-start | bytes 786436
  71.1 11.3 %collective-permute-start.8 = (bf16[32,3200]{1,0:T(8,128)(2,1)S(1)}, bf16[32,3200]{1,0:T(8,128)(2,1)S(1)}, u32[]{:S(2)}, u32[]{:S(2)}) collective-permute-start(bf16[32,3200]{1,0:T(8,128)(2,1)S(1)} %get-tuple-element.10), channel_id=1, source_target_pairs={{0,1},{1,2},{2,3},{3,0},{4,5},{5,6},{6,7},{7,4},{8,9},{9,10},{10,1... | collective-permute-start | bytes 614408 | tf_op jit(solution)/shard_map/ppermute | solution.py:24
  71.2 25.1 %collective-permute-start.7 = (bf16[32,3200]{1,0:T(8,128)(2,1)S(1)}, bf16[32,3200]{1,0:T(8,128)(2,1)S(1)}, u32[]{:S(2)}, u32[]{:S(2)}) collective-permute-start(bf16[32,3200]{1,0:T(8,128)(2,1)S(1)} %get-tuple-element.11), channel_id=1, source_target_pairs={{0,2},{1,3},{2,0},{3,1},{4,6},{5,7},{6,4},{7,5},{8,10},{9,11},{10,... | collective-permute-start | bytes 614408 | tf_op jit(solution)/shard_map/ppermute | solution.py:24
  77.9 19.4 %collective-permute-start.6 = (bf16[32,3200]{1,0:T(8,128)(2,1)S(1)}, bf16[32,3200]{1,0:T(8,128)(2,1)S(1)}, u32[]{:S(2)}, u32[]{:S(2)}) collective-permute-start(bf16[32,3200]{1,0:T(8,128)(2,1)S(1)} %get-tuple-element.9), channel_id=1, source_target_pairs={{0,3},{1,0},{2,1},{3,2},{4,7},{5,4},{6,5},{7,6},{8,11},{9,8},{10,9... | collective-permute-start | bytes 614408 | tf_op jit(solution)/shard_map/ppermute | solution.py:24
  78.8 27.0 %collective-permute-start.12 = (bf16[128,1024]{1,0:T(8,128)(2,1)S(1)}, bf16[128,1024]{1,0:T(8,128)(2,1)S(1)}, u32[]{:S(2)}, u32[]{:S(2)}) collective-permute-start(bf16[128,1024]{1,0:T(8,128)(2,1)S(1)} %get-tuple-element.27), channel_id=1, source_target_pairs={{0,16},{4,20},{8,24},{12,28},{16,0},{20,4},{24,8},{28,12},{1,17},{... | collective-permute-start | bytes 786440 | tf_op jit(solution)/shard_map/ppermute | solution.py:29
  80.2 28.9 %collective-permute-start.9 = (bf16[128,1024]{1,0:T(8,128)(2,1)}, bf16[128,1024]{1,0:T(8,128)(2,1)S(1)}, u32[]{:S(2)}, u32[]{:S(2)}) collective-permute-start(bf16[128,1024]{1,0:T(8,128)(2,1)} %get-tuple-element.24), channel_id=1, source_target_pairs={{0,8},{4,12},{8,0},{12,4},{16,24},{20,28},{24,16},{28,20},{1,9},{5... | collective-permute-start | bytes 786440 | tf_op jit(solution)/shard_map/ppermute | solution.py:29
  82.5 28.6 %collective-permute-start.18 = (bf16[128,1024]{1,0:T(8,128)(2,1)}, bf16[128,1024]{1,0:T(8,128)(2,1)S(1)}, u32[]{:S(2)}, u32[]{:S(2)}) collective-permute-start(bf16[128,1024]{1,0:T(8,128)(2,1)} %get-tuple-element.21), channel_id=1, source_target_pairs={{0,16},{4,20},{8,24},{12,28},{16,0},{20,4},{24,8},{28,12},{1,17},{... | collective-permute-start | bytes 786440 | tf_op jit(solution)/shard_map/ppermute | solution.py:29
  96.3 17.9 %collective-permute-start.15 = (bf16[128,1024]{1,0:T(8,128)(2,1)}, bf16[128,1024]{1,0:T(8,128)(2,1)S(1)}, u32[]{:S(2)}, u32[]{:S(2)}) collective-permute-start(bf16[128,1024]{1,0:T(8,128)(2,1)} %get-tuple-element.18), channel_id=1, source_target_pairs={{0,8},{4,12},{8,0},{12,4},{16,24},{20,28},{24,16},{28,20},{1,9},{5... | collective-permute-start | bytes 786440 | tf_op jit(solution)/shard_map/ppermute | solution.py:29
  97.2 19.9 %collective-permute-start.24 = (bf16[128,1024]{1,0:T(8,128)(2,1)}, bf16[128,1024]{1,0:T(8,128)(2,1)S(1)}, u32[]{:S(2)}, u32[]{:S(2)}) collective-permute-start(bf16[128,1024]{1,0:T(8,128)(2,1)} %get-tuple-element.15), channel_id=1, source_target_pairs={{0,16},{4,20},{8,24},{12,28},{16,0},{20,4},{24,8},{28,12},{1,17},{... | collective-permute-start | bytes 786440 | tf_op jit(solution)/shard_map/ppermute | solution.py:29
  100.6 22.9 %all-to-all-start = ((bf16[128,8,384]{2,0,1:T(8,128)(2,1)}), bf16[128,8,384]{2,0,1:T(8,128)(2,1)S(1)}, u32[]{:S(2)}, u32[]{:S(2)}) async-start(bf16[128,8,384]{2,0,1:T(8,128)(2,1)} %bitcast.77), calls=%async_computation | async-start | bytes 1572864 | tf_op jit(solution)/shard_map/all_to_all | solution.py:61
  105.8 16.6 %collective-permute-start.21 = (bf16[128,1024]{1,0:T(8,128)(2,1)}, bf16[128,1024]{1,0:T(8,128)(2,1)S(1)}, u32[]{:S(2)}, u32[]{:S(2)}) collective-permute-start(bf16[128,1024]{1,0:T(8,128)(2,1)} %get-tuple-element.12), channel_id=1, source_target_pairs={{0,8},{4,12},{8,0},{12,4},{16,24},{20,28},{24,16},{28,20},{1,9},{5... | collective-permute-start | bytes 786440 | tf_op jit(solution)/shard_map/ppermute | solution.py:29
  109.1 24.6 %collective-permute-start.13 = (bf16[256,1024]{1,0:T(8,128)(2,1)}, bf16[256,1024]{1,0:T(8,128)(2,1)}, u32[]{:S(2)}, u32[]{:S(2)}) collective-permute-start(bf16[256,1024]{1,0:T(8,128)(2,1)} %pad_maximum_fusion.15), channel_id=1, source_target_pairs={{0,8},{4,12},{8,0},{12,4},{16,24},{20,28},{24,16},{28,20},{1,9},{5... | collective-permute-start | bytes 1572872 | tf_op jit(solution)/shard_map/ppermute | solution.py:29
  111.0 25.0 %collective-permute-start.10 = (bf16[256,1024]{1,0:T(8,128)(2,1)}, bf16[256,1024]{1,0:T(8,128)(2,1)}, u32[]{:S(2)}, u32[]{:S(2)}) collective-permute-start(bf16[256,1024]{1,0:T(8,128)(2,1)} %pad_maximum_fusion.14), channel_id=1, source_target_pairs={{0,16},{4,20},{8,24},{12,28},{16,0},{20,4},{24,8},{28,12},{1,17},{... | collective-permute-start | bytes 1572872 | tf_op jit(solution)/shard_map/ppermute | solution.py:29
  114.2 30.7 %collective-permute-start.19 = (bf16[256,1024]{1,0:T(8,128)(2,1)}, bf16[256,1024]{1,0:T(8,128)(2,1)}, u32[]{:S(2)}, u32[]{:S(2)}) collective-permute-start(bf16[256,1024]{1,0:T(8,128)(2,1)} %pad_maximum_fusion.17), channel_id=1, source_target_pairs={{0,8},{4,12},{8,0},{12,4},{16,24},{20,28},{24,16},{28,20},{1,9},{5... | collective-permute-start | bytes 1572872 | tf_op jit(solution)/shard_map/ppermute | solution.py:29
  117.2 31.2 %collective-permute-start.16 = (bf16[256,1024]{1,0:T(8,128)(2,1)}, bf16[256,1024]{1,0:T(8,128)(2,1)}, u32[]{:S(2)}, u32[]{:S(2)}) collective-permute-start(bf16[256,1024]{1,0:T(8,128)(2,1)} %pad_maximum_fusion.16), channel_id=1, source_target_pairs={{0,16},{4,20},{8,24},{12,28},{16,0},{20,4},{24,8},{28,12},{1,17},{... | collective-permute-start | bytes 1572872 | tf_op jit(solution)/shard_map/ppermute | solution.py:29
  122.4 33.7 %collective-permute-start.25 = (bf16[256,1024]{1,0:T(8,128)(2,1)}, bf16[256,1024]{1,0:T(8,128)(2,1)}, u32[]{:S(2)}, u32[]{:S(2)}) collective-permute-start(bf16[256,1024]{1,0:T(8,128)(2,1)} %pad_maximum_fusion.19), channel_id=1, source_target_pairs={{0,8},{4,12},{8,0},{12,4},{16,24},{20,28},{24,16},{28,20},{1,9},{5... | collective-permute-start | bytes 1572872 | tf_op jit(solution)/shard_map/ppermute | solution.py:29
  123.9 13.8 %copy-start.11 = (bf16[128,1024]{1,0:T(8,128)(2,1)S(1)}, bf16[128,1024]{1,0:T(8,128)(2,1)}, u32[]{:S(2)}) copy-start(bf16[128,1024]{1,0:T(8,128)(2,1)} %copy-done.10) | copy-start | bytes 786436
  133.7 25.6 %collective-permute-start.22 = (bf16[256,1024]{1,0:T(8,128)(2,1)S(1)}, bf16[256,1024]{1,0:T(8,128)(2,1)S(1)}, u32[]{:S(2)}, u32[]{:S(2)}) collective-permute-start(bf16[256,1024]{1,0:T(8,128)(2,1)S(1)} %copy-done.22), channel_id=1, source_target_pairs={{0,16},{4,20},{8,24},{12,28},{16,0},{20,4},{24,8},{28,12},{1,17},{... | collective-permute-start | bytes 1572872 | tf_op jit(solution)/shard_map/ppermute | solution.py:29
  136.1 23.4 %collective-permute-start.14 = (bf16[512,1024]{1,0:T(8,128)(2,1)S(1)}, bf16[512,1024]{1,0:T(8,128)(2,1)S(1)}, u32[]{:S(2)}, u32[]{:S(2)}) collective-permute-start(bf16[512,1024]{1,0:T(8,128)(2,1)S(1)} %pad_maximum_fusion.4), channel_id=1, source_target_pairs={{0,4},{4,0},{8,12},{12,8},{16,20},{20,16},{24,28},{28,24},{1,5},{5... | collective-permute-start | bytes 3145736 | tf_op jit(solution)/shard_map/ppermute | solution.py:29
  144.9 17.4 %collective-permute-start.11 = (bf16[512,1024]{1,0:T(8,128)(2,1)S(1)}, bf16[512,1024]{1,0:T(8,128)(2,1)S(1)}, u32[]{:S(2)}, u32[]{:S(2)}) collective-permute-start(bf16[512,1024]{1,0:T(8,128)(2,1)S(1)} %pad_maximum_fusion.3), channel_id=1, source_target_pairs={{0,4},{4,0},{8,12},{12,8},{16,20},{20,16},{24,28},{28,24},{1,5},{5... | collective-permute-start | bytes 3145736 | tf_op jit(solution)/shard_map/ppermute | solution.py:29
  148.4 16.0 %collective-permute-start.20 = (bf16[512,1024]{1,0:T(8,128)(2,1)S(1)}, bf16[512,1024]{1,0:T(8,128)(2,1)S(1)}, u32[]{:S(2)}, u32[]{:S(2)}) collective-permute-start(bf16[512,1024]{1,0:T(8,128)(2,1)S(1)} %pad_maximum_fusion.6), channel_id=1, source_target_pairs={{0,4},{4,0},{8,12},{12,8},{16,20},{20,16},{24,28},{28,24},{1,5},{5... | collective-permute-start | bytes 3145736 | tf_op jit(solution)/shard_map/ppermute | solution.py:29
  156.1 10.5 %collective-permute-start.17 = (bf16[512,1024]{1,0:T(8,128)(2,1)S(1)}, bf16[512,1024]{1,0:T(8,128)(2,1)S(1)}, u32[]{:S(2)}, u32[]{:S(2)}) collective-permute-start(bf16[512,1024]{1,0:T(8,128)(2,1)S(1)} %pad_maximum_fusion.5), channel_id=1, source_target_pairs={{0,4},{4,0},{8,12},{12,8},{16,20},{20,16},{24,28},{28,24},{1,5},{5... | collective-permute-start | bytes 3145736 | tf_op jit(solution)/shard_map/ppermute | solution.py:29
  159.3 11.5 %collective-permute-start.26 = (bf16[512,1024]{1,0:T(8,128)(2,1)S(1)}, bf16[512,1024]{1,0:T(8,128)(2,1)S(1)}, u32[]{:S(2)}, u32[]{:S(2)}) collective-permute-start(bf16[512,1024]{1,0:T(8,128)(2,1)S(1)} %pad_maximum_fusion.8), channel_id=1, source_target_pairs={{0,4},{4,0},{8,12},{12,8},{16,20},{20,16},{24,28},{28,24},{1,5},{5... | collective-permute-start | bytes 3145736 | tf_op jit(solution)/shard_map/ppermute | solution.py:29
  159.5 17.3 %collective-permute-start.23 = (bf16[512,1024]{1,0:T(8,128)(2,1)S(1)}, bf16[512,1024]{1,0:T(8,128)(2,1)S(1)}, u32[]{:S(2)}, u32[]{:S(2)}) collective-permute-start(bf16[512,1024]{1,0:T(8,128)(2,1)S(1)} %pad_maximum_fusion.7), channel_id=1, source_target_pairs={{0,4},{4,0},{8,12},{12,8},{16,20},{20,16},{24,28},{28,24},{1,5},{5... | collective-permute-start | bytes 3145736 | tf_op jit(solution)/shard_map/ppermute | solution.py:29
  (28 other events, 178.4 us)

commit v2 on v0

v2 whole, which is shorter than its diff:
```python
import functools

import jax
import jax.numpy as jnp
from jax import lax
from jax.experimental import pallas as pl
from jax.experimental.pallas import tpu as pltpu
from jax.sharding import PartitionSpec as P

LOC_CAP = 32
LANES = 128
BLOCK = 256
MIB = 1024 * 1024
BF16 = jnp.bfloat16
F32 = jnp.float32
IN_VMEM = pl.BlockSpec(memory_space=pltpu.VMEM)
IN_HBM = pl.BlockSpec(memory_space=pltpu.HBM)
IN_SMEM = pl.BlockSpec(memory_space=pltpu.SMEM)


def call(body, name, out_shape, in_specs, flops, moved, scratch=(), limit=12, **kwargs):
    if "out_specs" not in kwargs:
        kwargs["out_specs"] = jax.tree.map(lambda _: IN_VMEM, out_shape)
    return pl.pallas_call(
        body,
        out_shape=out_shape,
        in_specs=in_specs,
        scratch_shapes=scratch,
        compiler_params=pltpu.CompilerParams(vmem_limit_bytes=limit * MIB),
        cost_estimate=pl.CostEstimate(
            flops=int(flops), bytes_accessed=int(moved), transcendentals=0
        ),
        name=name,
        **kwargs,
    )


def struct(shape, kind=BF16):
    return jax.ShapeDtypeStruct(shape, kind)


def nt_dot(left, right):
    return lax.dot_general(left, right, (((1,), (1,)), ((), ())), preferred_element_type=F32)


def shift(block, step):
    ways = lax.axis_size("etp")
    return lax.ppermute(block, "etp", [(i, (i + step) % ways) for i in range(ways)])


def exchange(block, bits):
    ways = lax.axis_size("dp")
    return lax.ppermute(block, "dp", [(i, i ^ bits) for i in range(ways)])


def chip_gather(piece, chips):
    rows = piece.shape[0] // 2
    held = {0: [piece]}
    for key in sorted(range(1, chips), key=lambda k: (k.bit_count(), k)):
        if key.bit_count() == 1:
            held[key] = [exchange(piece, 2 * key)]
            continue
        high, low = 1 << (key.bit_length() - 1), key & -key
        upper, lower = held[key ^ high], held[key ^ low]
        upper = upper[0] if len(upper) == 2 else upper[0][:rows]
        lower = lower[1] if len(lower) == 2 else lower[0][rows:]
        held[key] = [exchange(upper, 2 * high), exchange(lower, 2 * low)]
    return [held[key] for key in range(chips)]


def pack_x_body(ids_ref, prob_ref, tokens_ref, x_ref, sel_ref):
    rows, width = tokens_ref.shape
    ids = ids_ref[...]
    routed = jnp.logical_or(ids[0:1] == 0, ids[1:2] == 0)
    flags = jnp.broadcast_to(routed.astype(F32), (8, rows)).astype(BF16)
    upto = (
        lax.broadcasted_iota(jnp.int32, (rows, rows), 0)
        <= lax.broadcasted_iota(jnp.int32, (rows, rows), 1)
    ).astype(F32).astype(BF16)
    slot = jnp.dot(flags, upto, preferred_element_type=F32)[0:1].astype(jnp.int32) - 1
    slots = lax.broadcasted_iota(jnp.int32, (LOC_CAP, rows), 0)
    matches = jnp.logical_and(slots == slot, routed)
    sel = matches.astype(F32)
    weight = jnp.sum(sel * prob_ref[...].astype(F32), axis=1, keepdims=True)
    sel = sel.astype(BF16)
    sel_ref[...] = sel
    x_ref[:, :width] = jnp.dot(sel, tokens_ref[...], preferred_element_type=F32).astype(BF16)
    x_ref[:, width:] = jnp.broadcast_to(weight, (LOC_CAP, LANES)).astype(BF16)


def pack_x(ids, prob, tokens):
    rows, width = tokens.shape
    return call(
        pack_x_body,
        "pack_x",
        [struct((LOC_CAP, width + LANES)), struct((LOC_CAP, rows))],
        [IN_VMEM] * 3,
        2 * LOC_CAP * rows * width,
        2 * rows * width,
    )(ids, prob, tokens)


def pack_dy_body(chips, chip_ref, sel_ref, grad_ref, dy_ref, *slice_refs):
    dy_ref[...] = jnp.dot(sel_ref[...], grad_ref[...], preferred_element_type=F32).astype(BF16)
    part = slice_refs[0].shape[1]
    for key in range(chips):
        first = pl.multiple_of((chip_ref[0] ^ key) * part, LANES)
        slice_refs[key][...] = dy_ref[:, pl.ds(first, part)]


def pack_dy(chip, sel, out_grad, chips):
    rows, width = out_grad.shape
    return call(
        functools.partial(pack_dy_body, chips),
        "pack_dy",
        [struct((LOC_CAP, width))] + [struct((LOC_CAP, width // chips))] * chips,
        [IN_SMEM] + [IN_VMEM] * 2,
        2 * LOC_CAP * rows * width,
        2 * rows * width,
    )(chip, sel, out_grad)


def join_x_body(chips, count, chip_ref, *refs):
    blocks, x_ref, slice_refs = refs[:count], refs[count], refs[count + 1 :]
    part = slice_refs[0].shape[1]
    for at, block in enumerate(blocks):
        x_ref[at * LOC_CAP : (at + 1) * LOC_CAP, :] = block[...]
    for key in range(chips):
        first = pl.multiple_of((chip_ref[0] ^ key) * part, LANES)
        slice_refs[key][...] = x_ref[:, pl.ds(first, part)]


def join_x(chip, blocks, chips):
    count = len(blocks)
    wide = blocks[0].shape[1]
    rows = count * LOC_CAP
    part = (wide - LANES) // chips
    return call(
        functools.partial(join_x_body, chips, count),
        "join_x",
        [struct((rows, wide))] + [struct((rows, part))] * chips,
        [IN_SMEM] + [IN_VMEM] * count,
        0,
        4 * rows * wide,
    )(chip, *blocks)


def windowed(groups, sems, ahead):
    made, at = [], 0
    for group in groups:
        made.append(
            [pltpu.make_async_copy(src, dst, sems.at[at + k]) for k, (src, dst) in enumerate(group)]
        )
        at += len(group)
    for copies in made[:ahead]:
        for copy in copies:
            copy.start()
    for step, copies in enumerate(made):
        for copy in copies:
            copy.wait()
        if step + ahead < len(made):
            for copy in made[step + ahead]:
                copy.start()
        yield step


def forward_body(
    x_ref, gate_hbm, up_hbm, scaled_ref, hidden_ref, silu_ref, slope_ref, gate_ref, up_ref, sems
):
    width, units = gate_hbm.shape
    x = x_ref[:, :width]
    weight = x_ref[:, width : width + 1].astype(F32)
    spans = [pl.ds(at, BLOCK) for at in range(0, units, BLOCK)]
    groups = [
        [(gate_hbm.at[:, span], gate_ref.at[:, span]), (up_hbm.at[:, span], up_ref.at[:, span])]
        for span in spans
    ]
    for step in windowed(groups, sems, 3):
        cols = slice(step * BLOCK, (step + 1) * BLOCK)
        gate = jnp.dot(x, gate_ref[:, cols], preferred_element_type=F32)
        up = jnp.dot(x, up_ref[:, cols], preferred_element_type=F32)
        sig = 1.0 / (1.0 + jnp.exp(-gate))
        act = gate * sig
        hidden = (act * up).astype(BF16)
        hidden_ref[:, cols] = hidden
        scaled_ref[:, cols] = (weight * hidden.astype(F32)).astype(BF16)
        silu_ref[:, cols] = weight * act
        slope_ref[:, cols] = weight * up * sig * (1.0 + gate * (1.0 - sig))


def forward(x_all, w_gate, w_up):
    rows = x_all.shape[0]
    width, units = w_gate.shape
    return call(
        forward_body,
        "forward",
        [struct((rows, units), kind) for kind in (BF16, BF16, F32, F32)],
        [IN_VMEM] + [IN_HBM] * 2,
        4 * rows * width * units,
        4 * width * units,
        [pltpu.VMEM(w_gate.shape, BF16)] * 2 + [pltpu.SemaphoreType.DMA((2 * (units // BLOCK),))],
        limit=54,
    )(x_all, w_gate, w_up)


def backward_body(count, *refs):
    blocks = refs[:count]
    down_hbm, hidden_ref, silu_ref, slope_ref, grad_ref, prob_ref, down_ref, sems = refs[count:]
    rows, units = hidden_ref.shape
    spans = [pl.ds(at, BLOCK) for at in range(0, units, BLOCK)]
    groups = [[(down_hbm.at[span], down_ref.at[span])] for span in spans]
    dy = jnp.concatenate([block[...] for block in blocks], axis=0)
    prob = jnp.zeros((rows, 1), F32)
    for step in windowed(groups, sems, 5):
        at = step * BLOCK
        cols = slice(at, at + BLOCK)
        raw = nt_dot(dy, down_ref[cols, :])
        grad_ref[:, cols] = (raw * slope_ref[:, cols]).astype(BF16)
        grad_ref[:, units + at : units + at + BLOCK] = (raw * silu_ref[:, cols]).astype(BF16)
        prob = prob + jnp.sum(hidden_ref[:, cols].astype(F32) * raw, axis=1, keepdims=True)
    prob_ref[...] = prob


def backward(dy_blocks, w_down, hidden, silu, slope):
    count = len(dy_blocks)
    rows, units = hidden.shape
    width = w_down.shape[1]
    return call(
        functools.partial(backward_body, count),
        "backward",
        [struct((rows, 2 * units)), struct((rows, 1), F32)],
        [IN_VMEM] * count + [IN_HBM] + [IN_VMEM] * 3,
        2 * rows * width * units,
        2 * width * units + 12 * rows * units,
        [pltpu.VMEM(w_down.shape, BF16), pltpu.SemaphoreType.DMA((units // BLOCK,))],
        limit=54,
    )(*dy_blocks, w_down, hidden, silu, slope)


def token_body(count, gate_hbm, up_hbm, grad_ref, prob_ref, *refs):
    outs = refs[:count]
    gate_w, up_w, sems = refs[count:]
    width, units = gate_hbm.shape
    spans = [pl.ds(at, BLOCK) for at in range(0, width, BLOCK)]
    groups = [
        [(gate_hbm.at[span], gate_w.at[span]), (up_hbm.at[span], up_w.at[span])] for span in spans
    ]
    prob = prob_ref[...]
    high = prob.astype(BF16).astype(F32)
    mid = (prob - high).astype(BF16).astype(F32)
    low = prob - high - mid
    lane = lax.broadcasted_iota(jnp.int32, (prob.shape[0], LANES), 1)
    terms = jnp.where(
        lane == 0, high, jnp.where(lane == 1, mid, jnp.where(lane == 2, low, 0.0))
    ).astype(BF16)
    for z in range(count):
        outs[z][:, width:] = terms[z * LOC_CAP : (z + 1) * LOC_CAP]
    gate = grad_ref[:, :units]
    up = grad_ref[:, units:]
    for step in windowed(groups, sems, 4):
        cols = slice(step * BLOCK, (step + 1) * BLOCK)
        share = (nt_dot(gate, gate_w[cols, :]) + nt_dot(up, up_w[cols, :])).astype(BF16)
        for z in range(count):
            outs[z][:, cols] = share[z * LOC_CAP : (z + 1) * LOC_CAP]


def token_shares(w_gate, w_up, grad, prob, count):
    width, units = w_gate.shape
    rows = count * LOC_CAP
    return call(
        functools.partial(token_body, count),
        "token_shares",
        [struct((LOC_CAP, width + LANES))] * count,
        [IN_HBM] * 2 + [IN_VMEM] * 2,
        4 * rows * width * units,
        4 * width * units,
        [pltpu.VMEM(w_gate.shape, BF16)] * 2 + [pltpu.SemaphoreType.DMA((2 * (width // BLOCK),))],
        limit=54,
    )(w_gate, w_up, grad, prob)


def place_body(*refs):
    shares, sel_ref, tokens_ref, prob_ref = refs[:-3], refs[-3], refs[-2], refs[-1]
    width = tokens_ref.shape[1]
    total = shares[0][...].astype(F32)
    for share in shares[1:]:
        total = total + share[...].astype(F32)
    rows = total[:, :width].astype(BF16)
    sel = sel_ref[...]
    tokens_ref[...] = lax.dot_general(
        sel, rows, (((0,), (0,)), ((), ())), preferred_element_type=F32
    ).astype(BF16)
    prob = jnp.sum(total[:, width:], axis=1, keepdims=True)
    prob_ref[...] = jnp.sum(jnp.where(sel.astype(F32) > 0.5, prob, 0.0), axis=0, keepdims=True)


def place(shares, sel):
    rows = sel.shape[1]
    width = shares[0].shape[1] - LANES
    return call(
        place_body,
        "place",
        [struct((rows, width)), struct((1, rows), F32)],
        [IN_VMEM] * (len(shares) + 1),
        2 * LOC_CAP * rows * width,
        4 * rows * width,
    )(*shares, sel)


def split_cores(core_ref, mine_ref, theirs_ref, cols, block):
    part = mine_ref.shape[0]
    turned = block.T

    @pl.when(core_ref[0] == 0)
    def _():
        mine_ref[:, cols] = turned[:part]
        theirs_ref[:, cols] = turned[part:]

    @pl.when(core_ref[0] == 1)
    def _():
        mine_ref[:, cols] = turned[part:]
        theirs_ref[:, cols] = turned[:part]


def turn_x_body(core_ref, *refs):
    slices, (mine_ref, theirs_ref) = refs[:-2], refs[-2:]
    rows = slices[0].shape[0]
    for key, block in enumerate(slices):
        split_cores(core_ref, mine_ref, theirs_ref, slice(key * rows, (key + 1) * rows), block[...])


def turn_x(core, slices):
    rows, wide = slices[0].shape
    depth = rows * len(slices)
    return call(
        turn_x_body,
        "turn_x",
        [struct((wide // 2, depth))] * 2,
        [IN_SMEM] + [IN_VMEM] * len(slices),
        0,
        4 * depth * wide,
    )(core, *slices)


def turn_dy_body(chips, core_ref, *refs):
    slices, (mine_ref, theirs_ref) = refs[:-2], refs[-2:]
    rows = len(slices) * LOC_CAP
    for key in range(chips):
        span = slice(key * LOC_CAP, (key + 1) * LOC_CAP)
        block = jnp.concatenate([ref[span, :] for ref in slices], axis=0)
        split_cores(core_ref, mine_ref, theirs_ref, slice(key * rows, (key + 1) * rows), block)


def turn_dy(core, slices, chips):
    wide = slices[0].shape[1]
    depth = len(slices) * slices[0].shape[0]
    return call(
        functools.partial(turn_dy_body, chips),
        "turn_dy",
        [struct((wide // 2, depth))] * 2,
        [IN_SMEM] + [IN_VMEM] * len(slices),
        0,
        4 * depth * wide,
    )(core, *slices)


def stacked(refs):
    return jnp.concatenate([ref[...] for ref in refs], axis=0)


def wide_specs(parts, block):
    return [pl.BlockSpec((part.shape[0], block), lambda j: (0, j)) for part in parts]


def kept(array):
    return pl.BlockSpec(array.shape, lambda j: (0, 0))


def theirs_body(left_ref, *refs):
    out_ref = refs[-1]
    depth = sum(ref.shape[0] for ref in refs[:-1])
    out_ref[...] = jnp.dot(
        left_ref[:, :depth], stacked(refs[:-1]), preferred_element_type=F32
    ).astype(BF16)


def theirs_sums(left, parts):
    units = parts[0].shape[1]
    block = min(4 * BLOCK, units)
    depth = sum(part.shape[0] for part in parts)
    return call(
        theirs_body,
        "theirs_sums",
        struct((left.shape[0], units)),
        [kept(left)] + wide_specs(parts, block),
        2 * left.shape[0] * depth * units,
        2 * (depth + left.shape[0]) * units,
        grid=(units // block,),
        out_specs=pl.BlockSpec((left.shape[0], block), lambda j: (0, j)),
        limit=24,
    )(left, *parts)


def down_body(inv, left_ref, got_ref, *refs):
    out_ref = refs[-1]
    total = jnp.dot(left_ref[...], stacked(refs[:-1]), preferred_element_type=F32)
    out_ref[...] = ((total + got_ref[...].astype(F32)) * inv).T.astype(BF16)


def down_sums(left, got, parts, inv):
    part, units = got.shape
    block = min(2 * BLOCK, units)
    return call(
        functools.partial(down_body, inv),
        "down_sums",
        struct((units, part)),
        [kept(left)] + wide_specs([got, *parts], block),
        2 * left.size * units,
        2 * (left.shape[1] + 2 * part) * units,
        grid=(units // block,),
        out_specs=pl.BlockSpec((block, part), lambda j: (j, 0)),
        limit=24,
    )(left, got, *parts)


def pair_body(inv, count, steps, left_ref, other_ref, *refs):
    parts, others, (gate_ref, up_ref) = refs[:count], refs[count:-2], refs[-2:]
    total = jnp.dot(left_ref[...], stacked(parts), preferred_element_type=F32)
    total = total + jnp.dot(other_ref[...], stacked(others), preferred_element_type=F32)
    total = (total * inv).astype(BF16)

    @pl.when(pl.program_id(0) < steps)
    def _():
        gate_ref[...] = total

    @pl.when(pl.program_id(0) >= steps)
    def _():
        up_ref[...] = total


def pair_sums(left, other, parts, others, inv):
    part = left.shape[0]
    units = parts[0].shape[1]
    block = min(2 * BLOCK, units // 2)
    steps = units // 2 // block
    return call(
        functools.partial(pair_body, inv, len(parts), steps),
        "pair_sums",
        [struct((part, units // 2))] * 2,
        [kept(left), kept(other)] + wide_specs([*parts, *others], block),
        4 * left.size * units,
        4 * (left.shape[1] + part) * units,
        grid=(2 * steps,),
        out_specs=[
            pl.BlockSpec((part, block), lambda j: (0, jnp.minimum(j, steps - 1))),
            pl.BlockSpec((part, block), lambda j: (0, jnp.maximum(j - steps, 0))),
        ],
        limit=24,
    )(left, other, *parts, *others)


def after(value, *earlier):
    return lax.optimization_barrier((value, *earlier))[0]


def shards(tokens, out_grad, route_ids, route_prob, w_gate, w_up, w_down):
    data_ways = lax.axis_size("dp")
    etp_ways = lax.axis_size("etp")
    chips = data_ways // 2
    me = lax.axis_index("dp")
    chip = lax.shift_right_logical(me, 1).reshape(1)
    core = lax.bitwise_and(me, 1).reshape(1)
    inv = 1.0 / data_ways

    x_pack, sel = pack_x(route_ids.T, route_prob.reshape(1, -1), tokens)
    x_blocks = [x_pack] + [shift(x_pack, step) for step in range(1, etp_ways)]
    dy_pack, *dy_parts = pack_dy(chip, sel, out_grad, chips)
    dy_parts = jnp.concatenate(
        [dy_parts[0]] + [exchange(dy_parts[key], 2 * key) for key in range(1, chips)], axis=0
    )
    x_blocks[0] = after(x_blocks[0], dy_parts)
    x_all, *x_parts = join_x(chip, x_blocks, chips)
    x_slices = [x_parts[0]] + [exchange(x_parts[key], 2 * key) for key in range(1, chips)]
    dy_pack = after(dy_pack, x_all)
    dy_blocks = [dy_pack] + [shift(dy_pack, step) for step in range(1, etp_ways)]
    scaled, hidden, silu, slope = forward(x_all, w_gate, w_up)
    scaled = chip_gather(scaled, chips)

    grad, prob = backward(dy_blocks, w_down, after(hidden, *x_slices[1:]), silu, slope)
    grads = sum(chip_gather(grad, chips), [])
    dy_parts = after(dy_parts, *dy_blocks[1:])
    dy_slices = [dy_parts] + [shift(dy_parts, step) for step in range(1, etp_ways)]

    scaled = sum(scaled, [])
    shares = token_shares(w_gate, w_up, grad, after(prob, *scaled[1:]), etp_ways)
    shares = [after(share, *dy_slices[1:]) for share in shares]
    shares = [shares[0]] + [shift(shares[step], -step) for step in range(1, etp_ways)]
    grad_tokens, grad_prob = place(shares, sel)

    mine, theirs = turn_dy(core, dy_slices, chips)
    theirs = after(theirs, *shares[1:])
    got = exchange(theirs_sums(theirs, scaled), 1)
    grad_down = down_sums(mine, got, scaled, inv)

    mine, theirs = turn_x(core, x_slices)
    others = [
        exchange(after(part, *shares[1:]) if part.shape == grad.shape else part, 1) for part in grads
    ]
    mine = after(mine, grad_down, grad_tokens)
    grad_gate, grad_up = pair_sums(mine, exchange(theirs, 1), grads, others, inv)
    return (grad_tokens, grad_prob.reshape(-1), grad_gate, grad_up, grad_down)


def solution(mesh):
    placed = (
        P(("dp", "etp"), None),
        P(("dp", "etp"), None),
        P(("dp", "etp"), None),
        P(("dp", "etp")),
        P(None, "etp"),
        P(None, "etp"),
        P("etp", None),
    )
    return jax.shard_map(
        shards,
        mesh=mesh,
        in_specs=placed,
        out_specs=(
            P(("dp", "etp"), None),
            P(("dp", "etp")),
            P("dp", "etp"),
            P("dp", "etp"),
            P("etp", "dp"),
        ),
        check_vma=False,
    )
```

time: 388 us -> 160 us (0.41)
  waiting for transfers between devices: 204 us -> 40.9 us
  matrix products: 70.2 us -> 0 us
  Pallas kernels: 0 us -> 61 us
  blocking collectives: 58.4 us -> 0 us
  starting transfers between devices: 0.08 us -> 45.7 us
  other arithmetic: 33 us -> 0 us
  between operations: 15.5 us -> 0.98 us
  local copies, waits for them, and re-layouts: 6.06 us -> 11.2 us
    reduce_scatter x2 -> x0, waiting for transfers between devices: 204 us -> none  [the longest x1 204 us: shards(): lax.psum_scatter(jnp.concatenate([contract_rows(x_all, gate_up), contract...]
    dot_general x11 -> x0, matrix products: 70.2 us -> none  [the longest x3 25.3 us: contract_cols(): lax.dot_general(left, right, (((1,), (1,)), ((), ())), preferred_element_...]
    pallas_call x0 -> x12, Pallas kernels: none -> 61 us  [the longest x1 19.2 us: token_shares(): call(functools.partial(token_body, count), 'token_shares', [struct((LOC_C...]
    ppermute x0 -> x33, starting transfers between devices: none -> 45.7 us  [the longest x12 27.6 us: shift(): lax.ppermute(block, 'etp', [(i, (i + step) % ways) for i in range(ways)])]
    ppermute x0 -> x33, waiting for transfers between devices: none -> 40.9 us  [the longest x21 21 us: exchange(): return lax.ppermute(block, 'dp', [(i, i ^ bits) for i in range(ways)])]
    all_gather x2 -> x0, blocking collectives: 33 us -> none  [the longest x1 16.6 us: shards(): lax.all_gather(dy_pack, 'etp', axis=0, tiled=True)]
    concatenate x1 -> x0, other arithmetic: 25.7 us -> none  [shards(): jnp.concatenate([contract_rows(x_all, gate_up), contract_rows(dy_all, sca...]
    unnamed x2 -> x0, blocking collectives: 25.4 us -> none
  transfers between devices with their start and end apart: 2 -> 33, of which waited for: 1 -> 10; matrix products, arithmetic and copies ran while one was open for 14% -> 1% of each run, Pallas kernels for 0% -> 25%
where the time goes in v2:
time: 160 us
  Pallas kernels  61 us (38%)
  starting transfers between devices  45.7 us (29%)
  waiting for transfers between devices  40.9 us (26%)
  local copies, waits for them, and re-layouts  11.2 us (7%)
    ppermute x12, starting transfers between devices, shift(): lax.ppermute(block, 'etp', [(i, (i + step) % ways) for i in range(ways)])  27.6 us
    ppermute x21, waiting for transfers between devices, exchange(): return lax.ppermute(block, 'dp', [(i, i ^ bits) for i in range(ways)])  21 us
    ppermute x12, waiting for transfers between devices, shift(): lax.ppermute(block, 'etp', [(i, (i + step) % ways) for i in range(ways)])  20 us
    pallas_call x1, Pallas kernels, token_shares(): call(functools.partial(token_body, count), 'token_shares', [struct((LOC_C...  19.2 us
    ppermute x21, starting transfers between devices, exchange(): return lax.ppermute(block, 'dp', [(i, i ^ bits) for i in range(ways)])  18.1 us
    pallas_call x1, Pallas kernels, backward(): call(functools.partial(backward_body, count), 'backward', [struct((rows,...  12.9 us
    pallas_call x1, Pallas kernels, forward(): call(forward_body, 'forward', [struct((rows, units), kind) for kind in (B...  12.3 us
    unnamed x55, local copies, waits for them, and re-layouts  10 us
  transfers between devices with their start and end apart: 33, of which 10 were waited for; matrix products, arithmetic and copies ran while one was open for 1% of the time, Pallas kernels for 25%

profile of v2, /device:TPU:0, one launch (start us, length us, event | category | flops | bytes accessed | tf_op | source)
XLA Modules:
  0.0 159.9 jit_solution(9704915216390131950)
XLA Ops:
  3.5 3.1 %collective-permute-start.3 = (bf16[32,3200]{1,0:T(8,128)(2,1)S(1)}, bf16[32,3200]{1,0:T(8,128)(2,1)S(1)}, u32[]{:S(2)}, u32[]{:S(2)}) collective-permute-start(bf16[32,3200]{1,0:T(8,128)(2,1)S(1)} %get-tuple-element.56.refs_0_), channel_id=1, source_target_pairs={{0,1},{1,2},{2,3},{3,0},{4,5},{5,6},{6,7},{7,4},{8,9},{9,10},{10,1... | collective-permute-start | bytes 614408 | tf_op jit(solution)/shard_map/ppermute | solution.py:48
  6.5 2.6 %collective-permute-start.4 = (bf16[32,3200]{1,0:T(8,128)(2,1)S(1)}, bf16[32,3200]{1,0:T(8,128)(2,1)S(1)}, u32[]{:S(2)}, u32[]{:S(2)}) collective-permute-start(bf16[32,3200]{1,0:T(8,128)(2,1)S(1)} %get-tuple-element.56.refs_0_), channel_id=1, source_target_pairs={{0,2},{1,3},{2,0},{3,1},{4,6},{5,7},{6,4},{7,5},{8,10},{9,11},{10,... | collective-permute-start | bytes 614408 | tf_op jit(solution)/shard_map/ppermute | solution.py:48
  9.1 1.3 collective-permute-start.5
  11.9 1.6 collective-permute-start
  13.4 1.5 collective-permute-start.1
  16.0 2.5 %collective-permute-start.2 = (bf16[32,768]{1,0:T(8,128)(2,1)S(1)}, bf16[32,768]{1,0:T(8,128)(2,1)S(1)}, u32[]{:S(2)}, u32[]{:S(2)}) collective-permute-start(bf16[32,768]{1,0:T(8,128)(2,1)S(1)} %get-tuple-element.55), channel_id=1, source_target_pairs={{0,24},{4,28},{8,16},{12,20},{16,8},{20,12},{24,0},{28,4},{1,25},{... | collective-permute-start | bytes 147464 | tf_op jit(solution)/shard_map/ppermute | solution.py:53
  18.5 2.5 %collective-permute-done.2 = bf16[32,768]{1,0:T(8,128)(2,1)S(1)} collective-permute-done((bf16[32,768]{1,0:T(8,128)(2,1)S(1)}, bf16[32,768]{1,0:T(8,128)(2,1)S(1)}, u32[]{:S(2)}, u32[]{:S(2)}) %collective-permute-start.2) | collective-permute-done | bytes 49184 | tf_op jit(solution)/shard_map/ppermute | solution.py:53
  21.0 1.5 collective-permute-done.4.refs_2_
  24.3 12.3 %forward.1 = (bf16[128,2048]{1,0:T(8,128)(2,1)}, bf16[128,2048]{1,0:T(8,128)(2,1)}, f32[128,2048]{1,0:T(8,128)}, f32[128,2048]{1,0:T(8,128)}) custom-call(bf16[128,3200]{1,0:T(8,128)(2,1)} %copy-done.2, bf16[3072,2048]{1,0:T(8,128)(2,1)} %gate_hbm.3, bf16[3072,2048]{1,0:T(8,128)(2,1)} %up_hbm.3), custom_call_target="tpu_custom_call" | custom-call | flops 3221225472 | bytes 25165824 | tf_op jit(solution)/shard_map/forward/pallas_call | solution.py:194
  36.5 1.5 collective-permute-start.12
  38.1 1.5 collective-permute-start.13
  39.6 4.9 %collective-permute-start.6 = (bf16[32,3072]{1,0:T(8,128)(2,1)S(1)}, bf16[32,3072]{1,0:T(8,128)(2,1)S(1)}, u32[]{:S(2)}, u32[]{:S(2)}) collective-permute-start(bf16[32,3072]{1,0:T(8,128)(2,1)S(1)} %get-tuple-element.58.refs_0_), channel_id=1, source_target_pairs={{0,1},{1,2},{2,3},{3,0},{4,5},{5,6},{6,7},{7,4},{8,9},{9,10},{10,1... | collective-permute-start | bytes 589832 | tf_op jit(solution)/shard_map/ppermute | solution.py:48
  44.5 1.6 %collective-permute-start.7 = (bf16[32,3072]{1,0:T(8,128)(2,1)S(1)}, bf16[32,3072]{1,0:T(8,128)(2,1)S(1)}, u32[]{:S(2)}, u32[]{:S(2)}) collective-permute-start(bf16[32,3072]{1,0:T(8,128)(2,1)S(1)} %get-tuple-element.58.refs_0_), channel_id=1, source_target_pairs={{0,2},{1,3},{2,0},{3,1},{4,6},{5,7},{6,4},{7,5},{8,10},{9,11},{10,... | collective-permute-start | bytes 589832 | tf_op jit(solution)/shard_map/ppermute | solution.py:48
  46.8 4.6 %collective-permute-done.6.refs_1_ = bf16[32,3072]{1,0:T(8,128)(2,1)S(1)} collective-permute-done((bf16[32,3072]{1,0:T(8,128)(2,1)S(1)}, bf16[32,3072]{1,0:T(8,128)(2,1)S(1)}, u32[]{:S(2)}, u32[]{:S(2)}) %collective-permute-start.6) | collective-permute-done | bytes 196640 | tf_op jit(solution)/shard_map/ppermute | solution.py:48
  52.0 5.5 %collective-permute-done.7.refs_2_ = bf16[32,3072]{1,0:T(8,128)(2,1)S(1)} collective-permute-done((bf16[32,3072]{1,0:T(8,128)(2,1)S(1)}, bf16[32,3072]{1,0:T(8,128)(2,1)S(1)}, u32[]{:S(2)}, u32[]{:S(2)}) %collective-permute-start.7) | collective-permute-done | bytes 196640 | tf_op jit(solution)/shard_map/ppermute | solution.py:48
  58.0 1.5 collective-permute-start.11
  60.1 1.6 collective-permute-start.15
  61.7 3.7 %collective-permute-start.16 = (bf16[128,768]{1,0:T(8,128)(2,1)S(1)}, bf16[128,768]{1,0:T(8,128)(2,1)S(1)}, u32[]{:S(2)}, u32[]{:S(2)}) collective-permute-start(bf16[128,768]{1,0:T(8,128)(2,1)S(1)} %constant_dynamic-update-slice_fusion.refs_0_), channel_id=1, source_target_pairs={{0,1},{1,2},{2,3},{3,0},{4,5},{5,6},{6,7},{7,4},{8,9},{9,10},{10,1... | collective-permute-start | bytes 589832 | tf_op jit(solution)/shard_map/ppermute | solution.py:48
  65.4 4.1 %collective-permute-done.10.refs_2_ = bf16[128,768]{1,0:T(8,128)(2,1)S(1)} collective-permute-done((bf16[128,768]{1,0:T(8,128)(2,1)S(1)}, bf16[128,768]{1,0:T(8,128)(2,1)S(1)}, u32[]{:S(2)}, u32[]{:S(2)}) %collective-permute-start.10) | collective-permute-done | bytes 196640 | tf_op jit(solution)/shard_map/ppermute | solution.py:53
  69.5 5.9 %collective-permute-start.18 = (bf16[128,768]{1,0:T(8,128)(2,1)S(1)}, bf16[128,768]{1,0:T(8,128)(2,1)S(1)}, u32[]{:S(2)}, u32[]{:S(2)}) collective-permute-start(bf16[128,768]{1,0:T(8,128)(2,1)S(1)} %constant_dynamic-update-slice_fusion.refs_0_), channel_id=1, source_target_pairs={{0,3},{1,0},{2,1},{3,2},{4,7},{5,4},{6,5},{7,6},{8,11},{9,8},{10,9... | collective-permute-start | bytes 589832 | tf_op jit(solution)/shard_map/ppermute | solution.py:48
  75.4 12.9 %backward.1 = (bf16[128,4096]{1,0:T(8,128)(2,1)}, f32[128,1]{1,0:T(8,128)}) custom-call(bf16[32,3072]{1,0:T(8,128)(2,1)} %copy-done.6, bf16[32,3072]{1,0:T(8,128)(2,1)} %copy-done.23, bf16[32,3072]{1,0:T(8,128)(2,1)} %copy-done.24, bf16[32,3072]{1,0:T(8,128)(2,1)} %copy-done.25, bf16[2048,3072]{1,0:T(8,128)(2,1)} %refs_4_.1, ...), custom_call_target="tpu_custom_call" | custom-call | flops 1610612736 | bytes 15728640 | tf_op jit(solution)/shard_map/backward/pallas_call | solution.py:228
  89.0 19.2 %token_shares.1 = (bf16[32,3200]{1,0:T(8,128)(2,1)}, bf16[32,3200]{1,0:T(8,128)(2,1)}, bf16[32,3200]{1,0:T(8,128)(2,1)}, bf16[32,3200]{1,0:T(8,128)(2,1)}) custom-call(bf16[3072,2048]{1,0:T(8,128)(2,1)} %gate_hbm.3, bf16[3072,2048]{1,0:T(8,128)(2,1)} %up_hbm.3, bf16[128,4096]{1,0:T(8,128)(2,1)} %get-tuple-element.88.grad_ref.refs_0_, ...), custom_call_target="tpu_custom_call" | custom-call | flops 3221225472 | bytes 25165824 | tf_op jit(solution)/shard_map/token_shares/pallas_call | solution.py:270
  110.3 1.8 %collective-permute-start.20 = (bf16[32,3200]{1,0:T(8,128)(2,1)}, bf16[32,3200]{1,0:T(8,128)(2,1)}, u32[]{:S(2)}, u32[]{:S(2)}) collective-permute-start(bf16[32,3200]{1,0:T(8,128)(2,1)} %get-tuple-element.76), channel_id=1, source_target_pairs={{0,2},{1,3},{2,0},{3,1},{4,6},{5,7},{6,4},{7,5},{8,10},{9,11},{10,... | collective-permute-start | bytes 614408 | tf_op jit(solution)/shard_map/ppermute | solution.py:48
  112.1 2.0 %collective-permute-start.21 = (bf16[32,3200]{1,0:T(8,128)(2,1)}, bf16[32,3200]{1,0:T(8,128)(2,1)}, u32[]{:S(2)}, u32[]{:S(2)}) collective-permute-start(bf16[32,3200]{1,0:T(8,128)(2,1)} %get-tuple-element.78), channel_id=1, source_target_pairs={{0,1},{1,2},{2,3},{3,0},{4,5},{5,6},{6,7},{7,4},{8,9},{9,10},{10,1... | collective-permute-start | bytes 614408 | tf_op jit(solution)/shard_map/ppermute | solution.py:48
  119.4 7.5 %collective-permute-done.20.refs_2_ = bf16[32,3200]{1,0:T(8,128)(2,1)} collective-permute-done((bf16[32,3200]{1,0:T(8,128)(2,1)}, bf16[32,3200]{1,0:T(8,128)(2,1)}, u32[]{:S(2)}, u32[]{:S(2)}) %collective-permute-start.20) | collective-permute-done | bytes 204832 | tf_op jit(solution)/shard_map/ppermute | solution.py:48
  126.9 1.4 theirs_sums.1
  130.8 5.0 %collective-permute-done.25.refs_2_ = bf16[128,4096]{1,0:T(8,128)(2,1)S(1)} collective-permute-done((bf16[128,4096]{1,0:T(8,128)(2,1)S(1)}, bf16[128,4096]{1,0:T(8,128)(2,1)S(1)}, u32[]{:S(2)}, u32[]{:S(2)}) %collective-permute-start.25) | collective-permute-done | bytes 1048608 | tf_op jit(solution)/shard_map/ppermute | solution.py:53
  135.9 1.4 collective-permute-start.27
  137.3 8.2 %collective-permute-done.26.refs_3_ = bf16[64,4096]{1,0:T(8,128)(2,1)S(1)} collective-permute-done((bf16[64,4096]{1,0:T(8,128)(2,1)S(1)}, bf16[64,4096]{1,0:T(8,128)(2,1)S(1)}, u32[]{:S(2)}, u32[]{:S(2)}) %collective-permute-start.26) | collective-permute-done | bytes 524320 | tf_op jit(solution)/shard_map/ppermute | solution.py:53
  146.2 2.3 %place.1 = (bf16[128,3072]{1,0:T(8,128)(2,1)}, f32[1,128]{1,0:T(1,128)}) custom-call(bf16[32,3200]{1,0:T(8,128)(2,1)S(1)} %copy-done.5, bf16[32,3200]{1,0:T(8,128)(2,1)S(1)} %collective-permute-done.19.refs_1_, bf16[32,3200]{1,0:T(8,128)(2,1)} %collective-permute-done.20.refs_2_, bf16[32,3200]{1,0:T(8,128)(2,1)} %collective-permute-done.21.refs_3_, ...), custom_call_target="tpu_custom_call" | custom-call | flops 25165824 | bytes 1572864 | tf_op jit(solution)/shard_map/place/pallas_call | solution.py:300
  148.5 3.1 %down_sums.1 = bf16[2048,384]{1,0:T(8,128)(2,1)} custom-call(bf16[384,512]{1,0:T(8,128)(2,1)S(1)} %get-tuple-element.83.left_ref, bf16[384,2048]{1,0:T(8,128)(2,1)S(1)} %collective-permute-done.22.got_ref, bf16[128,2048]{1,0:T(8,128)(2,1)S(1)} %copy-done, bf16[128,2048]{1,0:T(8,128)(2,1)S(1)} %collective-permute-done.12.refs_1_, ...), custom_call_target="tpu_custom_call" | custom-call | flops 805306368 | bytes 5242880 | tf_op jit(solution)/shard_map/down_sums/pallas_call | solution.py:413
  151.6 8.3 %pair_sums.1 = (bf16[384,2048]{1,0:T(8,128)(2,1)}, bf16[384,2048]{1,0:T(8,128)(2,1)}) custom-call(bf16[384,512]{1,0:T(8,128)(2,1)S(1)} %get-tuple-element.86.left_ref, bf16[384,512]{1,0:T(8,128)(2,1)S(1)} %collective-permute-done.23.other_ref, bf16[128,4096]{1,0:T(8,128)(2,1)S(1)} %copy-done.1, bf16[128,4096]{1,0:T(8,128)(2,1)} %collective-permute-done.24.refs_1_, ...), custom_call_target="tpu_custom_call" | custom-call | flops 3221225472 | bytes 14680064 | tf_op jit(solution)/shard_map/pair_sums/pallas_call | solution.py:446
  (106 shorter events, 20.6 us)
Async XLA Ops:
  3.5 17.6 %collective-permute-start.3 = (bf16[32,3200]{1,0:T(8,128)(2,1)S(1)}, bf16[32,3200]{1,0:T(8,128)(2,1)S(1)}, u32[]{:S(2)}, u32[]{:S(2)}) collective-permute-start(bf16[32,3200]{1,0:T(8,128)(2,1)S(1)} %get-tuple-element.56.refs_0_), channel_id=1, source_target_pairs={{0,1},{1,2},{2,3},{3,0},{4,5},{5,6},{6,7},{7,4},{8,9},{9,10},{10,1... | collective-permute-start | bytes 614408 | tf_op jit(solution)/shard_map/ppermute | solution.py:48
  6.5 16.0 %collective-permute-start.4 = (bf16[32,3200]{1,0:T(8,128)(2,1)S(1)}, bf16[32,3200]{1,0:T(8,128)(2,1)S(1)}, u32[]{:S(2)}, u32[]{:S(2)}) collective-permute-start(bf16[32,3200]{1,0:T(8,128)(2,1)S(1)} %get-tuple-element.56.refs_0_), channel_id=1, source_target_pairs={{0,2},{1,3},{2,0},{3,1},{4,6},{5,7},{6,4},{7,5},{8,10},{9,11},{10,... | collective-permute-start | bytes 614408 | tf_op jit(solution)/shard_map/ppermute | solution.py:48
  9.1 13.4 %collective-permute-start.5 = (bf16[32,3200]{1,0:T(8,128)(2,1)S(1)}, bf16[32,3200]{1,0:T(8,128)(2,1)S(1)}, u32[]{:S(2)}, u32[]{:S(2)}) collective-permute-start(bf16[32,3200]{1,0:T(8,128)(2,1)S(1)} %get-tuple-element.56.refs_0_), channel_id=1, source_target_pairs={{0,3},{1,0},{2,1},{3,2},{4,7},{5,4},{6,5},{7,6},{8,11},{9,8},{10,9... | collective-permute-start | bytes 614408 | tf_op jit(solution)/shard_map/ppermute | solution.py:48
  13.4 5.1 %collective-permute-start.1 = (bf16[32,768]{1,0:T(8,128)(2,1)S(1)}, bf16[32,768]{1,0:T(8,128)(2,1)S(1)}, u32[]{:S(2)}, u32[]{:S(2)}) collective-permute-start(bf16[32,768]{1,0:T(8,128)(2,1)S(1)} %get-tuple-element.54), channel_id=1, source_target_pairs={{0,16},{4,20},{8,24},{12,28},{16,0},{20,4},{24,8},{28,12},{1,17},{... | collective-permute-start | bytes 147464 | tf_op jit(solution)/shard_map/ppermute | solution.py:53
  16.0 5.0 %collective-permute-start.2 = (bf16[32,768]{1,0:T(8,128)(2,1)S(1)}, bf16[32,768]{1,0:T(8,128)(2,1)S(1)}, u32[]{:S(2)}, u32[]{:S(2)}) collective-permute-start(bf16[32,768]{1,0:T(8,128)(2,1)S(1)} %get-tuple-element.55), channel_id=1, source_target_pairs={{0,24},{4,28},{8,16},{12,20},{16,8},{20,12},{24,0},{28,4},{1,25},{... | collective-permute-start | bytes 147464 | tf_op jit(solution)/shard_map/ppermute | solution.py:53
  36.5 21.5 %collective-permute-start.12 = (bf16[128,2048]{1,0:T(8,128)(2,1)}, bf16[128,2048]{1,0:T(8,128)(2,1)S(1)}, u32[]{:S(2)}, u32[]{:S(2)}) collective-permute-start(bf16[128,2048]{1,0:T(8,128)(2,1)} %get-tuple-element.68.refs_0_), channel_id=1, source_target_pairs={{0,8},{4,12},{8,0},{12,4},{16,24},{20,28},{24,16},{28,20},{1,9},{5... | collective-permute-start | bytes 1572872 | tf_op jit(solution)/shard_map/ppermute | solution.py:53
  38.1 21.4 %collective-permute-start.13 = (bf16[128,2048]{1,0:T(8,128)(2,1)}, bf16[128,2048]{1,0:T(8,128)(2,1)S(1)}, u32[]{:S(2)}, u32[]{:S(2)}) collective-permute-start(bf16[128,2048]{1,0:T(8,128)(2,1)} %get-tuple-element.68.refs_0_), channel_id=1, source_target_pairs={{0,16},{4,20},{8,24},{12,28},{16,0},{20,4},{24,8},{28,12},{1,17},{... | collective-permute-start | bytes 1572872 | tf_op jit(solution)/shard_map/ppermute | solution.py:53
  39.6 11.8 %collective-permute-start.6 = (bf16[32,3072]{1,0:T(8,128)(2,1)S(1)}, bf16[32,3072]{1,0:T(8,128)(2,1)S(1)}, u32[]{:S(2)}, u32[]{:S(2)}) collective-permute-start(bf16[32,3072]{1,0:T(8,128)(2,1)S(1)} %get-tuple-element.58.refs_0_), channel_id=1, source_target_pairs={{0,1},{1,2},{2,3},{3,0},{4,5},{5,6},{6,7},{7,4},{8,9},{9,10},{10,1... | collective-permute-start | bytes 589832 | tf_op jit(solution)/shard_map/ppermute | solution.py:48
  44.5 13.0 %collective-permute-start.7 = (bf16[32,3072]{1,0:T(8,128)(2,1)S(1)}, bf16[32,3072]{1,0:T(8,128)(2,1)S(1)}, u32[]{:S(2)}, u32[]{:S(2)}) collective-permute-start(bf16[32,3072]{1,0:T(8,128)(2,1)S(1)} %get-tuple-element.58.refs_0_), channel_id=1, source_target_pairs={{0,2},{1,3},{2,0},{3,1},{4,6},{5,7},{6,4},{7,5},{8,10},{9,11},{10,... | collective-permute-start | bytes 589832 | tf_op jit(solution)/shard_map/ppermute | solution.py:48
  46.1 14.1 %collective-permute-start.8 = (bf16[32,3072]{1,0:T(8,128)(2,1)S(1)}, bf16[32,3072]{1,0:T(8,128)(2,1)S(1)}, u32[]{:S(2)}, u32[]{:S(2)}) collective-permute-start(bf16[32,3072]{1,0:T(8,128)(2,1)S(1)} %get-tuple-element.58.refs_0_), channel_id=1, source_target_pairs={{0,3},{1,0},{2,1},{3,2},{4,7},{5,4},{6,5},{7,6},{8,11},{9,8},{10,9... | collective-permute-start | bytes 589832 | tf_op jit(solution)/shard_map/ppermute | solution.py:48
  51.4 10.3 %collective-permute-start.9 = (bf16[128,768]{1,0:T(8,128)(2,1)S(1)}, bf16[128,768]{1,0:T(8,128)(2,1)S(1)}, u32[]{:S(2)}, u32[]{:S(2)}) collective-permute-start(bf16[128,768]{1,0:T(8,128)(2,1)S(1)} %get-tuple-element.60), channel_id=1, source_target_pairs={{0,8},{4,12},{8,0},{12,4},{16,24},{20,28},{24,16},{28,20},{1,9},{5... | collective-permute-start | bytes 589832 | tf_op jit(solution)/shard_map/ppermute | solution.py:53
  57.5 12.0 %collective-permute-start.10 = (bf16[128,768]{1,0:T(8,128)(2,1)S(1)}, bf16[128,768]{1,0:T(8,128)(2,1)S(1)}, u32[]{:S(2)}, u32[]{:S(2)}) collective-permute-start(bf16[128,768]{1,0:T(8,128)(2,1)S(1)} %get-tuple-element.61), channel_id=1, source_target_pairs={{0,16},{4,20},{8,24},{12,28},{16,0},{20,4},{24,8},{28,12},{1,17},{... | collective-permute-start | bytes 589832 | tf_op jit(solution)/shard_map/ppermute | solution.py:53
  58.0 11.5 %collective-permute-start.11 = (bf16[128,768]{1,0:T(8,128)(2,1)S(1)}, bf16[128,768]{1,0:T(8,128)(2,1)S(1)}, u32[]{:S(2)}, u32[]{:S(2)}) collective-permute-start(bf16[128,768]{1,0:T(8,128)(2,1)S(1)} %get-tuple-element.62), channel_id=1, source_target_pairs={{0,24},{4,28},{8,16},{12,20},{16,8},{20,12},{24,0},{28,4},{1,25},{... | collective-permute-start | bytes 589832 | tf_op jit(solution)/shard_map/ppermute | solution.py:53
  59.5 28.8 %collective-permute-start.14 = (bf16[64,2048]{1,0:T(8,128)(2,1)S(1)}, bf16[64,2048]{1,0:T(8,128)(2,1)S(1)}, u32[]{:S(2)}, u32[]{:S(2)}) collective-permute-start(bf16[64,2048]{1,0:T(8,128)(2,1)S(1)} %slice.16), channel_id=1, source_target_pairs={{0,16},{4,20},{8,24},{12,28},{16,0},{20,4},{24,8},{28,12},{1,17},{... | collective-permute-start | bytes 786440 | tf_op jit(solution)/shard_map/ppermute | solution.py:53
  60.1 28.9 %collective-permute-start.15 = (bf16[64,2048]{1,0:T(8,128)(2,1)S(1)}, bf16[64,2048]{1,0:T(8,128)(2,1)S(1)}, u32[]{:S(2)}, u32[]{:S(2)}) collective-permute-start(bf16[64,2048]{1,0:T(8,128)(2,1)S(1)} %slice.17), channel_id=1, source_target_pairs={{0,8},{4,12},{8,0},{12,4},{16,24},{20,28},{24,16},{28,20},{1,9},{5... | collective-permute-start | bytes 786440 | tf_op jit(solution)/shard_map/ppermute | solution.py:53
  61.7 46.5 %collective-permute-start.16 = (bf16[128,768]{1,0:T(8,128)(2,1)S(1)}, bf16[128,768]{1,0:T(8,128)(2,1)S(1)}, u32[]{:S(2)}, u32[]{:S(2)}) collective-permute-start(bf16[128,768]{1,0:T(8,128)(2,1)S(1)} %constant_dynamic-update-slice_fusion.refs_0_), channel_id=1, source_target_pairs={{0,1},{1,2},{2,3},{3,0},{4,5},{5,6},{6,7},{7,4},{8,9},{9,10},{10,1... | collective-permute-start | bytes 589832 | tf_op jit(solution)/shard_map/ppermute | solution.py:48
  69.5 39.4 %collective-permute-start.17 = (bf16[128,768]{1,0:T(8,128)(2,1)S(1)}, bf16[128,768]{1,0:T(8,128)(2,1)S(1)}, u32[]{:S(2)}, u32[]{:S(2)}) collective-permute-start(bf16[128,768]{1,0:T(8,128)(2,1)S(1)} %constant_dynamic-update-slice_fusion.refs_0_), channel_id=1, source_target_pairs={{0,2},{1,3},{2,0},{3,1},{4,6},{5,7},{6,4},{7,5},{8,10},{9,11},{10,... | collective-permute-start | bytes 589832 | tf_op jit(solution)/shard_map/ppermute | solution.py:48
  69.5 40.1 %collective-permute-start.18 = (bf16[128,768]{1,0:T(8,128)(2,1)S(1)}, bf16[128,768]{1,0:T(8,128)(2,1)S(1)}, u32[]{:S(2)}, u32[]{:S(2)}) collective-permute-start(bf16[128,768]{1,0:T(8,128)(2,1)S(1)} %constant_dynamic-update-slice_fusion.refs_0_), channel_id=1, source_target_pairs={{0,3},{1,0},{2,1},{3,2},{4,7},{5,4},{6,5},{7,6},{8,11},{9,8},{10,9... | collective-permute-start | bytes 589832 | tf_op jit(solution)/shard_map/ppermute | solution.py:48
  88.4 40.1 %collective-permute-start.24 = (bf16[128,4096]{1,0:T(8,128)(2,1)}, bf16[128,4096]{1,0:T(8,128)(2,1)}, u32[]{:S(2)}, u32[]{:S(2)}) collective-permute-start(bf16[128,4096]{1,0:T(8,128)(2,1)} %get-tuple-element.88.grad_ref.refs_0_), channel_id=1, source_target_pairs={{0,8},{4,12},{8,0},{12,4},{16,24},{20,28},{24,16},{28,20},{1,9},{5... | collective-permute-start | bytes 3145736 | tf_op jit(solution)/shard_map/ppermute | solution.py:53
  110.2 9.2 %collective-permute-start.19 = (bf16[32,3200]{1,0:T(8,128)(2,1)}, bf16[32,3200]{1,0:T(8,128)(2,1)S(1)}, u32[]{:S(2)}, u32[]{:S(2)}) collective-permute-start(bf16[32,3200]{1,0:T(8,128)(2,1)} %get-tuple-element.74), channel_id=1, source_target_pairs={{0,3},{1,0},{2,1},{3,2},{4,7},{5,4},{6,5},{7,6},{8,11},{9,8},{10,9... | collective-permute-start | bytes 614408 | tf_op jit(solution)/shard_map/ppermute | solution.py:48
  110.3 16.6 %collective-permute-start.20 = (bf16[32,3200]{1,0:T(8,128)(2,1)}, bf16[32,3200]{1,0:T(8,128)(2,1)}, u32[]{:S(2)}, u32[]{:S(2)}) collective-permute-start(bf16[32,3200]{1,0:T(8,128)(2,1)} %get-tuple-element.76), channel_id=1, source_target_pairs={{0,2},{1,3},{2,0},{3,1},{4,6},{5,7},{6,4},{7,5},{8,10},{9,11},{10,... | collective-permute-start | bytes 614408 | tf_op jit(solution)/shard_map/ppermute | solution.py:48
  112.1 14.8 %collective-permute-start.21 = (bf16[32,3200]{1,0:T(8,128)(2,1)}, bf16[32,3200]{1,0:T(8,128)(2,1)}, u32[]{:S(2)}, u32[]{:S(2)}) collective-permute-start(bf16[32,3200]{1,0:T(8,128)(2,1)} %get-tuple-element.78), channel_id=1, source_target_pairs={{0,1},{1,2},{2,3},{3,0},{4,5},{5,6},{6,7},{7,4},{8,9},{9,10},{10,1... | collective-permute-start | bytes 614408 | tf_op jit(solution)/shard_map/ppermute | solution.py:48
  114.0 21.8 %collective-permute-start.25 = (bf16[128,4096]{1,0:T(8,128)(2,1)S(1)}, bf16[128,4096]{1,0:T(8,128)(2,1)S(1)}, u32[]{:S(2)}, u32[]{:S(2)}) collective-permute-start(bf16[128,4096]{1,0:T(8,128)(2,1)S(1)} %copy-done.1), channel_id=1, source_target_pairs={{0,16},{4,20},{8,24},{12,28},{16,0},{20,4},{24,8},{28,12},{1,17},{... | collective-permute-start | bytes 3145736 | tf_op jit(solution)/shard_map/ppermute | solution.py:53
  128.4 17.7 %collective-permute-start.22 = (bf16[384,2048]{1,0:T(8,128)(2,1)S(1)}, bf16[384,2048]{1,0:T(8,128)(2,1)S(1)}, u32[]{:S(2)}, u32[]{:S(2)}) collective-permute-start(bf16[384,2048]{1,0:T(8,128)(2,1)S(1)} %theirs_sums.1), channel_id=1, source_target_pairs={{0,4},{4,0},{8,12},{12,8},{16,20},{20,16},{24,28},{28,24},{1,5},{5... | collective-permute-start | bytes 4718600 | tf_op jit(solution)/shard_map/ppermute | solution.py:53
  129.6 16.0 %collective-permute-start.26 = (bf16[64,4096]{1,0:T(8,128)(2,1)S(1)}, bf16[64,4096]{1,0:T(8,128)(2,1)S(1)}, u32[]{:S(2)}, u32[]{:S(2)}) collective-permute-start(bf16[64,4096]{1,0:T(8,128)(2,1)S(1)} %slice.18), channel_id=1, source_target_pairs={{0,16},{4,20},{8,24},{12,28},{16,0},{20,4},{24,8},{28,12},{1,17},{... | collective-permute-start | bytes 1572872 | tf_op jit(solution)/shard_map/ppermute | solution.py:53
  130.1 7.2 %collective-permute-start.23 = (bf16[384,512]{1,0:T(8,128)(2,1)S(1)}, bf16[384,512]{1,0:T(8,128)(2,1)S(1)}, u32[]{:S(2)}, u32[]{:S(2)}) collective-permute-start(bf16[384,512]{1,0:T(8,128)(2,1)S(1)} %get-tuple-element.87), channel_id=1, source_target_pairs={{0,4},{4,0},{8,12},{12,8},{16,20},{20,16},{24,28},{28,24},{1,5},{5... | collective-permute-start | bytes 1179656 | tf_op jit(solution)/shard_map/ppermute | solution.py:53
  130.8 20.8 %collective-permute-start.28 = (bf16[128,4096]{1,0:T(8,128)(2,1)S(1)}, bf16[128,4096]{1,0:T(8,128)(2,1)S(1)}, u32[]{:S(2)}, u32[]{:S(2)}) collective-permute-start(bf16[128,4096]{1,0:T(8,128)(2,1)S(1)} %copy-done.1), channel_id=1, source_target_pairs={{0,4},{4,0},{8,12},{12,8},{16,20},{20,16},{24,28},{28,24},{1,5},{5... | collective-permute-start | bytes 3145736 | tf_op jit(solution)/shard_map/ppermute | solution.py:53
  135.9 9.7 %collective-permute-start.27 = (bf16[64,4096]{1,0:T(8,128)(2,1)S(1)}, bf16[64,4096]{1,0:T(8,128)(2,1)S(1)}, u32[]{:S(2)}, u32[]{:S(2)}) collective-permute-start(bf16[64,4096]{1,0:T(8,128)(2,1)S(1)} %slice.19), channel_id=1, source_target_pairs={{0,8},{4,12},{8,0},{12,4},{16,24},{20,28},{24,16},{28,20},{1,9},{5... | collective-permute-start | bytes 1572872 | tf_op jit(solution)/shard_map/ppermute | solution.py:53
  137.3 14.2 %collective-permute-start.29 = (bf16[128,4096]{1,0:T(8,128)(2,1)}, bf16[128,4096]{1,0:T(8,128)(2,1)S(1)}, u32[]{:S(2)}, u32[]{:S(2)}) collective-permute-start(bf16[128,4096]{1,0:T(8,128)(2,1)} %collective-permute-done.24.refs_1_), channel_id=1, source_target_pairs={{0,4},{4,0},{8,12},{12,8},{16,20},{20,16},{24,28},{28,24},{1,5},{5... | collective-permute-start | bytes 3145736 | tf_op jit(solution)/shard_map/ppermute | solution.py:53
  145.6 6.0 %collective-permute-start.30 = (bf16[128,4096]{1,0:T(8,128)(2,1)S(1)}, bf16[128,4096]{1,0:T(8,128)(2,1)S(1)}, u32[]{:S(2)}, u32[]{:S(2)}) collective-permute-start(bf16[128,4096]{1,0:T(8,128)(2,1)S(1)} %collective-permute-done.25.refs_2_), channel_id=1, source_target_pairs={{0,4},{4,0},{8,12},{12,8},{16,20},{20,16},{24,28},{28,24},{1,5},{5... | collective-permute-start | bytes 3145736 | tf_op jit(solution)/shard_map/ppermute | solution.py:53
  145.6 6.0 %collective-permute-start.31 = (bf16[64,4096]{1,0:T(8,128)(2,1)S(1)}, bf16[64,4096]{1,0:T(8,128)(2,1)S(1)}, u32[]{:S(2)}, u32[]{:S(2)}) collective-permute-start(bf16[64,4096]{1,0:T(8,128)(2,1)S(1)} %collective-permute-done.26.refs_3_), channel_id=1, source_target_pairs={{0,4},{4,0},{8,12},{12,8},{16,20},{20,16},{24,28},{28,24},{1,5},{5... | collective-permute-start | bytes 1572872 | tf_op jit(solution)/shard_map/ppermute | solution.py:53
  146.1 5.5 %collective-permute-start.32 = (bf16[64,4096]{1,0:T(8,128)(2,1)S(1)}, bf16[64,4096]{1,0:T(8,128)(2,1)S(1)}, u32[]{:S(2)}, u32[]{:S(2)}) collective-permute-start(bf16[64,4096]{1,0:T(8,128)(2,1)S(1)} %collective-permute-done.27.refs_4_), channel_id=1, source_target_pairs={{0,4},{4,0},{8,12},{12,8},{16,20},{20,16},{24,28},{28,24},{1,5},{5... | collective-permute-start | bytes 1572872 | tf_op jit(solution)/shard_map/ppermute | solution.py:53
  (27 other events, 261.5 us)

commit v3 on v2

--- a/solution.py
+++ b/solution.py
@@ -53,18 +53,12 @@
     return lax.ppermute(block, "dp", [(i, i ^ bits) for i in range(ways)])
 
 
-def chip_gather(piece, chips):
-    rows = piece.shape[0] // 2
-    held = {0: [piece]}
-    for key in sorted(range(1, chips), key=lambda k: (k.bit_count(), k)):
-        if key.bit_count() == 1:
-            held[key] = [exchange(piece, 2 * key)]
-            continue
-        high, low = 1 << (key.bit_length() - 1), key & -key
-        upper, lower = held[key ^ high], held[key ^ low]
-        upper = upper[0] if len(upper) == 2 else upper[0][:rows]
-        lower = lower[1] if len(lower) == 2 else lower[0][rows:]
-        held[key] = [exchange(upper, 2 * high), exchange(lower, 2 * low)]
+def chip_gather(piece, chips, turned):
+    bits = [1 << k for k in range(chips.bit_length() - 1)]
+    held = {0: piece}
+    for bit in bits[::-1] if turned else bits:
+        for key in sorted(held):
+            held[key ^ bit] = exchange(held[key], 2 * bit)
     return [held[key] for key in range(chips)]
 
 
@@ -165,18 +159,21 @@
 
 
 def forward_body(
-    x_ref, gate_hbm, up_hbm, scaled_ref, hidden_ref, silu_ref, slope_ref, gate_ref, up_ref, sems
+    half, x_ref, gate_hbm, up_hbm, scaled_ref, hidden_ref, silu_ref, slope_ref, gate_ref, up_ref, sems
 ):
     width, units = gate_hbm.shape
     x = x_ref[:, :width]
     weight = x_ref[:, width : width + 1].astype(F32)
-    spans = [pl.ds(at, BLOCK) for at in range(0, units, BLOCK)]
-    groups = [
-        [(gate_hbm.at[:, span], gate_ref.at[:, span]), (up_hbm.at[:, span], up_ref.at[:, span])]
-        for span in spans
-    ]
-    for step in windowed(groups, sems, 3):
-        cols = slice(step * BLOCK, (step + 1) * BLOCK)
+    part = units // 2
+    block = min(BLOCK, part)
+    groups = []
+    for at in range(0, part, block):
+        src, dst = pl.ds(half * part + at, block), pl.ds(at, block)
+        groups.append(
+            [(gate_hbm.at[:, src], gate_ref.at[:, dst]), (up_hbm.at[:, src], up_ref.at[:, dst])]
+        )
+    for step in windowed(groups, sems, 4):
+        cols = slice(step * block, (step + 1) * block)
         gate = jnp.dot(x, gate_ref[:, cols], preferred_element_type=F32)
         up = jnp.dot(x, up_ref[:, cols], preferred_element_type=F32)
         sig = 1.0 / (1.0 + jnp.exp(-gate))
@@ -188,56 +185,61 @@
         slope_ref[:, cols] = weight * up * sig * (1.0 + gate * (1.0 - sig))
 
 
-def forward(x_all, w_gate, w_up):
+def forward(x_all, w_gate, w_up, half):
     rows = x_all.shape[0]
     width, units = w_gate.shape
-    return call(
-        forward_body,
+    part = units // 2
+    return call(
+        functools.partial(forward_body, half),
         "forward",
-        [struct((rows, units), kind) for kind in (BF16, BF16, F32, F32)],
+        [struct((rows, part), kind) for kind in (BF16, BF16, F32, F32)],
         [IN_VMEM] + [IN_HBM] * 2,
-        4 * rows * width * units,
-        4 * width * units,
-        [pltpu.VMEM(w_gate.shape, BF16)] * 2 + [pltpu.SemaphoreType.DMA((2 * (units // BLOCK),))],
-        limit=54,
+        4 * rows * width * part,
+        4 * width * part,
+        [pltpu.VMEM((width, part), BF16)] * 2
+        + [pltpu.SemaphoreType.DMA((2 * (part // min(BLOCK, part)),))],
+        limit=50,
     )(x_all, w_gate, w_up)
 
 
-def backward_body(count, *refs):
+def backward_body(half, count, *refs):
     blocks = refs[:count]
     down_hbm, hidden_ref, silu_ref, slope_ref, grad_ref, prob_ref, down_ref, sems = refs[count:]
-    rows, units = hidden_ref.shape
-    spans = [pl.ds(at, BLOCK) for at in range(0, units, BLOCK)]
-    groups = [[(down_hbm.at[span], down_ref.at[span])] for span in spans]
-    dy = jnp.concatenate([block[...] for block in blocks], axis=0)
+    rows, part = hidden_ref.shape
+    block = min(BLOCK, part)
+    groups = [
+        [(down_hbm.at[pl.ds(half * part + at, block)], down_ref.at[pl.ds(at, block)])]
+        for at in range(0, part, block)
+    ]
+    dy = jnp.concatenate([ref[...] for ref in blocks], axis=0)
     prob = jnp.zeros((rows, 1), F32)
-    for step in windowed(groups, sems, 5):
-        at = step * BLOCK
-        cols = slice(at, at + BLOCK)
+    for step in windowed(groups, sems, 4):
+        at = step * block
+        cols = slice(at, at + block)
         raw = nt_dot(dy, down_ref[cols, :])
         grad_ref[:, cols] = (raw * slope_ref[:, cols]).astype(BF16)
-        grad_ref[:, units + at : units + at + BLOCK] = (raw * silu_ref[:, cols]).astype(BF16)
+        grad_ref[:, part + at : part + at + block] = (raw * silu_ref[:, cols]).astype(BF16)
         prob = prob + jnp.sum(hidden_ref[:, cols].astype(F32) * raw, axis=1, keepdims=True)
     prob_ref[...] = prob
 
 
-def backward(dy_blocks, w_down, hidden, silu, slope):
+def backward(dy_blocks, w_down, hidden, silu, slope, half):
     count = len(dy_blocks)
-    rows, units = hidden.shape
+    rows, part = hidden.shape
     width = w_down.shape[1]
     return call(
-        functools.partial(backward_body, count),
+        functools.partial(backward_body, half, count),
         "backward",
-        [struct((rows, 2 * units)), struct((rows, 1), F32)],
+        [struct((rows, 2 * part)), struct((rows, 1), F32)],
         [IN_VMEM] * count + [IN_HBM] + [IN_VMEM] * 3,
-        2 * rows * width * units,
-        2 * width * units + 12 * rows * units,
-        [pltpu.VMEM(w_down.shape, BF16), pltpu.SemaphoreType.DMA((units // BLOCK,))],
-        limit=54,
+        2 * rows * width * part,
+        2 * width * part + 12 * rows * part,
+        [pltpu.VMEM((part, width), BF16), pltpu.SemaphoreType.DMA((part // min(BLOCK, part),))],
+        limit=50,
     )(*dy_blocks, w_down, hidden, silu, slope)
 
 
-def token_body(count, gate_hbm, up_hbm, grad_ref, prob_ref, *refs):
+def token_body(count, gate_hbm, up_hbm, grad_a, grad_b, prob_a, prob_b, *refs):
     outs = refs[:count]
     gate_w, up_w, sems = refs[count:]
     width, units = gate_hbm.shape
@@ -245,7 +247,7 @@
     groups = [
         [(gate_hbm.at[span], gate_w.at[span]), (up_hbm.at[span], up_w.at[span])] for span in spans
     ]
-    prob = prob_ref[...]
+    prob = prob_a[...] + prob_b[...]
     high = prob.astype(BF16).astype(F32)
     mid = (prob - high).astype(BF16).astype(F32)
     low = prob - high - mid
@@ -255,8 +257,9 @@
     ).astype(BF16)
     for z in range(count):
         outs[z][:, width:] = terms[z * LOC_CAP : (z + 1) * LOC_CAP]
-    gate = grad_ref[:, :units]
-    up = grad_ref[:, units:]
+    part = units // 2
+    gate = jnp.concatenate([grad_a[:, :part], grad_b[:, :part]], axis=1)
+    up = jnp.concatenate([grad_a[:, part:], grad_b[:, part:]], axis=1)
     for step in windowed(groups, sems, 4):
         cols = slice(step * BLOCK, (step + 1) * BLOCK)
         share = (nt_dot(gate, gate_w[cols, :]) + nt_dot(up, up_w[cols, :])).astype(BF16)
@@ -264,19 +267,19 @@
             outs[z][:, cols] = share[z * LOC_CAP : (z + 1) * LOC_CAP]
 
 
-def token_shares(w_gate, w_up, grad, prob, count):
+def token_shares(w_gate, w_up, grads, probs, count):
     width, units = w_gate.shape
     rows = count * LOC_CAP
     return call(
         functools.partial(token_body, count),
         "token_shares",
         [struct((LOC_CAP, width + LANES))] * count,
-        [IN_HBM] * 2 + [IN_VMEM] * 2,
+        [IN_HBM] * 2 + [IN_VMEM] * 4,
         4 * rows * width * units,
         4 * width * units,
         [pltpu.VMEM(w_gate.shape, BF16)] * 2 + [pltpu.SemaphoreType.DMA((2 * (width // BLOCK),))],
         limit=54,
-    )(w_gate, w_up, grad, prob)
+    )(w_gate, w_up, *grads, *probs)
 
 
 def place_body(*refs):
@@ -376,55 +379,74 @@
     return pl.BlockSpec(array.shape, lambda j: (0, 0))
 
 
-def theirs_body(left_ref, *refs):
+def half_specs(parts, block, steps, half):
+    at = (lambda j: jnp.minimum(j, steps - 1)) if half == 0 else (lambda j: jnp.maximum(j - steps, 0))
+    return [pl.BlockSpec((part.shape[0], block), lambda j: (0, at(j))) for part in parts]
+
+
+def theirs_body(chips, steps, left_ref, *refs):
     out_ref = refs[-1]
-    depth = sum(ref.shape[0] for ref in refs[:-1])
-    out_ref[...] = jnp.dot(
-        left_ref[:, :depth], stacked(refs[:-1]), preferred_element_type=F32
-    ).astype(BF16)
-
-
-def theirs_sums(left, parts):
-    units = parts[0].shape[1]
-    block = min(4 * BLOCK, units)
-    depth = sum(part.shape[0] for part in parts)
-    return call(
-        theirs_body,
+    step = pl.program_id(0)
+    for mine, parts in ((step < steps, refs[:chips]), (step >= steps, refs[chips:-1])):
+
+        @pl.when(mine)
+        def _():
+            out_ref[...] = jnp.dot(
+                left_ref[...], stacked(parts), preferred_element_type=F32
+            ).astype(BF16)
+
+
+def theirs_sums(left, parts_a, parts_b):
+    part, depth = left.shape
+    units = parts_a[0].shape[1]
+    block = min(2 * BLOCK, units)
+    steps = units // block
+    return call(
+        functools.partial(theirs_body, len(parts_a), steps),
         "theirs_sums",
-        struct((left.shape[0], units)),
-        [kept(left)] + wide_specs(parts, block),
-        2 * left.shape[0] * depth * units,
-        2 * (depth + left.shape[0]) * units,
-        grid=(units // block,),
-        out_specs=pl.BlockSpec((left.shape[0], block), lambda j: (0, j)),
+        struct((part, 2 * units)),
+        [kept(left)] + half_specs(parts_a, block, steps, 0) + half_specs(parts_b, block, steps, 1),
+        4 * part * depth * units,
+        4 * (depth + part) * units,
+        grid=(2 * steps,),
+        out_specs=pl.BlockSpec((part, block), lambda j: (0, j)),
         limit=24,
-    )(left, *parts)
-
-
-def down_body(inv, left_ref, got_ref, *refs):
+    )(left, *parts_a, *parts_b)
+
+
+def down_body(inv, chips, steps, left_ref, got_ref, *refs):
     out_ref = refs[-1]
-    total = jnp.dot(left_ref[...], stacked(refs[:-1]), preferred_element_type=F32)
-    out_ref[...] = ((total + got_ref[...].astype(F32)) * inv).T.astype(BF16)
-
-
-def down_sums(left, got, parts, inv):
-    part, units = got.shape
+    step = pl.program_id(0)
+    for mine, parts in ((step < steps, refs[:chips]), (step >= steps, refs[chips:-1])):
+
+        @pl.when(mine)
+        def _():
+            total = jnp.dot(left_ref[...], stacked(parts), preferred_element_type=F32)
+            out_ref[...] = ((total + got_ref[...].astype(F32)) * inv).T.astype(BF16)
+
+
+def down_sums(left, got, parts_a, parts_b, inv):
+    part, depth = left.shape
+    units = parts_a[0].shape[1]
     block = min(2 * BLOCK, units)
-    return call(
-        functools.partial(down_body, inv),
+    steps = units // block
+    return call(
+        functools.partial(down_body, inv, len(parts_a), steps),
         "down_sums",
-        struct((units, part)),
-        [kept(left)] + wide_specs([got, *parts], block),
-        2 * left.size * units,
-        2 * (left.shape[1] + 2 * part) * units,
-        grid=(units // block,),
+        struct((2 * units, part)),
+        [kept(left), pl.BlockSpec((part, block), lambda j: (0, j))]
+        + half_specs(parts_a, block, steps, 0)
+        + half_specs(parts_b, block, steps, 1),
+        4 * part * depth * units,
+        4 * (depth + 2 * part) * units,
+        grid=(2 * steps,),
         out_specs=pl.BlockSpec((block, part), lambda j: (j, 0)),
         limit=24,
-    )(left, got, *parts)
-
-
-def pair_body(inv, count, steps, left_ref, other_ref, *refs):
-    parts, others, (gate_ref, up_ref) = refs[:count], refs[count:-2], refs[-2:]
+    )(left, got, *parts_a, *parts_b)
+
+
+def pair_body(inv, chips, steps, left_ref, other_ref, *refs):
+    parts, others, (gate_ref, up_ref) = refs[:chips], refs[chips : 2 * chips], refs[-2:]
     total = jnp.dot(left_ref[...], stacked(parts), preferred_element_type=F32)
     total = total + jnp.dot(other_ref[...], stacked(others), preferred_element_type=F32)
     total = (total * inv).astype(BF16)
@@ -438,25 +460,30 @@
         up_ref[...] = total
 
 
-def pair_sums(left, other, parts, others, inv):
-    part = left.shape[0]
-    units = parts[0].shape[1]
-    block = min(2 * BLOCK, units // 2)
-    steps = units // 2 // block
+def pair_sums(left, other, parts, others, earlier, half, inv):
+    part, depth = left.shape
+    units = parts[0].shape[1] // 2
+    block = min(2 * BLOCK, units)
+    steps = units // block
+    held = list(earlier)
+    count = 2 + 2 * len(parts)
     return call(
         functools.partial(pair_body, inv, len(parts), steps),
         "pair_sums",
-        [struct((part, units // 2))] * 2,
-        [kept(left), kept(other)] + wide_specs([*parts, *others], block),
-        4 * left.size * units,
-        4 * (left.shape[1] + part) * units,
+        [struct((part, 2 * units))] * 2,
+        [kept(left), kept(other)]
+        + wide_specs([*parts, *others], block)
+        + [pl.BlockSpec(memory_space=pl.ANY)] * len(held),
+        8 * part * depth * units,
+        8 * (depth + part) * units,
         grid=(2 * steps,),
         out_specs=[
-            pl.BlockSpec((part, block), lambda j: (0, jnp.minimum(j, steps - 1))),
-            pl.BlockSpec((part, block), lambda j: (0, jnp.maximum(j - steps, 0))),
+            pl.BlockSpec((part, block), lambda j: (0, half * steps + jnp.minimum(j, steps - 1))),
+            pl.BlockSpec((part, block), lambda j: (0, half * steps + jnp.maximum(j - steps, 0))),
         ],
+        input_output_aliases={count: 0, count + 1: 1} if held else {},
         limit=24,
-    )(left, other, *parts, *others)
+    )(left, other, *parts, *others, *held)
 
 
 def after(value, *earlier):
@@ -478,36 +505,47 @@
     dy_parts = jnp.concatenate(
         [dy_parts[0]] + [exchange(dy_parts[key], 2 * key) for key in range(1, chips)], axis=0
     )
-    x_blocks[0] = after(x_blocks[0], dy_parts)
+    dy_pack = after(dy_pack, dy_parts)
+    dy_blocks = [dy_pack] + [shift(dy_pack, step) for step in range(1, etp_ways)]
     x_all, *x_parts = join_x(chip, x_blocks, chips)
     x_slices = [x_parts[0]] + [exchange(x_parts[key], 2 * key) for key in range(1, chips)]
-    dy_pack = after(dy_pack, x_all)
-    dy_blocks = [dy_pack] + [shift(dy_pack, step) for step in range(1, etp_ways)]
-    scaled, hidden, silu, slope = forward(x_all, w_gate, w_up)
-    scaled = chip_gather(scaled, chips)
-
-    grad, prob = backward(dy_blocks, w_down, after(hidden, *x_slices[1:]), silu, slope)
-    grads = sum(chip_gather(grad, chips), [])
+    near = [x_slices[1 << k] for k in range(chips.bit_length() - 1)]
+    inputs = (x_all, after(x_all, *near, *dy_blocks[1:-1]))
+    scaled, grads, probs, kept_halves = [], [], [], []
+    for half in range(2):
+        piece, *rest = forward(inputs[half], w_gate, w_up, half)
+        scaled.append(chip_gather(piece, chips, half == 1))
+        kept_halves.append(rest)
+    for half in range(2):
+        hidden, silu, slope = kept_halves[half]
+        grad, prob = backward(dy_blocks, w_down, after(hidden, *x_slices[1:]), silu, slope, half)
+        grads.append(grad)
+        probs.append(prob)
+    parts = [chip_gather(grads[half], chips, half == 1) for half in range(2)]
     dy_parts = after(dy_parts, *dy_blocks[1:])
     dy_slices = [dy_parts] + [shift(dy_parts, step) for step in range(1, etp_ways)]
 
-    scaled = sum(scaled, [])
-    shares = token_shares(w_gate, w_up, grad, after(prob, *scaled[1:]), etp_ways)
-    shares = [after(share, *dy_slices[1:]) for share in shares]
+    probs[0] = after(probs[0], *scaled[0][1:], *scaled[1][1:], *dy_slices[1:])
+    shares = token_shares(w_gate, w_up, grads, probs, etp_ways)
     shares = [shares[0]] + [shift(shares[step], -step) for step in range(1, etp_ways)]
     grad_tokens, grad_prob = place(shares, sel)
 
     mine, theirs = turn_dy(core, dy_slices, chips)
-    theirs = after(theirs, *shares[1:])
-    got = exchange(theirs_sums(theirs, scaled), 1)
-    grad_down = down_sums(mine, got, scaled, inv)
+    theirs = after(theirs, probs[1])
+    got = exchange(theirs_sums(theirs, *scaled), 1)
+    grad_down = down_sums(mine, got, *scaled, inv)
 
     mine, theirs = turn_x(core, x_slices)
-    others = [
-        exchange(after(part, *shares[1:]) if part.shape == grad.shape else part, 1) for part in grads
-    ]
     mine = after(mine, grad_down, grad_tokens)
-    grad_gate, grad_up = pair_sums(mine, exchange(theirs, 1), grads, others, inv)
+    far = exchange(theirs, 1)
+    held = ()
+    for half in range(2):
+        others = [
+            exchange(after(part, parts[0][-1]) if key.bit_count() == 1 else part, 1)
+            for key, part in enumerate(parts[half])
+        ]
+        held = pair_sums(mine, far, parts[half], others, held, half, inv)
+    grad_gate, grad_up = held
     return (grad_tokens, grad_prob.reshape(-1), grad_gate, grad_up, grad_down)
 
 

time: 160 us -> 164 us (1.025)
  waiting for transfers between devices: 40.9 us -> 31 us
  local copies, waits for them, and re-layouts: 11.2 us -> 18.6 us
  starting transfers between devices: 45.7 us -> 51.5 us
    ppermute x21 -> x28, waiting for transfers between devices: 21 us -> 10.6 us  [exchange(): return lax.ppermute(block, 'dp', [(i, i ^ bits) for i in range(ways)])]
    unnamed x55 -> x77, local copies, waits for them, and re-layouts: 10 us -> 18 us
    ppermute x21 -> x28, starting transfers between devices: 18.1 us -> 23.9 us  [exchange(): return lax.ppermute(block, 'dp', [(i, i ^ bits) for i in range(ways)])]
    pallas_call x1 -> x2, Pallas kernels: 8.26 us -> 9.61 us  [pair_sums(): call(functools.partial(pair_body, inv, len(parts), steps), 'pair_sums', [...]
    pallas_call x4 -> x6, Pallas kernels: 29.7 us -> 28.6 us  [the longest x2 12.2 us: backward(): call(functools.partial(backward_body, half, count), 'backward', [struct((...]
  transfers between devices with their start and end apart: 33 -> 40, of which waited for: 10 -> 10; matrix products, arithmetic and copies ran while one was open for 1% -> 2% of each run, Pallas kernels for 25% -> 34%
where the time goes in v3:
time: 164 us; the launch traced here: 163 us
  Pallas kernels  61.3 us (37%)
  starting transfers between devices  51.5 us (31%)
  waiting for transfers between devices  31 us (19%)
  local copies, waits for them, and re-layouts  18.6 us (11%)
    ppermute x12, starting transfers between devices, shift(): lax.ppermute(block, 'etp', [(i, (i + step) % ways) for i in range(ways)])  27.6 us
    ppermute x28, starting transfers between devices, exchange(): return lax.ppermute(block, 'dp', [(i, i ^ bits) for i in range(ways)])  23.9 us
    ppermute x12, waiting for transfers between devices, shift(): lax.ppermute(block, 'etp', [(i, (i + step) % ways) for i in range(ways)])  20.4 us
    pallas_call x1, Pallas kernels, token_shares(): call(functools.partial(token_body, count), 'token_shares', [struct((LOC_C...  19.1 us
    unnamed x77, local copies, waits for them, and re-layouts  18 us
    pallas_call x2, Pallas kernels, backward(): call(functools.partial(backward_body, half, count), 'backward', [struct((...  12.2 us
    pallas_call x2, Pallas kernels, forward(): call(functools.partial(forward_body, half), 'forward', [struct((rows, par...  11.1 us
    ppermute x28, waiting for transfers between devices, exchange(): return lax.ppermute(block, 'dp', [(i, i ^ bits) for i in range(ways)])  10.6 us
  transfers between devices with their start and end apart: 40, of which 10 were waited for; matrix products, arithmetic and copies ran while one was open for 2% of the time, Pallas kernels for 34%

profile of v3, /device:TPU:0, one launch (start us, length us, event | category | flops | bytes accessed | tf_op | source)
XLA Modules:
  0.0 163.4 jit_solution(3533267238671717453)
XLA Ops:
  3.5 3.1 %collective-permute-start.6 = (bf16[32,3200]{1,0:T(8,128)(2,1)S(1)}, bf16[32,3200]{1,0:T(8,128)(2,1)S(1)}, u32[]{:S(2)}, u32[]{:S(2)}) collective-permute-start(bf16[32,3200]{1,0:T(8,128)(2,1)S(1)} %get-tuple-element.62.refs_0_), channel_id=1, source_target_pairs={{0,1},{1,2},{2,3},{3,0},{4,5},{5,6},{6,7},{7,4},{8,9},{9,10},{10,1... | collective-permute-start | bytes 614408 | tf_op jit(solution)/shard_map/ppermute | solution.py:48
  6.5 2.6 %collective-permute-start.7 = (bf16[32,3200]{1,0:T(8,128)(2,1)S(1)}, bf16[32,3200]{1,0:T(8,128)(2,1)S(1)}, u32[]{:S(2)}, u32[]{:S(2)}) collective-permute-start(bf16[32,3200]{1,0:T(8,128)(2,1)S(1)} %get-tuple-element.62.refs_0_), channel_id=1, source_target_pairs={{0,2},{1,3},{2,0},{3,1},{4,6},{5,7},{6,4},{7,5},{8,10},{9,11},{10,... | collective-permute-start | bytes 614408 | tf_op jit(solution)/shard_map/ppermute | solution.py:48
  11.9 1.6 collective-permute-start
  13.4 1.5 collective-permute-start.1
  16.0 2.5 %collective-permute-start.2 = (bf16[32,768]{1,0:T(8,128)(2,1)S(1)}, bf16[32,768]{1,0:T(8,128)(2,1)S(1)}, u32[]{:S(2)}, u32[]{:S(2)}) collective-permute-start(bf16[32,768]{1,0:T(8,128)(2,1)S(1)} %get-tuple-element.60), channel_id=1, source_target_pairs={{0,24},{4,28},{8,16},{12,20},{16,8},{20,12},{24,0},{28,4},{1,25},{... | collective-permute-start | bytes 147464 | tf_op jit(solution)/shard_map/ppermute | solution.py:53
  23.5 1.5 collective-permute-start.10
  25.0 1.5 collective-permute-start.9
  26.5 11.2 %collective-permute-start.5 = (bf16[32,3072]{1,0:T(8,128)(2,1)S(1)}, bf16[32,3072]{1,0:T(8,128)(2,1)S(1)}, u32[]{:S(2)}, u32[]{:S(2)}) collective-permute-start(bf16[32,3072]{1,0:T(8,128)(2,1)S(1)} %get-tuple-element.61.refs_0_), channel_id=1, source_target_pairs={{0,3},{1,0},{2,1},{3,2},{4,7},{5,4},{6,5},{7,6},{8,11},{9,8},{10,9... | collective-permute-start | bytes 589832 | tf_op jit(solution)/shard_map/ppermute | solution.py:48
  37.6 5.5 %forward.2 = (bf16[128,1024]{1,0:T(8,128)(2,1)S(1)}, bf16[128,1024]{1,0:T(8,128)(2,1)S(1)}, f32[128,1024]{1,0:T(8,128)S(1)}, f32[128,1024]{1,0:T(8,128)S(1)}) custom-call(bf16[128,3200]{1,0:T(8,128)(2,1)S(1)} %get-tuple-element.72.x_ref, bf16[3072,2048]{1,0:T(8,128)(2,1)} %gate_hbm.5, bf16[3072,2048]{1,0:T(8,128)(2,1)} %up_hbm.5), custom_call_target="tpu_custom_call" | custom-call | flops 1610612736 | bytes 12582912 | tf_op jit(solution)/shard_map/forward/pallas_call | solution.py:192
  45.9 5.6 %forward.3 = (bf16[128,1024]{1,0:T(8,128)(2,1)S(1)}, bf16[128,1024]{1,0:T(8,128)(2,1)S(1)}, f32[128,1024]{1,0:T(8,128)S(1)}, f32[128,1024]{1,0:T(8,128)S(1)}) custom-call(bf16[128,3200]{1,0:T(8,128)(2,1)S(1)} %get-tuple-element.72.x_ref, bf16[3072,2048]{1,0:T(8,128)(2,1)} %gate_hbm.5, bf16[3072,2048]{1,0:T(8,128)(2,1)} %up_hbm.5), custom_call_target="tpu_custom_call" | custom-call | flops 1610612736 | bytes 12582912 | tf_op jit(solution)/shard_map/forward/pallas_call | solution.py:192
  54.3 2.5 %collective-permute-start.11 = (bf16[128,768]{1,0:T(8,128)(2,1)S(1)}, bf16[128,768]{1,0:T(8,128)(2,1)S(1)}, u32[]{:S(2)}, u32[]{:S(2)}) collective-permute-start(bf16[128,768]{1,0:T(8,128)(2,1)S(1)} %get-tuple-element.67), channel_id=1, source_target_pairs={{0,24},{4,28},{8,16},{12,20},{16,8},{20,12},{24,0},{28,4},{1,25},{... | collective-permute-start | bytes 589832 | tf_op jit(solution)/shard_map/ppermute | solution.py:53
  56.8 2.1 %collective-permute-start.18 = (bf16[128,768]{1,0:T(8,128)(2,1)}, bf16[128,768]{1,0:T(8,128)(2,1)S(1)}, u32[]{:S(2)}, u32[]{:S(2)}) collective-permute-start(bf16[128,768]{1,0:T(8,128)(2,1)} %constant_dynamic-update-slice_fusion.refs_0_), channel_id=1, source_target_pairs={{0,1},{1,2},{2,3},{3,0},{4,5},{5,6},{6,7},{7,4},{8,9},{9,10},{10,1... | collective-permute-start | bytes 589832 | tf_op jit(solution)/shard_map/ppermute | solution.py:48
  61.6 1.5 collective-permute-start.13
  63.1 3.1 %collective-permute-done.18.refs_1_ = bf16[128,768]{1,0:T(8,128)(2,1)S(1)} collective-permute-done((bf16[128,768]{1,0:T(8,128)(2,1)}, bf16[128,768]{1,0:T(8,128)(2,1)S(1)}, u32[]{:S(2)}, u32[]{:S(2)}) %collective-permute-start.18) | collective-permute-done | bytes 196640 | tf_op jit(solution)/shard_map/ppermute | solution.py:48
  68.0 1.5 collective-permute-start.17
  69.5 1.8 %collective-permute-done.19.refs_2_ = bf16[128,768]{1,0:T(8,128)(2,1)S(1)} collective-permute-done((bf16[128,768]{1,0:T(8,128)(2,1)}, bf16[128,768]{1,0:T(8,128)(2,1)S(1)}, u32[]{:S(2)}, u32[]{:S(2)}) %collective-permute-start.19) | collective-permute-done | bytes 196640 | tf_op jit(solution)/shard_map/ppermute | solution.py:48
  72.0 3.6 %collective-permute-start.20 = (bf16[128,768]{1,0:T(8,128)(2,1)}, bf16[128,768]{1,0:T(8,128)(2,1)}, u32[]{:S(2)}, u32[]{:S(2)}) collective-permute-start(bf16[128,768]{1,0:T(8,128)(2,1)} %constant_dynamic-update-slice_fusion.refs_0_), channel_id=1, source_target_pairs={{0,3},{1,0},{2,1},{3,2},{4,7},{5,4},{6,5},{7,6},{8,11},{9,8},{10,9... | collective-permute-start | bytes 589832 | tf_op jit(solution)/shard_map/ppermute | solution.py:48
  78.6 6.5 %backward.3 = (bf16[128,2048]{1,0:T(8,128)(2,1)}, f32[128,1]{1,0:T(8,128)S(1)}) custom-call(bf16[32,3072]{1,0:T(8,128)(2,1)S(1)} %get-tuple-element.61.refs_0_, bf16[32,3072]{1,0:T(8,128)(2,1)S(1)} %collective-permute-done.3.refs_1_, bf16[32,3072]{1,0:T(8,128)(2,1)S(1)} %collective-permute-done.4.refs_2_, ...), custom_call_target="tpu_custom_call" | custom-call | flops 805306368 | bytes 7864320 | tf_op jit(solution)/shard_map/backward/pallas_call | solution.py:230
  85.7 5.8 %backward.2 = (bf16[128,2048]{1,0:T(8,128)(2,1)S(1)}, f32[128,1]{1,0:T(8,128)S(1)}) custom-call(bf16[32,3072]{1,0:T(8,128)(2,1)S(1)} %get-tuple-element.61.refs_0_, bf16[32,3072]{1,0:T(8,128)(2,1)S(1)} %collective-permute-done.3.refs_1_, bf16[32,3072]{1,0:T(8,128)(2,1)S(1)} %collective-permute-done.4.refs_2_, ...), custom_call_target="tpu_custom_call" | custom-call | flops 805306368 | bytes 7864320 | tf_op jit(solution)/shard_map/backward/pallas_call | solution.py:230
  92.1 1.6 turn_dy.1
  94.4 2.0 %theirs_sums.1 = bf16[384,2048]{1,0:T(8,128)(2,1)S(1)} custom-call(bf16[384,512]{1,0:T(8,128)(2,1)S(1)} %get-tuple-element.94.left_ref, bf16[128,1024]{1,0:T(8,128)(2,1)S(1)} %get-tuple-element.79.refs_0_, bf16[128,1024]{1,0:T(8,128)(2,1)S(1)} %collective-permute-done.12.refs_1_, bf16[128,1024]{1,0:T(8,128)(2,1)S(1)} %collective-permute-done.13.refs_2_, ...), custom_call_target="tpu_custom_call" | custom-call | flops 805306368 | bytes 3670016 | tf_op jit(solution)/shard_map/theirs_sums/pallas_call | solution.py:404
  97.6 5.2 %collective-permute-done.30.refs_1_ = bf16[128,2048]{1,0:T(8,128)(2,1)S(1)} collective-permute-done((bf16[128,2048]{1,0:T(8,128)(2,1)S(1)}, bf16[128,2048]{1,0:T(8,128)(2,1)S(1)}, u32[]{:S(2)}, u32[]{:S(2)}) %collective-permute-start.30) | collective-permute-done | bytes 524320 | tf_op jit(solution)/shard_map/ppermute | solution.py:53
  103.2 1.6 collective-permute-start.27
  104.8 3.0 %collective-permute-done.35.refs_2_ = bf16[128,2048]{1,0:T(8,128)(2,1)S(1)} collective-permute-done((bf16[128,2048]{1,0:T(8,128)(2,1)S(1)}, bf16[128,2048]{1,0:T(8,128)(2,1)S(1)}, u32[]{:S(2)}, u32[]{:S(2)}) %collective-permute-start.35) | collective-permute-done | bytes 524320 | tf_op jit(solution)/shard_map/ppermute | solution.py:53
  107.8 2.4 %collective-permute-start.26 = (bf16[128,2048]{1,0:T(8,128)(2,1)}, bf16[128,2048]{1,0:T(8,128)(2,1)S(1)}, u32[]{:S(2)}, u32[]{:S(2)}) collective-permute-start(bf16[128,2048]{1,0:T(8,128)(2,1)} %get-tuple-element.77.grad_b.refs_0_), channel_id=1, source_target_pairs={{0,8},{4,12},{8,0},{12,4},{16,24},{20,28},{24,16},{28,20},{1,9},{5... | collective-permute-start | bytes 1572872 | tf_op jit(solution)/shard_map/ppermute | solution.py:53
  110.2 19.1 %token_shares.1 = (bf16[32,3200]{1,0:T(8,128)(2,1)}, bf16[32,3200]{1,0:T(8,128)(2,1)}, bf16[32,3200]{1,0:T(8,128)(2,1)}, bf16[32,3200]{1,0:T(8,128)(2,1)}) custom-call(bf16[3072,2048]{1,0:T(8,128)(2,1)} %gate_hbm.5, bf16[3072,2048]{1,0:T(8,128)(2,1)} %up_hbm.5, bf16[128,2048]{1,0:T(8,128)(2,1)} %copy-done.2, ...), custom_call_target="tpu_custom_call" | custom-call | flops 3221225472 | bytes 25165824 | tf_op jit(solution)/shard_map/token_shares/pallas_call | solution.py:273
  130.4 7.2 %collective-permute-done.21.refs_1_ = bf16[32,3200]{1,0:T(8,128)(2,1)S(1)} collective-permute-done((bf16[32,3200]{1,0:T(8,128)(2,1)}, bf16[32,3200]{1,0:T(8,128)(2,1)S(1)}, u32[]{:S(2)}, u32[]{:S(2)}) %collective-permute-start.21) | collective-permute-done | bytes 204832 | tf_op jit(solution)/shard_map/ppermute | solution.py:48
  137.6 1.6 collective-permute-done.22.refs_2_
  140.5 6.7 %collective-permute-done.23.refs_3_ = bf16[32,3200]{1,0:T(8,128)(2,1)S(1)} collective-permute-done((bf16[32,3200]{1,0:T(8,128)(2,1)}, bf16[32,3200]{1,0:T(8,128)(2,1)S(1)}, u32[]{:S(2)}, u32[]{:S(2)}) %collective-permute-start.23) | collective-permute-done | bytes 204832 | tf_op jit(solution)/shard_map/ppermute | solution.py:48
  150.5 3.2 %down_sums.1 = bf16[2048,384]{1,0:T(8,128)(2,1)} custom-call(bf16[384,512]{1,0:T(8,128)(2,1)S(1)} %get-tuple-element.92.left_ref, bf16[384,2048]{1,0:T(8,128)(2,1)S(1)} %collective-permute-done.24.got_ref, bf16[128,1024]{1,0:T(8,128)(2,1)S(1)} %get-tuple-element.79.refs_0_, bf16[128,1024]{1,0:T(8,128)(2,1)S(1)} %collective-permute-done.12.refs_1_, ...), custom_call_target="tpu_custom_call" | custom-call | flops 805306368 | bytes 5242880 | tf_op jit(solution)/shard_map/down_sums/pallas_call | solution.py:433
  153.8 4.8 %pair_sums.2 = (bf16[384,2048]{1,0:T(8,128)(2,1)}, bf16[384,2048]{1,0:T(8,128)(2,1)}) custom-call(bf16[384,512]{1,0:T(8,128)(2,1)S(1)} %get-tuple-element.95.left_ref, bf16[384,512]{1,0:T(8,128)(2,1)S(1)} %collective-permute-done.25.other_ref, bf16[128,2048]{1,0:T(8,128)(2,1)S(1)} %copy-done.3, bf16[128,2048]{1,0:T(8,128)(2,1)S(1)} %copy-done.32, ...), custom_call_target="tpu_custom_call" | custom-call | flops 1610612736 | bytes 7340032 | tf_op jit(solution)/shard_map/pair_sums/pallas_call | solution.py:470
  158.6 4.8 %pair_sums.3 = (bf16[384,2048]{1,0:T(8,128)(2,1)}, bf16[384,2048]{1,0:T(8,128)(2,1)}) custom-call(bf16[384,512]{1,0:T(8,128)(2,1)S(1)} %get-tuple-element.95.left_ref, bf16[384,512]{1,0:T(8,128)(2,1)S(1)} %collective-permute-done.25.other_ref, bf16[128,2048]{1,0:T(8,128)(2,1)} %get-tuple-element.77.grad_b.refs_0_, ...), custom_call_target="tpu_custom_call", output_to_operand_aliasing={{0}: (10, {}), {1}: (11, {})} | custom-call | flops 1610612736 | bytes 7340032 | tf_op jit(solution)/shard_map/pair_sums/pallas_call | solution.py:470
  (141 shorter events, 34.5 us)
Async XLA Ops:
  3.5 19.2 %collective-permute-start.6 = (bf16[32,3200]{1,0:T(8,128)(2,1)S(1)}, bf16[32,3200]{1,0:T(8,128)(2,1)S(1)}, u32[]{:S(2)}, u32[]{:S(2)}) collective-permute-start(bf16[32,3200]{1,0:T(8,128)(2,1)S(1)} %get-tuple-element.62.refs_0_), channel_id=1, source_target_pairs={{0,1},{1,2},{2,3},{3,0},{4,5},{5,6},{6,7},{7,4},{8,9},{9,10},{10,1... | collective-permute-start | bytes 614408 | tf_op jit(solution)/shard_map/ppermute | solution.py:48
  6.5 16.1 %collective-permute-start.7 = (bf16[32,3200]{1,0:T(8,128)(2,1)S(1)}, bf16[32,3200]{1,0:T(8,128)(2,1)S(1)}, u32[]{:S(2)}, u32[]{:S(2)}) collective-permute-start(bf16[32,3200]{1,0:T(8,128)(2,1)S(1)} %get-tuple-element.62.refs_0_), channel_id=1, source_target_pairs={{0,2},{1,3},{2,0},{3,1},{4,6},{5,7},{6,4},{7,5},{8,10},{9,11},{10,... | collective-permute-start | bytes 614408 | tf_op jit(solution)/shard_map/ppermute | solution.py:48
  9.1 13.5 %collective-permute-start.8 = (bf16[32,3200]{1,0:T(8,128)(2,1)S(1)}, bf16[32,3200]{1,0:T(8,128)(2,1)S(1)}, u32[]{:S(2)}, u32[]{:S(2)}) collective-permute-start(bf16[32,3200]{1,0:T(8,128)(2,1)S(1)} %get-tuple-element.62.refs_0_), channel_id=1, source_target_pairs={{0,3},{1,0},{2,1},{3,2},{4,7},{5,4},{6,5},{7,6},{8,11},{9,8},{10,9... | collective-permute-start | bytes 614408 | tf_op jit(solution)/shard_map/ppermute | solution.py:48
  21.6 23.1 %collective-permute-start.3 = (bf16[32,3072]{1,0:T(8,128)(2,1)S(1)}, bf16[32,3072]{1,0:T(8,128)(2,1)S(1)}, u32[]{:S(2)}, u32[]{:S(2)}) collective-permute-start(bf16[32,3072]{1,0:T(8,128)(2,1)S(1)} %get-tuple-element.61.refs_0_), channel_id=1, source_target_pairs={{0,1},{1,2},{2,3},{3,0},{4,5},{5,6},{6,7},{7,4},{8,9},{9,10},{10,1... | collective-permute-start | bytes 589832 | tf_op jit(solution)/shard_map/ppermute | solution.py:48
  22.3 22.9 %collective-permute-start.4 = (bf16[32,3072]{1,0:T(8,128)(2,1)S(1)}, bf16[32,3072]{1,0:T(8,128)(2,1)S(1)}, u32[]{:S(2)}, u32[]{:S(2)}) collective-permute-start(bf16[32,3072]{1,0:T(8,128)(2,1)S(1)} %get-tuple-element.61.refs_0_), channel_id=1, source_target_pairs={{0,2},{1,3},{2,0},{3,1},{4,6},{5,7},{6,4},{7,5},{8,10},{9,11},{10,... | collective-permute-start | bytes 589832 | tf_op jit(solution)/shard_map/ppermute | solution.py:48
  23.5 21.8 %collective-permute-start.10 = (bf16[128,768]{1,0:T(8,128)(2,1)S(1)}, bf16[128,768]{1,0:T(8,128)(2,1)S(1)}, u32[]{:S(2)}, u32[]{:S(2)}) collective-permute-start(bf16[128,768]{1,0:T(8,128)(2,1)S(1)} %get-tuple-element.66), channel_id=1, source_target_pairs={{0,16},{4,20},{8,24},{12,28},{16,0},{20,4},{24,8},{28,12},{1,17},{... | collective-permute-start | bytes 589832 | tf_op jit(solution)/shard_map/ppermute | solution.py:53
  25.0 20.9 %collective-permute-start.9 = (bf16[128,768]{1,0:T(8,128)(2,1)S(1)}, bf16[128,768]{1,0:T(8,128)(2,1)S(1)}, u32[]{:S(2)}, u32[]{:S(2)}) collective-permute-start(bf16[128,768]{1,0:T(8,128)(2,1)S(1)} %get-tuple-element.65), channel_id=1, source_target_pairs={{0,8},{4,12},{8,0},{12,4},{16,24},{20,28},{24,16},{28,20},{1,9},{5... | collective-permute-start | bytes 589832 | tf_op jit(solution)/shard_map/ppermute | solution.py:53
  26.5 30.3 %collective-permute-start.5 = (bf16[32,3072]{1,0:T(8,128)(2,1)S(1)}, bf16[32,3072]{1,0:T(8,128)(2,1)S(1)}, u32[]{:S(2)}, u32[]{:S(2)}) collective-permute-start(bf16[32,3072]{1,0:T(8,128)(2,1)S(1)} %get-tuple-element.61.refs_0_), channel_id=1, source_target_pairs={{0,3},{1,0},{2,1},{3,2},{4,7},{5,4},{6,5},{7,6},{8,11},{9,8},{10,9... | collective-permute-start | bytes 589832 | tf_op jit(solution)/shard_map/ppermute | solution.py:48
  44.7 22.8 %collective-permute-start.12 = (bf16[128,1024]{1,0:T(8,128)(2,1)S(1)}, bf16[128,1024]{1,0:T(8,128)(2,1)S(1)}, u32[]{:S(2)}, u32[]{:S(2)}) collective-permute-start(bf16[128,1024]{1,0:T(8,128)(2,1)S(1)} %get-tuple-element.79.refs_0_), channel_id=1, source_target_pairs={{0,8},{4,12},{8,0},{12,4},{16,24},{20,28},{24,16},{28,20},{1,9},{5... | collective-permute-start | bytes 786440 | tf_op jit(solution)/shard_map/ppermute | solution.py:53
  53.8 14.2 %collective-permute-start.16 = (bf16[128,1024]{1,0:T(8,128)(2,1)S(1)}, bf16[128,1024]{1,0:T(8,128)(2,1)S(1)}, u32[]{:S(2)}, u32[]{:S(2)}) collective-permute-start(bf16[128,1024]{1,0:T(8,128)(2,1)S(1)} %get-tuple-element.80.refs_4_), channel_id=1, source_target_pairs={{0,16},{4,20},{8,24},{12,28},{16,0},{20,4},{24,8},{28,12},{1,17},{... | collective-permute-start | bytes 786440 | tf_op jit(solution)/shard_map/ppermute | solution.py:53
  56.8 9.5 %collective-permute-start.18 = (bf16[128,768]{1,0:T(8,128)(2,1)}, bf16[128,768]{1,0:T(8,128)(2,1)S(1)}, u32[]{:S(2)}, u32[]{:S(2)}) collective-permute-start(bf16[128,768]{1,0:T(8,128)(2,1)} %constant_dynamic-update-slice_fusion.refs_0_), channel_id=1, source_target_pairs={{0,1},{1,2},{2,3},{3,0},{4,5},{5,6},{6,7},{7,4},{8,9},{9,10},{10,1... | collective-permute-start | bytes 589832 | tf_op jit(solution)/shard_map/ppermute | solution.py:48
  58.8 12.4 %collective-permute-start.19 = (bf16[128,768]{1,0:T(8,128)(2,1)}, bf16[128,768]{1,0:T(8,128)(2,1)S(1)}, u32[]{:S(2)}, u32[]{:S(2)}) collective-permute-start(bf16[128,768]{1,0:T(8,128)(2,1)} %constant_dynamic-update-slice_fusion.refs_0_), channel_id=1, source_target_pairs={{0,2},{1,3},{2,0},{3,1},{4,6},{5,7},{6,4},{7,5},{8,10},{9,11},{10,... | collective-permute-start | bytes 589832 | tf_op jit(solution)/shard_map/ppermute | solution.py:48
  61.6 32.2 %collective-permute-start.13 = (bf16[128,1024]{1,0:T(8,128)(2,1)S(1)}, bf16[128,1024]{1,0:T(8,128)(2,1)S(1)}, u32[]{:S(2)}, u32[]{:S(2)}) collective-permute-start(bf16[128,1024]{1,0:T(8,128)(2,1)S(1)} %get-tuple-element.79.refs_0_), channel_id=1, source_target_pairs={{0,16},{4,20},{8,24},{12,28},{16,0},{20,4},{24,8},{28,12},{1,17},{... | collective-permute-start | bytes 786440 | tf_op jit(solution)/shard_map/ppermute | solution.py:53
  66.9 27.4 %collective-permute-start.15 = (bf16[128,1024]{1,0:T(8,128)(2,1)S(1)}, bf16[128,1024]{1,0:T(8,128)(2,1)S(1)}, u32[]{:S(2)}, u32[]{:S(2)}) collective-permute-start(bf16[128,1024]{1,0:T(8,128)(2,1)S(1)} %get-tuple-element.80.refs_4_), channel_id=1, source_target_pairs={{0,8},{4,12},{8,0},{12,4},{16,24},{20,28},{24,16},{28,20},{1,9},{5... | collective-permute-start | bytes 786440 | tf_op jit(solution)/shard_map/ppermute | solution.py:53
  67.5 26.9 %collective-permute-start.14 = (bf16[128,1024]{1,0:T(8,128)(2,1)S(1)}, bf16[128,1024]{1,0:T(8,128)(2,1)S(1)}, u32[]{:S(2)}, u32[]{:S(2)}) collective-permute-start(bf16[128,1024]{1,0:T(8,128)(2,1)S(1)} %collective-permute-done.12.refs_1_), channel_id=1, source_target_pairs={{0,16},{4,20},{8,24},{12,28},{16,0},{20,4},{24,8},{28,12},{1,17},{... | collective-permute-start | bytes 786440 | tf_op jit(solution)/shard_map/ppermute | solution.py:53
  68.0 26.4 %collective-permute-start.17 = (bf16[128,1024]{1,0:T(8,128)(2,1)S(1)}, bf16[128,1024]{1,0:T(8,128)(2,1)S(1)}, u32[]{:S(2)}, u32[]{:S(2)}) collective-permute-start(bf16[128,1024]{1,0:T(8,128)(2,1)S(1)} %collective-permute-done.16.refs_6_), channel_id=1, source_target_pairs={{0,8},{4,12},{8,0},{12,4},{16,24},{20,28},{24,16},{28,20},{1,9},{5... | collective-permute-start | bytes 786440 | tf_op jit(solution)/shard_map/ppermute | solution.py:53
  72.0 19.5 %collective-permute-start.20 = (bf16[128,768]{1,0:T(8,128)(2,1)}, bf16[128,768]{1,0:T(8,128)(2,1)}, u32[]{:S(2)}, u32[]{:S(2)}) collective-permute-start(bf16[128,768]{1,0:T(8,128)(2,1)} %constant_dynamic-update-slice_fusion.refs_0_), channel_id=1, source_target_pairs={{0,3},{1,0},{2,1},{3,2},{4,7},{5,4},{6,5},{7,6},{8,11},{9,8},{10,9... | collective-permute-start | bytes 589832 | tf_op jit(solution)/shard_map/ppermute | solution.py:48
  91.5 11.3 %collective-permute-start.30 = (bf16[128,2048]{1,0:T(8,128)(2,1)S(1)}, bf16[128,2048]{1,0:T(8,128)(2,1)S(1)}, u32[]{:S(2)}, u32[]{:S(2)}) collective-permute-start(bf16[128,2048]{1,0:T(8,128)(2,1)S(1)} %get-tuple-element.71.grad_a.refs_0_), channel_id=1, source_target_pairs={{0,8},{4,12},{8,0},{12,4},{16,24},{20,28},{24,16},{28,20},{1,9},{5... | collective-permute-start | bytes 1572872 | tf_op jit(solution)/shard_map/ppermute | solution.py:53
  93.8 14.0 %collective-permute-start.35 = (bf16[128,2048]{1,0:T(8,128)(2,1)S(1)}, bf16[128,2048]{1,0:T(8,128)(2,1)S(1)}, u32[]{:S(2)}, u32[]{:S(2)}) collective-permute-start(bf16[128,2048]{1,0:T(8,128)(2,1)S(1)} %get-tuple-element.71.grad_a.refs_0_), channel_id=1, source_target_pairs={{0,16},{4,20},{8,24},{12,28},{16,0},{20,4},{24,8},{28,12},{1,17},{... | collective-permute-start | bytes 1572872 | tf_op jit(solution)/shard_map/ppermute | solution.py:53
  96.4 51.9 %collective-permute-start.24 = (bf16[384,2048]{1,0:T(8,128)(2,1)S(1)}, bf16[384,2048]{1,0:T(8,128)(2,1)S(1)}, u32[]{:S(2)}, u32[]{:S(2)}) collective-permute-start(bf16[384,2048]{1,0:T(8,128)(2,1)S(1)} %theirs_sums.1), channel_id=1, source_target_pairs={{0,4},{4,0},{8,12},{12,8},{16,20},{20,16},{24,28},{28,24},{1,5},{5... | collective-permute-start | bytes 4718600 | tf_op jit(solution)/shard_map/ppermute | solution.py:53
  97.6 31.7 %collective-permute-start.36 = (bf16[128,2048]{1,0:T(8,128)(2,1)S(1)}, bf16[128,2048]{1,0:T(8,128)(2,1)S(1)}, u32[]{:S(2)}, u32[]{:S(2)}) collective-permute-start(bf16[128,2048]{1,0:T(8,128)(2,1)S(1)} %get-tuple-element.71.grad_a.refs_0_), channel_id=1, source_target_pairs={{0,4},{4,0},{8,12},{12,8},{16,20},{20,16},{24,28},{28,24},{1,5},{5... | collective-permute-start | bytes 1572872 | tf_op jit(solution)/shard_map/ppermute | solution.py:53
  102.8 27.3 %collective-permute-start.31 = (bf16[128,2048]{1,0:T(8,128)(2,1)S(1)}, bf16[128,2048]{1,0:T(8,128)(2,1)}, u32[]{:S(2)}, u32[]{:S(2)}) collective-permute-start(bf16[128,2048]{1,0:T(8,128)(2,1)S(1)} %collective-permute-done.30.refs_1_), channel_id=1, source_target_pairs={{0,16},{4,20},{8,24},{12,28},{16,0},{20,4},{24,8},{28,12},{1,17},{... | collective-permute-start | bytes 1572872 | tf_op jit(solution)/shard_map/ppermute | solution.py:53
  103.2 26.9 %collective-permute-start.27 = (bf16[128,2048]{1,0:T(8,128)(2,1)}, bf16[128,2048]{1,0:T(8,128)(2,1)S(1)}, u32[]{:S(2)}, u32[]{:S(2)}) collective-permute-start(bf16[128,2048]{1,0:T(8,128)(2,1)} %get-tuple-element.77.grad_b.refs_0_), channel_id=1, source_target_pairs={{0,16},{4,20},{8,24},{12,28},{16,0},{20,4},{24,8},{28,12},{1,17},{... | collective-permute-start | bytes 1572872 | tf_op jit(solution)/shard_map/ppermute | solution.py:53
  107.8 22.5 %collective-permute-start.26 = (bf16[128,2048]{1,0:T(8,128)(2,1)}, bf16[128,2048]{1,0:T(8,128)(2,1)S(1)}, u32[]{:S(2)}, u32[]{:S(2)}) collective-permute-start(bf16[128,2048]{1,0:T(8,128)(2,1)} %get-tuple-element.77.grad_b.refs_0_), channel_id=1, source_target_pairs={{0,8},{4,12},{8,0},{12,4},{16,24},{20,28},{24,16},{28,20},{1,9},{5... | collective-permute-start | bytes 1572872 | tf_op jit(solution)/shard_map/ppermute | solution.py:53
  130.1 9.1 %collective-permute-start.22 = (bf16[32,3200]{1,0:T(8,128)(2,1)}, bf16[32,3200]{1,0:T(8,128)(2,1)S(1)}, u32[]{:S(2)}, u32[]{:S(2)}) collective-permute-start(bf16[32,3200]{1,0:T(8,128)(2,1)} %get-tuple-element.86), channel_id=1, source_target_pairs={{0,2},{1,3},{2,0},{3,1},{4,6},{5,7},{6,4},{7,5},{8,10},{9,11},{10,... | collective-permute-start | bytes 614408 | tf_op jit(solution)/shard_map/ppermute | solution.py:48
  130.1 17.1 %collective-permute-start.28 = (bf16[128,2048]{1,0:T(8,128)(2,1)S(1)}, bf16[128,2048]{1,0:T(8,128)(2,1)S(1)}, u32[]{:S(2)}, u32[]{:S(2)}) collective-permute-start(bf16[128,2048]{1,0:T(8,128)(2,1)S(1)} %collective-permute-done.27.refs_2_), channel_id=1, source_target_pairs={{0,8},{4,12},{8,0},{12,4},{16,24},{20,28},{24,16},{28,20},{1,9},{5... | collective-permute-start | bytes 1572872 | tf_op jit(solution)/shard_map/ppermute | solution.py:53
  130.4 17.4 %collective-permute-start.37 = (bf16[128,2048]{1,0:T(8,128)(2,1)S(1)}, bf16[128,2048]{1,0:T(8,128)(2,1)S(1)}, u32[]{:S(2)}, u32[]{:S(2)}) collective-permute-start(bf16[128,2048]{1,0:T(8,128)(2,1)S(1)} %collective-permute-done.30.refs_1_), channel_id=1, source_target_pairs={{0,4},{4,0},{8,12},{12,8},{16,20},{20,16},{24,28},{28,24},{1,5},{5... | collective-permute-start | bytes 1572872 | tf_op jit(solution)/shard_map/ppermute | solution.py:53
  137.6 10.2 %collective-permute-start.38 = (bf16[128,2048]{1,0:T(8,128)(2,1)S(1)}, bf16[128,2048]{1,0:T(8,128)(2,1)S(1)}, u32[]{:S(2)}, u32[]{:S(2)}) collective-permute-start(bf16[128,2048]{1,0:T(8,128)(2,1)S(1)} %collective-permute-done.35.refs_2_), channel_id=1, source_target_pairs={{0,4},{4,0},{8,12},{12,8},{16,20},{20,16},{24,28},{28,24},{1,5},{5... | collective-permute-start | bytes 1572872 | tf_op jit(solution)/shard_map/ppermute | solution.py:53
  147.2 11.4 %collective-permute-start.29 = (bf16[128,2048]{1,0:T(8,128)(2,1)}, bf16[128,2048]{1,0:T(8,128)(2,1)S(1)}, u32[]{:S(2)}, u32[]{:S(2)}) collective-permute-start(bf16[128,2048]{1,0:T(8,128)(2,1)} %get-tuple-element.77.grad_b.refs_0_), channel_id=1, source_target_pairs={{0,4},{4,0},{8,12},{12,8},{16,20},{20,16},{24,28},{28,24},{1,5},{5... | collective-permute-start | bytes 1572872 | tf_op jit(solution)/shard_map/ppermute | solution.py:53
  147.7 10.9 %collective-permute-start.32 = (bf16[128,2048]{1,0:T(8,128)(2,1)S(1)}, bf16[128,2048]{1,0:T(8,128)(2,1)S(1)}, u32[]{:S(2)}, u32[]{:S(2)}) collective-permute-start(bf16[128,2048]{1,0:T(8,128)(2,1)S(1)} %collective-permute-done.26.refs_1_), channel_id=1, source_target_pairs={{0,4},{4,0},{8,12},{12,8},{16,20},{20,16},{24,28},{28,24},{1,5},{5... | collective-permute-start | bytes 1572872 | tf_op jit(solution)/shard_map/ppermute | solution.py:53
  147.8 10.8 %collective-permute-start.33 = (bf16[128,2048]{1,0:T(8,128)(2,1)S(1)}, bf16[128,2048]{1,0:T(8,128)(2,1)S(1)}, u32[]{:S(2)}, u32[]{:S(2)}) collective-permute-start(bf16[128,2048]{1,0:T(8,128)(2,1)S(1)} %collective-permute-done.27.refs_2_), channel_id=1, source_target_pairs={{0,4},{4,0},{8,12},{12,8},{16,20},{20,16},{24,28},{28,24},{1,5},{5... | collective-permute-start | bytes 1572872 | tf_op jit(solution)/shard_map/ppermute | solution.py:53
  148.2 10.4 %collective-permute-start.34 = (bf16[128,2048]{1,0:T(8,128)(2,1)S(1)}, bf16[128,2048]{1,0:T(8,128)(2,1)S(1)}, u32[]{:S(2)}, u32[]{:S(2)}) collective-permute-start(bf16[128,2048]{1,0:T(8,128)(2,1)S(1)} %collective-permute-done.28.refs_3_), channel_id=1, source_target_pairs={{0,4},{4,0},{8,12},{12,8},{16,20},{20,16},{24,28},{28,24},{1,5},{5... | collective-permute-start | bytes 1572872 | tf_op jit(solution)/shard_map/ppermute | solution.py:53
  (45 other events, 190.8 us)

commit v4 on v3

--- a/solution.py
+++ b/solution.py
@@ -204,23 +204,22 @@
 
 def backward_body(half, count, *refs):
     blocks = refs[:count]
-    down_hbm, hidden_ref, silu_ref, slope_ref, grad_ref, prob_ref, down_ref, sems = refs[count:]
-    rows, part = hidden_ref.shape
-    block = min(BLOCK, part)
-    groups = [
-        [(down_hbm.at[pl.ds(half * part + at, block)], down_ref.at[pl.ds(at, block)])]
-        for at in range(0, part, block)
-    ]
-    dy = jnp.concatenate([ref[...] for ref in blocks], axis=0)
-    prob = jnp.zeros((rows, 1), F32)
+    down_hbm, hidden_ref, silu_ref, slope_ref, grad_ref, prob_ref = refs[count : count + 6]
+    down_ref, raw_ref, sems = refs[count + 6 :]
+    part = hidden_ref.shape[1]
+    rows, width = pl.ds(half * part, part), down_hbm.shape[1]
+    block = 2 * BLOCK
+    spans = [pl.ds(at, block) for at in range(0, width, block)]
+    groups = [[(down_hbm.at[rows, span], down_ref.at[:, span])] for span in spans]
     for step in windowed(groups, sems, 4):
-        at = step * block
-        cols = slice(at, at + block)
-        raw = nt_dot(dy, down_ref[cols, :])
-        grad_ref[:, cols] = (raw * slope_ref[:, cols]).astype(BF16)
-        grad_ref[:, part + at : part + at + block] = (raw * silu_ref[:, cols]).astype(BF16)
-        prob = prob + jnp.sum(hidden_ref[:, cols].astype(F32) * raw, axis=1, keepdims=True)
-    prob_ref[...] = prob
+        cols = slice(step * block, (step + 1) * block)
+        dy = jnp.concatenate([ref[:, cols] for ref in blocks], axis=0)
+        raw = nt_dot(dy, down_ref[:, cols])
+        raw_ref[...] = raw if step == 0 else raw_ref[...] + raw
+    raw = raw_ref[...]
+    grad_ref[:, :part] = (raw * slope_ref[...]).astype(BF16)
+    grad_ref[:, part:] = (raw * silu_ref[...]).astype(BF16)
+    prob_ref[...] = jnp.sum(hidden_ref[...].astype(F32) * raw, axis=1, keepdims=True)
 
 
 def backward(dy_blocks, w_down, hidden, silu, slope, half):
@@ -234,19 +233,37 @@
         [IN_VMEM] * count + [IN_HBM] + [IN_VMEM] * 3,
         2 * rows * width * part,
         2 * width * part + 12 * rows * part,
-        [pltpu.VMEM((part, width), BF16), pltpu.SemaphoreType.DMA((part // min(BLOCK, part),))],
+        [
+            pltpu.VMEM((part, width), BF16),
+            pltpu.VMEM((rows, part), F32),
+            pltpu.SemaphoreType.DMA((width // (2 * BLOCK),)),
+        ],
         limit=50,
     )(*dy_blocks, w_down, hidden, silu, slope)
 
 
-def token_body(count, gate_hbm, up_hbm, grad_a, grad_b, prob_a, prob_b, *refs):
-    outs = refs[:count]
-    gate_w, up_w, sems = refs[count:]
+def token_body(half, count, gate_hbm, up_hbm, grad_ref, *refs):
+    gate_w, up_w, sems = refs[-3:]
     width, units = gate_hbm.shape
-    spans = [pl.ds(at, BLOCK) for at in range(0, width, BLOCK)]
-    groups = [
-        [(gate_hbm.at[span], gate_w.at[span]), (up_hbm.at[span], up_w.at[span])] for span in spans
-    ]
+    part = units // 2
+    block = min(BLOCK, part)
+    groups = []
+    for at in range(0, part, block):
+        src, dst = pl.ds(half * part + at, block), pl.ds(at, block)
+        groups.append(
+            [(gate_hbm.at[:, src], gate_w.at[:, dst]), (up_hbm.at[:, src], up_w.at[:, dst])]
+        )
+    total_ref = refs[0] if half == 0 else refs[-4]
+    for step in windowed(groups, sems, 4):
+        at = step * block
+        cols = slice(at, at + block)
+        share = nt_dot(grad_ref[:, cols], gate_w[:, cols])
+        share = share + nt_dot(grad_ref[:, part + at : part + at + block], up_w[:, cols])
+        total_ref[...] = share if step == 0 else total_ref[...] + share
+    if half == 0:
+        return
+    earlier_ref, prob_a, prob_b = refs[:3]
+    outs = refs[3 : 3 + count]
     prob = prob_a[...] + prob_b[...]
     high = prob.astype(BF16).astype(F32)
     mid = (prob - high).astype(BF16).astype(F32)
@@ -256,30 +273,27 @@
         lane == 0, high, jnp.where(lane == 1, mid, jnp.where(lane == 2, low, 0.0))
     ).astype(BF16)
     for z in range(count):
-        outs[z][:, width:] = terms[z * LOC_CAP : (z + 1) * LOC_CAP]
+        rows = slice(z * LOC_CAP, (z + 1) * LOC_CAP)
+        outs[z][:, :width] = (total_ref[rows, :] + earlier_ref[rows, :]).astype(BF16)
+        outs[z][:, width:] = terms[rows]
+
+
+def token_sums(w_gate, w_up, grad, half, earlier, count):
+    width, units = w_gate.shape
     part = units // 2
-    gate = jnp.concatenate([grad_a[:, :part], grad_b[:, :part]], axis=1)
-    up = jnp.concatenate([grad_a[:, part:], grad_b[:, part:]], axis=1)
-    for step in windowed(groups, sems, 4):
-        cols = slice(step * BLOCK, (step + 1) * BLOCK)
-        share = (nt_dot(gate, gate_w[cols, :]) + nt_dot(up, up_w[cols, :])).astype(BF16)
-        for z in range(count):
-            outs[z][:, cols] = share[z * LOC_CAP : (z + 1) * LOC_CAP]
-
-
-def token_shares(w_gate, w_up, grads, probs, count):
-    width, units = w_gate.shape
     rows = count * LOC_CAP
-    return call(
-        functools.partial(token_body, count),
-        "token_shares",
-        [struct((LOC_CAP, width + LANES))] * count,
-        [IN_HBM] * 2 + [IN_VMEM] * 4,
-        4 * rows * width * units,
-        4 * width * units,
-        [pltpu.VMEM(w_gate.shape, BF16)] * 2 + [pltpu.SemaphoreType.DMA((2 * (width // BLOCK),))],
-        limit=54,
-    )(w_gate, w_up, *grads, *probs)
+    weights = [pltpu.VMEM((width, part), BF16)] * 2
+    total = [] if half == 0 else [pltpu.VMEM((rows, width), F32)]
+    return call(
+        functools.partial(token_body, half, count),
+        "token_sums",
+        struct((rows, width), F32) if half == 0 else [struct((LOC_CAP, width + LANES))] * count,
+        [IN_HBM] * 2 + [IN_VMEM] * (1 + len(earlier)),
+        4 * rows * width * part,
+        4 * width * part,
+        total + weights + [pltpu.SemaphoreType.DMA((2 * (part // min(BLOCK, part)),))],
+        limit=50,
+    )(w_gate, w_up, grad, *earlier)
 
 
 def place_body(*refs):
@@ -505,10 +519,11 @@
     dy_parts = jnp.concatenate(
         [dy_parts[0]] + [exchange(dy_parts[key], 2 * key) for key in range(1, chips)], axis=0
     )
-    dy_pack = after(dy_pack, dy_parts)
-    dy_blocks = [dy_pack] + [shift(dy_pack, step) for step in range(1, etp_ways)]
+    x_blocks[0] = after(x_blocks[0], dy_parts)
     x_all, *x_parts = join_x(chip, x_blocks, chips)
     x_slices = [x_parts[0]] + [exchange(x_parts[key], 2 * key) for key in range(1, chips)]
+    dy_pack = after(dy_pack, x_all)
+    dy_blocks = [dy_pack] + [shift(dy_pack, step) for step in range(1, etp_ways)]
     near = [x_slices[1 << k] for k in range(chips.bit_length() - 1)]
     inputs = (x_all, after(x_all, *near, *dy_blocks[1:-1]))
     scaled, grads, probs, kept_halves = [], [], [], []
@@ -516,34 +531,42 @@
         piece, *rest = forward(inputs[half], w_gate, w_up, half)
         scaled.append(chip_gather(piece, chips, half == 1))
         kept_halves.append(rest)
+    earlier = list(x_slices[1:])
+    later = []
+    for key in range(1, chips):
+        (earlier if key.bit_count() == 1 else later).extend((scaled[0][key], scaled[1][key]))
     for half in range(2):
         hidden, silu, slope = kept_halves[half]
-        grad, prob = backward(dy_blocks, w_down, after(hidden, *x_slices[1:]), silu, slope, half)
+        hidden = after(hidden, *earlier)
+        grad, prob = backward(dy_blocks, w_down, hidden, silu, slope, half)
         grads.append(grad)
         probs.append(prob)
+        if half == 0:
+            first = token_sums(w_gate, w_up, grad, 0, (), etp_ways)
+            earlier = [*later, first]
     parts = [chip_gather(grads[half], chips, half == 1) for half in range(2)]
-    dy_parts = after(dy_parts, *dy_blocks[1:])
+    dy_parts = after(dy_parts, probs[1])
     dy_slices = [dy_parts] + [shift(dy_parts, step) for step in range(1, etp_ways)]
 
-    probs[0] = after(probs[0], *scaled[0][1:], *scaled[1][1:], *dy_slices[1:])
-    shares = token_shares(w_gate, w_up, grads, probs, etp_ways)
+    shares = token_sums(w_gate, w_up, grads[1], 1, (first, *probs), etp_ways)
+    shares = [after(share, *dy_slices[1:]) for share in shares]
     shares = [shares[0]] + [shift(shares[step], -step) for step in range(1, etp_ways)]
     grad_tokens, grad_prob = place(shares, sel)
 
     mine, theirs = turn_dy(core, dy_slices, chips)
-    theirs = after(theirs, probs[1])
     got = exchange(theirs_sums(theirs, *scaled), 1)
     grad_down = down_sums(mine, got, *scaled, inv)
 
     mine, theirs = turn_x(core, x_slices)
-    mine = after(mine, grad_down, grad_tokens)
     far = exchange(theirs, 1)
     held = ()
     for half in range(2):
         others = [
-            exchange(after(part, parts[0][-1]) if key.bit_count() == 1 else part, 1)
+            exchange(after(part, parts[0][-1]) if key.bit_count() < 2 else part, 1)
             for key, part in enumerate(parts[half])
         ]
+        if half == 1:
+            mine = after(mine, grad_down)
         held = pair_sums(mine, far, parts[half], others, held, half, inv)
     grad_gate, grad_up = held
     return (grad_tokens, grad_prob.reshape(-1), grad_gate, grad_up, grad_down)

time: 164 us -> 157 us (0.957)
  waiting for transfers between devices: 31 us -> 50.1 us
  starting transfers between devices: 51.5 us -> 39.7 us
  Pallas kernels: 61.3 us -> 51.6 us
  local copies, waits for them, and re-layouts: 18.6 us -> 14.6 us
    ppermute x12, waiting for transfers between devices: 20.4 us -> 36.4 us  [shift(): lax.ppermute(block, 'etp', [(i, (i + step) % ways) for i in range(ways)])]
    ppermute x12, starting transfers between devices: 27.6 us -> 15.1 us  [shift(): lax.ppermute(block, 'etp', [(i, (i + step) % ways) for i in range(ways)])]
    pallas_call x1 -> x2, Pallas kernels: 19.1 us -> 13.5 us  [token_sums(): call(functools.partial(token_body, half, count), 'token_sums', struct((ro...]
    pallas_call x2, Pallas kernels: 12.2 us -> 8.21 us  [backward(): call(functools.partial(backward_body, half, count), 'backward', [struct((...]
    unnamed x77 -> x39, local copies, waits for them, and re-layouts: 18 us -> 14 us
    ppermute x28, waiting for transfers between devices: 10.6 us -> 13.6 us  [exchange(): return lax.ppermute(block, 'dp', [(i, i ^ bits) for i in range(ways)])]
  transfers between devices with their start and end apart: 40 -> 40, of which waited for: 10 -> 13; matrix products, arithmetic and copies ran while one was open for 2% -> 2% of each run, Pallas kernels for 34% -> 30%
where the time goes in v4:
time: 157 us
  Pallas kernels  51.6 us (33%)
  waiting for transfers between devices  50.1 us (32%)
  starting transfers between devices  39.7 us (25%)
  local copies, waits for them, and re-layouts  14.6 us (9%)
    ppermute x12, waiting for transfers between devices, shift(): lax.ppermute(block, 'etp', [(i, (i + step) % ways) for i in range(ways)])  36.4 us
    ppermute x28, starting transfers between devices, exchange(): return lax.ppermute(block, 'dp', [(i, i ^ bits) for i in range(ways)])  24.6 us
    ppermute x12, starting transfers between devices, shift(): lax.ppermute(block, 'etp', [(i, (i + step) % ways) for i in range(ways)])  15.1 us
    unnamed x39, local copies, waits for them, and re-layouts  14 us
    ppermute x28, waiting for transfers between devices, exchange(): return lax.ppermute(block, 'dp', [(i, i ^ bits) for i in range(ways)])  13.6 us
    pallas_call x2, Pallas kernels, token_sums(): call(functools.partial(token_body, half, count), 'token_sums', struct((ro...  13.5 us
    pallas_call x2, Pallas kernels, forward(): call(functools.partial(forward_body, half), 'forward', [struct((rows, par...  11 us
    pallas_call x2, Pallas kernels, pair_sums(): call(functools.partial(pair_body, inv, len(parts), steps), 'pair_sums', [...  9.69 us
  transfers between devices with their start and end apart: 40, of which 13 were waited for; matrix products, arithmetic and copies ran while one was open for 2% of the time, Pallas kernels for 30%

profile of v4, /device:TPU:0, one launch (start us, length us, event | category | flops | bytes accessed | tf_op | source)
XLA Modules:
  0.0 156.8 jit_solution(6146067056288944991)
XLA Ops:
  3.5 5.1 %collective-permute-start.5 = (bf16[32,3200]{1,0:T(8,128)(2,1)S(1)}, bf16[32,3200]{1,0:T(8,128)(2,1)S(1)}, u32[]{:S(2)}, u32[]{:S(2)}) collective-permute-start(bf16[32,3200]{1,0:T(8,128)(2,1)S(1)} %get-tuple-element.67.refs_0_), channel_id=1, source_target_pairs={{0,3},{1,0},{2,1},{3,2},{4,7},{5,4},{6,5},{7,6},{8,11},{9,8},{10,9... | collective-permute-start | bytes 614408 | tf_op jit(solution)/shard_map/ppermute | solution.py:48
  11.0 1.6 collective-permute-start
  12.5 1.5 collective-permute-start.1
  15.1 2.5 %collective-permute-start.2 = (bf16[32,768]{1,0:T(8,128)(2,1)S(1)}, bf16[32,768]{1,0:T(8,128)(2,1)S(1)}, u32[]{:S(2)}, u32[]{:S(2)}) collective-permute-start(bf16[32,768]{1,0:T(8,128)(2,1)S(1)} %get-tuple-element.66), channel_id=1, source_target_pairs={{0,24},{4,28},{8,16},{12,20},{16,8},{20,12},{24,0},{28,4},{1,25},{... | collective-permute-start | bytes 147464 | tf_op jit(solution)/shard_map/ppermute | solution.py:53
  20.7 5.2 %collective-permute-done.4.refs_2_ = bf16[32,3200]{1,0:T(8,128)(2,1)S(1)} collective-permute-done((bf16[32,3200]{1,0:T(8,128)(2,1)S(1)}, bf16[32,3200]{1,0:T(8,128)(2,1)S(1)}, u32[]{:S(2)}, u32[]{:S(2)}) %collective-permute-start.4) | collective-permute-done | bytes 204832 | tf_op jit(solution)/shard_map/ppermute | solution.py:48
  26.7 2.8 %collective-permute-start.7 = (bf16[32,3072]{1,0:T(8,128)(2,1)S(1)}, bf16[32,3072]{1,0:T(8,128)(2,1)S(1)}, u32[]{:S(2)}, u32[]{:S(2)}) collective-permute-start(bf16[32,3072]{1,0:T(8,128)(2,1)S(1)} %get-tuple-element.69.refs_0_), channel_id=1, source_target_pairs={{0,2},{1,3},{2,0},{3,1},{4,6},{5,7},{6,4},{7,5},{8,10},{9,11},{10,... | collective-permute-start | bytes 589832 | tf_op jit(solution)/shard_map/ppermute | solution.py:48
  31.0 1.5 collective-permute-start.10
  33.0 5.5 %forward.3 = (bf16[128,1024]{1,0:T(8,128)(2,1)S(1)}, bf16[128,1024]{1,0:T(8,128)(2,1)S(1)}, f32[128,1024]{1,0:T(8,128)S(1)}, f32[128,1024]{1,0:T(8,128)S(1)}) custom-call(bf16[128,3200]{1,0:T(8,128)(2,1)S(1)} %get-tuple-element.72.x_ref, bf16[3072,2048]{1,0:T(8,128)(2,1)} %gate_hbm.7, bf16[3072,2048]{1,0:T(8,128)(2,1)} %up_hbm.7), custom_call_target="tpu_custom_call" | custom-call | flops 1610612736 | bytes 12582912 | tf_op jit(solution)/shard_map/forward/pallas_call | solution.py:192
  38.6 3.7 %collective-permute-done.7.refs_2_ = bf16[32,3072]{1,0:T(8,128)(2,1)S(1)} collective-permute-done((bf16[32,3072]{1,0:T(8,128)(2,1)S(1)}, bf16[32,3072]{1,0:T(8,128)(2,1)S(1)}, u32[]{:S(2)}, u32[]{:S(2)}) %collective-permute-start.7) | collective-permute-done | bytes 196640 | tf_op jit(solution)/shard_map/ppermute | solution.py:48
  45.1 5.5 %forward.2 = (bf16[128,1024]{1,0:T(8,128)(2,1)S(1)}, bf16[128,1024]{1,0:T(8,128)(2,1)S(1)}, f32[128,1024]{1,0:T(8,128)S(1)}, f32[128,1024]{1,0:T(8,128)S(1)}) custom-call(bf16[128,3200]{1,0:T(8,128)(2,1)S(1)} %get-tuple-element.72.x_ref, bf16[3072,2048]{1,0:T(8,128)(2,1)} %gate_hbm.7, bf16[3072,2048]{1,0:T(8,128)(2,1)} %up_hbm.7), custom_call_target="tpu_custom_call" | custom-call | flops 1610612736 | bytes 12582912 | tf_op jit(solution)/shard_map/forward/pallas_call | solution.py:192
  50.6 1.6 %collective-permute-start.13 = (bf16[128,1024]{1,0:T(8,128)(2,1)S(1)}, bf16[128,1024]{1,0:T(8,128)(2,1)S(1)}, u32[]{:S(2)}, u32[]{:S(2)}) collective-permute-start(bf16[128,1024]{1,0:T(8,128)(2,1)S(1)} %get-tuple-element.75.refs_4_), channel_id=1, source_target_pairs={{0,16},{4,20},{8,24},{12,28},{16,0},{20,4},{24,8},{28,12},{1,17},{... | collective-permute-start | bytes 786440 | tf_op jit(solution)/shard_map/ppermute | solution.py:53
  54.2 1.5 collective-permute-start.12
  55.7 4.3 %collective-permute-done.13.refs_6_ = bf16[128,1024]{1,0:T(8,128)(2,1)S(1)} collective-permute-done((bf16[128,1024]{1,0:T(8,128)(2,1)S(1)}, bf16[128,1024]{1,0:T(8,128)(2,1)S(1)}, u32[]{:S(2)}, u32[]{:S(2)}) %collective-permute-start.13) | collective-permute-done | bytes 262176 | tf_op jit(solution)/shard_map/ppermute | solution.py:53
  60.5 5.1 %collective-permute-done.17.refs_2_ = bf16[128,1024]{1,0:T(8,128)(2,1)S(1)} collective-permute-done((bf16[128,1024]{1,0:T(8,128)(2,1)S(1)}, bf16[128,1024]{1,0:T(8,128)(2,1)S(1)}, u32[]{:S(2)}, u32[]{:S(2)}) %collective-permute-start.17) | collective-permute-done | bytes 262176 | tf_op jit(solution)/shard_map/ppermute | solution.py:53
  66.3 4.5 %backward.2 = (bf16[128,2048]{1,0:T(8,128)(2,1)}, f32[128,1]{1,0:T(8,128)S(1)}) custom-call(bf16[32,3072]{1,0:T(8,128)(2,1)S(1)} %get-tuple-element.69.refs_0_, bf16[32,3072]{1,0:T(8,128)(2,1)S(1)} %collective-permute-done.6.refs_1_, bf16[32,3072]{1,0:T(8,128)(2,1)S(1)} %collective-permute-done.7.refs_2_, ...), custom_call_target="tpu_custom_call" | custom-call | flops 805306368 | bytes 7864320 | tf_op jit(solution)/shard_map/backward/pallas_call | solution.py:229
  71.3 7.3 %token_sums.2.refs_0_ = f32[128,3072]{1,0:T(8,128)S(1)} custom-call(bf16[3072,2048]{1,0:T(8,128)(2,1)} %gate_hbm.7, bf16[3072,2048]{1,0:T(8,128)(2,1)} %up_hbm.7, bf16[128,2048]{1,0:T(8,128)(2,1)} %get-tuple-element.108.grad_ref.refs_0_), custom_call_target="tpu_custom_call" | custom-call | flops 1610612736 | bytes 12582912 | tf_op jit(solution)/shard_map/token_sums/pallas_call | solution.py:287
  80.0 3.7 %backward.3 = (bf16[128,2048]{1,0:T(8,128)(2,1)S(1)}, f32[128,1]{1,0:T(8,128)S(1)}) custom-call(bf16[32,3072]{1,0:T(8,128)(2,1)S(1)} %get-tuple-element.69.refs_0_, bf16[32,3072]{1,0:T(8,128)(2,1)S(1)} %collective-permute-done.6.refs_1_, bf16[32,3072]{1,0:T(8,128)(2,1)S(1)} %collective-permute-done.7.refs_2_, ...), custom_call_target="tpu_custom_call" | custom-call | flops 805306368 | bytes 7864320 | tf_op jit(solution)/shard_map/backward/pallas_call | solution.py:229
  83.8 1.6 %collective-permute-start.27 = (bf16[128,2048]{1,0:T(8,128)(2,1)S(1)}, bf16[128,2048]{1,0:T(8,128)(2,1)}, u32[]{:S(2)}, u32[]{:S(2)}) collective-permute-start(bf16[128,2048]{1,0:T(8,128)(2,1)S(1)} %get-tuple-element.105.grad_ref.refs_0_), channel_id=1, source_target_pairs={{0,16},{4,20},{8,24},{12,28},{16,0},{20,4},{24,8},{28,12},{1,17},{... | collective-permute-start | bytes 1572872 | tf_op jit(solution)/shard_map/ppermute | solution.py:53
  90.5 1.8 %collective-permute-start.35 = (bf16[128,2048]{1,0:T(8,128)(2,1)}, bf16[128,2048]{1,0:T(8,128)(2,1)S(1)}, u32[]{:S(2)}, u32[]{:S(2)}) collective-permute-start(bf16[128,2048]{1,0:T(8,128)(2,1)} %get-tuple-element.108.grad_ref.refs_0_), channel_id=1, source_target_pairs={{0,16},{4,20},{8,24},{12,28},{16,0},{20,4},{24,8},{28,12},{1,17},{... | collective-permute-start | bytes 1572872 | tf_op jit(solution)/shard_map/ppermute | solution.py:53
  92.4 3.4 %collective-permute-done.19.refs_2_ = bf16[128,768]{1,0:T(8,128)(2,1)} collective-permute-done((bf16[128,768]{1,0:T(8,128)(2,1)}, bf16[128,768]{1,0:T(8,128)(2,1)}, u32[]{:S(2)}, u32[]{:S(2)}) %collective-permute-start.19) | collective-permute-done | bytes 196640 | tf_op jit(solution)/shard_map/ppermute | solution.py:48
  97.1 6.6 %collective-permute-done.18.refs_1_ = bf16[128,768]{1,0:T(8,128)(2,1)S(1)} collective-permute-done((bf16[128,768]{1,0:T(8,128)(2,1)}, bf16[128,768]{1,0:T(8,128)(2,1)S(1)}, u32[]{:S(2)}, u32[]{:S(2)}) %collective-permute-start.18) | collective-permute-done | bytes 196640 | tf_op jit(solution)/shard_map/ppermute | solution.py:48
  103.8 1.5 turn_dy.1
  105.3 2.0 %theirs_sums.1 = bf16[384,2048]{1,0:T(8,128)(2,1)S(1)} custom-call(bf16[384,512]{1,0:T(8,128)(2,1)S(1)} %get-tuple-element.102.left_ref, bf16[128,1024]{1,0:T(8,128)(2,1)S(1)} %get-tuple-element.74.refs_0_, bf16[128,1024]{1,0:T(8,128)(2,1)S(1)} %collective-permute-done.11.refs_1_, bf16[128,1024]{1,0:T(8,128)(2,1)S(1)} %collective-permute-done.17.refs_2_, ...), custom_call_target="tpu_custom_call" | custom-call | flops 805306368 | bytes 3670016 | tf_op jit(solution)/shard_map/theirs_sums/pallas_call | solution.py:418
  107.4 1.6 %collective-permute-start.26 = (bf16[128,2048]{1,0:T(8,128)(2,1)S(1)}, bf16[128,2048]{1,0:T(8,128)(2,1)S(1)}, u32[]{:S(2)}, u32[]{:S(2)}) collective-permute-start(bf16[128,2048]{1,0:T(8,128)(2,1)S(1)} %get-tuple-element.105.grad_ref.refs_0_), channel_id=1, source_target_pairs={{0,8},{4,12},{8,0},{12,4},{16,24},{20,28},{24,16},{28,20},{1,9},{5... | collective-permute-start | bytes 1572872 | tf_op jit(solution)/shard_map/ppermute | solution.py:53
  109.5 6.2 %token_sums.3 = (bf16[32,3200]{1,0:T(8,128)(2,1)S(1)}, bf16[32,3200]{1,0:T(8,128)(2,1)S(1)}, bf16[32,3200]{1,0:T(8,128)(2,1)S(1)}, bf16[32,3200]{1,0:T(8,128)(2,1)S(1)}) custom-call(bf16[3072,2048]{1,0:T(8,128)(2,1)} %gate_hbm.7, bf16[3072,2048]{1,0:T(8,128)(2,1)} %up_hbm.7, bf16[128,2048]{1,0:T(8,128)(2,1)S(1)} %get-tuple-element.105.grad_ref.refs_0_, ...), custom_call_target="tpu_custom_call" | custom-call | flops 1610612736 | bytes 12582912 | tf_op jit(solution)/shard_map/token_sums/pallas_call | solution.py:287
  115.7 1.8 %collective-permute-start.21 = (bf16[32,3200]{1,0:T(8,128)(2,1)S(1)}, bf16[32,3200]{1,0:T(8,128)(2,1)S(1)}, u32[]{:S(2)}, u32[]{:S(2)}) collective-permute-start(bf16[32,3200]{1,0:T(8,128)(2,1)S(1)} %get-tuple-element.92), channel_id=1, source_target_pairs={{0,3},{1,0},{2,1},{3,2},{4,7},{5,4},{6,5},{7,6},{8,11},{9,8},{10,9... | collective-permute-start | bytes 614408 | tf_op jit(solution)/shard_map/ppermute | solution.py:48
  117.5 5.1 %collective-permute-done.21.refs_1_ = bf16[32,3200]{1,0:T(8,128)(2,1)S(1)} collective-permute-done((bf16[32,3200]{1,0:T(8,128)(2,1)S(1)}, bf16[32,3200]{1,0:T(8,128)(2,1)S(1)}, u32[]{:S(2)}, u32[]{:S(2)}) %collective-permute-start.21) | collective-permute-done | bytes 204832 | tf_op jit(solution)/shard_map/ppermute | solution.py:48
  123.2 3.5 %collective-permute-start.23 = (bf16[32,3200]{1,0:T(8,128)(2,1)S(1)}, bf16[32,3200]{1,0:T(8,128)(2,1)S(1)}, u32[]{:S(2)}, u32[]{:S(2)}) collective-permute-start(bf16[32,3200]{1,0:T(8,128)(2,1)S(1)} %get-tuple-element.96), channel_id=1, source_target_pairs={{0,1},{1,2},{2,3},{3,0},{4,5},{5,6},{6,7},{7,4},{8,9},{9,10},{10,1... | collective-permute-start | bytes 614408 | tf_op jit(solution)/shard_map/ppermute | solution.py:48
  126.8 11.6 %collective-permute-done.22.refs_2_ = bf16[32,3200]{1,0:T(8,128)(2,1)S(1)} collective-permute-done((bf16[32,3200]{1,0:T(8,128)(2,1)S(1)}, bf16[32,3200]{1,0:T(8,128)(2,1)S(1)}, u32[]{:S(2)}, u32[]{:S(2)}) %collective-permute-start.22) | collective-permute-done | bytes 204832 | tf_op jit(solution)/shard_map/ppermute | solution.py:48
  143.9 4.9 %pair_sums.2 = (bf16[384,2048]{1,0:T(8,128)(2,1)}, bf16[384,2048]{1,0:T(8,128)(2,1)}) custom-call(bf16[384,512]{1,0:T(8,128)(2,1)S(1)} %get-tuple-element.103.left_ref, bf16[384,512]{1,0:T(8,128)(2,1)S(1)} %collective-permute-done.25.other_ref, bf16[128,2048]{1,0:T(8,128)(2,1)} %get-tuple-element.108.grad_ref.refs_0_, ...), custom_call_target="tpu_custom_call" | custom-call | flops 1610612736 | bytes 7340032 | tf_op jit(solution)/shard_map/pair_sums/pallas_call | solution.py:484
  148.8 3.2 %down_sums.1 = bf16[2048,384]{1,0:T(8,128)(2,1)} custom-call(bf16[384,512]{1,0:T(8,128)(2,1)S(1)} %get-tuple-element.101.left_ref, bf16[384,2048]{1,0:T(8,128)(2,1)S(1)} %collective-permute-done.24.got_ref, bf16[128,1024]{1,0:T(8,128)(2,1)S(1)} %get-tuple-element.74.refs_0_, bf16[128,1024]{1,0:T(8,128)(2,1)S(1)} %collective-permute-done.11.refs_1_, ...), custom_call_target="tpu_custom_call" | custom-call | flops 805306368 | bytes 5242880 | tf_op jit(solution)/shard_map/down_sums/pallas_call | solution.py:447
  152.0 4.8 %pair_sums.3 = (bf16[384,2048]{1,0:T(8,128)(2,1)}, bf16[384,2048]{1,0:T(8,128)(2,1)}) custom-call(bf16[384,512]{1,0:T(8,128)(2,1)S(1)} %get-tuple-element.103.left_ref, bf16[384,512]{1,0:T(8,128)(2,1)S(1)} %collective-permute-done.25.other_ref, ...), custom_call_target="tpu_custom_call", output_to_operand_aliasing={{0}: (10, {}), {1}: (11, {})} | custom-call | flops 1610612736 | bytes 7340032 | tf_op jit(solution)/shard_map/pair_sums/pallas_call | solution.py:484
  (104 shorter events, 33.4 us)
Async XLA Ops:
  3.5 17.3 %collective-permute-start.5 = (bf16[32,3200]{1,0:T(8,128)(2,1)S(1)}, bf16[32,3200]{1,0:T(8,128)(2,1)S(1)}, u32[]{:S(2)}, u32[]{:S(2)}) collective-permute-start(bf16[32,3200]{1,0:T(8,128)(2,1)S(1)} %get-tuple-element.67.refs_0_), channel_id=1, source_target_pairs={{0,3},{1,0},{2,1},{3,2},{4,7},{5,4},{6,5},{7,6},{8,11},{9,8},{10,9... | collective-permute-start | bytes 614408 | tf_op jit(solution)/shard_map/ppermute | solution.py:48
  8.6 17.4 %collective-permute-start.4 = (bf16[32,3200]{1,0:T(8,128)(2,1)S(1)}, bf16[32,3200]{1,0:T(8,128)(2,1)S(1)}, u32[]{:S(2)}, u32[]{:S(2)}) collective-permute-start(bf16[32,3200]{1,0:T(8,128)(2,1)S(1)} %get-tuple-element.67.refs_0_), channel_id=1, source_target_pairs={{0,2},{1,3},{2,0},{3,1},{4,6},{5,7},{6,4},{7,5},{8,10},{9,11},{10,... | collective-permute-start | bytes 614408 | tf_op jit(solution)/shard_map/ppermute | solution.py:48
  8.6 17.4 %collective-permute-start.3 = (bf16[32,3200]{1,0:T(8,128)(2,1)S(1)}, bf16[32,3200]{1,0:T(8,128)(2,1)S(1)}, u32[]{:S(2)}, u32[]{:S(2)}) collective-permute-start(bf16[32,3200]{1,0:T(8,128)(2,1)S(1)} %get-tuple-element.67.refs_0_), channel_id=1, source_target_pairs={{0,1},{1,2},{2,3},{3,0},{4,5},{5,6},{6,7},{7,4},{8,9},{9,10},{10,1... | collective-permute-start | bytes 614408 | tf_op jit(solution)/shard_map/ppermute | solution.py:48
  26.7 15.5 %collective-permute-start.7 = (bf16[32,3072]{1,0:T(8,128)(2,1)S(1)}, bf16[32,3072]{1,0:T(8,128)(2,1)S(1)}, u32[]{:S(2)}, u32[]{:S(2)}) collective-permute-start(bf16[32,3072]{1,0:T(8,128)(2,1)S(1)} %get-tuple-element.69.refs_0_), channel_id=1, source_target_pairs={{0,2},{1,3},{2,0},{3,1},{4,6},{5,7},{6,4},{7,5},{8,10},{9,11},{10,... | collective-permute-start | bytes 589832 | tf_op jit(solution)/shard_map/ppermute | solution.py:48
  29.5 14.2 %collective-permute-start.6 = (bf16[32,3072]{1,0:T(8,128)(2,1)S(1)}, bf16[32,3072]{1,0:T(8,128)(2,1)S(1)}, u32[]{:S(2)}, u32[]{:S(2)}) collective-permute-start(bf16[32,3072]{1,0:T(8,128)(2,1)S(1)} %get-tuple-element.69.refs_0_), channel_id=1, source_target_pairs={{0,1},{1,2},{2,3},{3,0},{4,5},{5,6},{6,7},{7,4},{8,9},{9,10},{10,1... | collective-permute-start | bytes 589832 | tf_op jit(solution)/shard_map/ppermute | solution.py:48
  29.5 14.2 %collective-permute-start.9 = (bf16[128,768]{1,0:T(8,128)(2,1)S(1)}, bf16[128,768]{1,0:T(8,128)(2,1)S(1)}, u32[]{:S(2)}, u32[]{:S(2)}) collective-permute-start(bf16[128,768]{1,0:T(8,128)(2,1)S(1)} %get-tuple-element.70), channel_id=1, source_target_pairs={{0,8},{4,12},{8,0},{12,4},{16,24},{20,28},{24,16},{28,20},{1,9},{5... | collective-permute-start | bytes 589832 | tf_op jit(solution)/shard_map/ppermute | solution.py:53
  31.0 13.4 %collective-permute-start.10 = (bf16[128,768]{1,0:T(8,128)(2,1)S(1)}, bf16[128,768]{1,0:T(8,128)(2,1)S(1)}, u32[]{:S(2)}, u32[]{:S(2)}) collective-permute-start(bf16[128,768]{1,0:T(8,128)(2,1)S(1)} %get-tuple-element.71), channel_id=1, source_target_pairs={{0,16},{4,20},{8,24},{12,28},{16,0},{20,4},{24,8},{28,12},{1,17},{... | collective-permute-start | bytes 589832 | tf_op jit(solution)/shard_map/ppermute | solution.py:53
  32.6 20.7 %collective-permute-start.15 = (bf16[128,768]{1,0:T(8,128)(2,1)S(1)}, bf16[128,768]{1,0:T(8,128)(2,1)S(1)}, u32[]{:S(2)}, u32[]{:S(2)}) collective-permute-start(bf16[128,768]{1,0:T(8,128)(2,1)S(1)} %get-tuple-element.77), channel_id=1, source_target_pairs={{0,24},{4,28},{8,16},{12,20},{16,8},{20,12},{24,0},{28,4},{1,25},{... | collective-permute-start | bytes 589832 | tf_op jit(solution)/shard_map/ppermute | solution.py:53
  42.3 11.9 %collective-permute-start.11 = (bf16[128,1024]{1,0:T(8,128)(2,1)S(1)}, bf16[128,1024]{1,0:T(8,128)(2,1)S(1)}, u32[]{:S(2)}, u32[]{:S(2)}) collective-permute-start(bf16[128,1024]{1,0:T(8,128)(2,1)S(1)} %get-tuple-element.74.refs_0_), channel_id=1, source_target_pairs={{0,8},{4,12},{8,0},{12,4},{16,24},{20,28},{24,16},{28,20},{1,9},{5... | collective-permute-start | bytes 786440 | tf_op jit(solution)/shard_map/ppermute | solution.py:53
  50.6 9.3 %collective-permute-start.13 = (bf16[128,1024]{1,0:T(8,128)(2,1)S(1)}, bf16[128,1024]{1,0:T(8,128)(2,1)S(1)}, u32[]{:S(2)}, u32[]{:S(2)}) collective-permute-start(bf16[128,1024]{1,0:T(8,128)(2,1)S(1)} %get-tuple-element.75.refs_4_), channel_id=1, source_target_pairs={{0,16},{4,20},{8,24},{12,28},{16,0},{20,4},{24,8},{28,12},{1,17},{... | collective-permute-start | bytes 786440 | tf_op jit(solution)/shard_map/ppermute | solution.py:53
  52.2 13.3 %collective-permute-start.17 = (bf16[128,1024]{1,0:T(8,128)(2,1)S(1)}, bf16[128,1024]{1,0:T(8,128)(2,1)S(1)}, u32[]{:S(2)}, u32[]{:S(2)}) collective-permute-start(bf16[128,1024]{1,0:T(8,128)(2,1)S(1)} %get-tuple-element.74.refs_0_), channel_id=1, source_target_pairs={{0,16},{4,20},{8,24},{12,28},{16,0},{20,4},{24,8},{28,12},{1,17},{... | collective-permute-start | bytes 786440 | tf_op jit(solution)/shard_map/ppermute | solution.py:53
  52.7 12.8 %collective-permute-start.16 = (bf16[128,1024]{1,0:T(8,128)(2,1)S(1)}, bf16[128,1024]{1,0:T(8,128)(2,1)S(1)}, u32[]{:S(2)}, u32[]{:S(2)}) collective-permute-start(bf16[128,1024]{1,0:T(8,128)(2,1)S(1)} %get-tuple-element.75.refs_4_), channel_id=1, source_target_pairs={{0,8},{4,12},{8,0},{12,4},{16,24},{20,28},{24,16},{28,20},{1,9},{5... | collective-permute-start | bytes 786440 | tf_op jit(solution)/shard_map/ppermute | solution.py:53
  53.9 12.3 %collective-permute-start.8 = (bf16[32,3072]{1,0:T(8,128)(2,1)S(1)}, bf16[32,3072]{1,0:T(8,128)(2,1)S(1)}, u32[]{:S(2)}, u32[]{:S(2)}) collective-permute-start(bf16[32,3072]{1,0:T(8,128)(2,1)S(1)} %get-tuple-element.69.refs_0_), channel_id=1, source_target_pairs={{0,3},{1,0},{2,1},{3,2},{4,7},{5,4},{6,5},{7,6},{8,11},{9,8},{10,9... | collective-permute-start | bytes 589832 | tf_op jit(solution)/shard_map/ppermute | solution.py:48
  54.2 24.4 %collective-permute-start.12 = (bf16[128,1024]{1,0:T(8,128)(2,1)S(1)}, bf16[128,1024]{1,0:T(8,128)(2,1)S(1)}, u32[]{:S(2)}, u32[]{:S(2)}) collective-permute-start(bf16[128,1024]{1,0:T(8,128)(2,1)S(1)} %collective-permute-done.11.refs_1_), channel_id=1, source_target_pairs={{0,16},{4,20},{8,24},{12,28},{16,0},{20,4},{24,8},{28,12},{1,17},{... | collective-permute-start | bytes 786440 | tf_op jit(solution)/shard_map/ppermute | solution.py:53
  59.9 19.4 %collective-permute-start.14 = (bf16[128,1024]{1,0:T(8,128)(2,1)S(1)}, bf16[128,1024]{1,0:T(8,128)(2,1)S(1)}, u32[]{:S(2)}, u32[]{:S(2)}) collective-permute-start(bf16[128,1024]{1,0:T(8,128)(2,1)S(1)} %collective-permute-done.13.refs_6_), channel_id=1, source_target_pairs={{0,8},{4,12},{8,0},{12,4},{16,24},{20,28},{24,16},{28,20},{1,9},{5... | collective-permute-start | bytes 786440 | tf_op jit(solution)/shard_map/ppermute | solution.py:53
  70.7 25.1 %collective-permute-start.29 = (bf16[128,2048]{1,0:T(8,128)(2,1)}, bf16[128,2048]{1,0:T(8,128)(2,1)}, u32[]{:S(2)}, u32[]{:S(2)}) collective-permute-start(bf16[128,2048]{1,0:T(8,128)(2,1)} %get-tuple-element.108.grad_ref.refs_0_), channel_id=1, source_target_pairs={{0,8},{4,12},{8,0},{12,4},{16,24},{20,28},{24,16},{28,20},{1,9},{5... | collective-permute-start | bytes 1572872 | tf_op jit(solution)/shard_map/ppermute | solution.py:53
  83.8 25.1 %collective-permute-start.27 = (bf16[128,2048]{1,0:T(8,128)(2,1)S(1)}, bf16[128,2048]{1,0:T(8,128)(2,1)}, u32[]{:S(2)}, u32[]{:S(2)}) collective-permute-start(bf16[128,2048]{1,0:T(8,128)(2,1)S(1)} %get-tuple-element.105.grad_ref.refs_0_), channel_id=1, source_target_pairs={{0,16},{4,20},{8,24},{12,28},{16,0},{20,4},{24,8},{28,12},{1,17},{... | collective-permute-start | bytes 1572872 | tf_op jit(solution)/shard_map/ppermute | solution.py:53
  85.4 10.4 %collective-permute-start.19 = (bf16[128,768]{1,0:T(8,128)(2,1)}, bf16[128,768]{1,0:T(8,128)(2,1)}, u32[]{:S(2)}, u32[]{:S(2)}) collective-permute-start(bf16[128,768]{1,0:T(8,128)(2,1)} %constant_dynamic-update-slice_fusion.refs_0_), channel_id=1, source_target_pairs={{0,2},{1,3},{2,0},{3,1},{4,6},{5,7},{6,4},{7,5},{8,10},{9,11},{10,... | collective-permute-start | bytes 589832 | tf_op jit(solution)/shard_map/ppermute | solution.py:48
  89.7 17.7 %collective-permute-start.25 = (bf16[384,512]{1,0:T(8,128)(2,1)S(1)}, bf16[384,512]{1,0:T(8,128)(2,1)S(1)}, u32[]{:S(2)}, u32[]{:S(2)}) collective-permute-start(bf16[384,512]{1,0:T(8,128)(2,1)S(1)} %get-tuple-element.104), channel_id=1, source_target_pairs={{0,4},{4,0},{8,12},{12,8},{16,20},{20,16},{24,28},{28,24},{1,5},{5... | collective-permute-start | bytes 1179656 | tf_op jit(solution)/shard_map/ppermute | solution.py:53
  90.5 25.2 %collective-permute-start.35 = (bf16[128,2048]{1,0:T(8,128)(2,1)}, bf16[128,2048]{1,0:T(8,128)(2,1)S(1)}, u32[]{:S(2)}, u32[]{:S(2)}) collective-permute-start(bf16[128,2048]{1,0:T(8,128)(2,1)} %get-tuple-element.108.grad_ref.refs_0_), channel_id=1, source_target_pairs={{0,16},{4,20},{8,24},{12,28},{16,0},{20,4},{24,8},{28,12},{1,17},{... | collective-permute-start | bytes 1572872 | tf_op jit(solution)/shard_map/ppermute | solution.py:53
  95.8 8.0 %collective-permute-start.18 = (bf16[128,768]{1,0:T(8,128)(2,1)}, bf16[128,768]{1,0:T(8,128)(2,1)S(1)}, u32[]{:S(2)}, u32[]{:S(2)}) collective-permute-start(bf16[128,768]{1,0:T(8,128)(2,1)} %constant_dynamic-update-slice_fusion.refs_0_), channel_id=1, source_target_pairs={{0,1},{1,2},{2,3},{3,0},{4,5},{5,6},{6,7},{7,4},{8,9},{9,10},{10,1... | collective-permute-start | bytes 589832 | tf_op jit(solution)/shard_map/ppermute | solution.py:48
  95.8 27.4 %collective-permute-start.30 = (bf16[128,2048]{1,0:T(8,128)(2,1)}, bf16[128,2048]{1,0:T(8,128)(2,1)S(1)}, u32[]{:S(2)}, u32[]{:S(2)}) collective-permute-start(bf16[128,2048]{1,0:T(8,128)(2,1)} %collective-permute-done.29.refs_1_), channel_id=1, source_target_pairs={{0,16},{4,20},{8,24},{12,28},{16,0},{20,4},{24,8},{28,12},{1,17},{... | collective-permute-start | bytes 1572872 | tf_op jit(solution)/shard_map/ppermute | solution.py:53
  107.3 41.5 %collective-permute-start.24 = (bf16[384,2048]{1,0:T(8,128)(2,1)S(1)}, bf16[384,2048]{1,0:T(8,128)(2,1)S(1)}, u32[]{:S(2)}, u32[]{:S(2)}) collective-permute-start(bf16[384,2048]{1,0:T(8,128)(2,1)S(1)} %theirs_sums.1), channel_id=1, source_target_pairs={{0,4},{4,0},{8,12},{12,8},{16,20},{20,16},{24,28},{28,24},{1,5},{5... | collective-permute-start | bytes 4718600 | tf_op jit(solution)/shard_map/ppermute | solution.py:53
  107.4 31.4 %collective-permute-start.26 = (bf16[128,2048]{1,0:T(8,128)(2,1)S(1)}, bf16[128,2048]{1,0:T(8,128)(2,1)S(1)}, u32[]{:S(2)}, u32[]{:S(2)}) collective-permute-start(bf16[128,2048]{1,0:T(8,128)(2,1)S(1)} %get-tuple-element.105.grad_ref.refs_0_), channel_id=1, source_target_pairs={{0,8},{4,12},{8,0},{12,4},{16,24},{20,28},{24,16},{28,20},{1,9},{5... | collective-permute-start | bytes 1572872 | tf_op jit(solution)/shard_map/ppermute | solution.py:53
  109.0 29.9 %collective-permute-start.28 = (bf16[128,2048]{1,0:T(8,128)(2,1)}, bf16[128,2048]{1,0:T(8,128)(2,1)S(1)}, u32[]{:S(2)}, u32[]{:S(2)}) collective-permute-start(bf16[128,2048]{1,0:T(8,128)(2,1)} %collective-permute-done.27.refs_2_), channel_id=1, source_target_pairs={{0,8},{4,12},{8,0},{12,4},{16,24},{20,28},{24,16},{28,20},{1,9},{5... | collective-permute-start | bytes 1572872 | tf_op jit(solution)/shard_map/ppermute | solution.py:53
  115.7 6.9 %collective-permute-start.21 = (bf16[32,3200]{1,0:T(8,128)(2,1)S(1)}, bf16[32,3200]{1,0:T(8,128)(2,1)S(1)}, u32[]{:S(2)}, u32[]{:S(2)}) collective-permute-start(bf16[32,3200]{1,0:T(8,128)(2,1)S(1)} %get-tuple-element.92), channel_id=1, source_target_pairs={{0,3},{1,0},{2,1},{3,2},{4,7},{5,4},{6,5},{7,6},{8,11},{9,8},{10,9... | collective-permute-start | bytes 614408 | tf_op jit(solution)/shard_map/ppermute | solution.py:48
  122.7 15.7 %collective-permute-start.22 = (bf16[32,3200]{1,0:T(8,128)(2,1)S(1)}, bf16[32,3200]{1,0:T(8,128)(2,1)S(1)}, u32[]{:S(2)}, u32[]{:S(2)}) collective-permute-start(bf16[32,3200]{1,0:T(8,128)(2,1)S(1)} %get-tuple-element.94), channel_id=1, source_target_pairs={{0,2},{1,3},{2,0},{3,1},{4,6},{5,7},{6,4},{7,5},{8,10},{9,11},{10,... | collective-permute-start | bytes 614408 | tf_op jit(solution)/shard_map/ppermute | solution.py:48
  123.2 15.1 %collective-permute-start.23 = (bf16[32,3200]{1,0:T(8,128)(2,1)S(1)}, bf16[32,3200]{1,0:T(8,128)(2,1)S(1)}, u32[]{:S(2)}, u32[]{:S(2)}) collective-permute-start(bf16[32,3200]{1,0:T(8,128)(2,1)S(1)} %get-tuple-element.96), channel_id=1, source_target_pairs={{0,1},{1,2},{2,3},{3,0},{4,5},{5,6},{6,7},{7,4},{8,9},{9,10},{10,1... | collective-permute-start | bytes 614408 | tf_op jit(solution)/shard_map/ppermute | solution.py:48
  140.4 11.5 %collective-permute-start.31 = (bf16[128,2048]{1,0:T(8,128)(2,1)S(1)}, bf16[128,2048]{1,0:T(8,128)(2,1)S(1)}, u32[]{:S(2)}, u32[]{:S(2)}) collective-permute-start(bf16[128,2048]{1,0:T(8,128)(2,1)S(1)} %get-tuple-element.105.grad_ref.refs_0_), channel_id=1, source_target_pairs={{0,4},{4,0},{8,12},{12,8},{16,20},{20,16},{24,28},{28,24},{1,5},{5... | collective-permute-start | bytes 1572872 | tf_op jit(solution)/shard_map/ppermute | solution.py:53
  141.9 10.1 %collective-permute-start.33 = (bf16[128,2048]{1,0:T(8,128)(2,1)}, bf16[128,2048]{1,0:T(8,128)(2,1)S(1)}, u32[]{:S(2)}, u32[]{:S(2)}) collective-permute-start(bf16[128,2048]{1,0:T(8,128)(2,1)} %collective-permute-done.27.refs_2_), channel_id=1, source_target_pairs={{0,4},{4,0},{8,12},{12,8},{16,20},{20,16},{24,28},{28,24},{1,5},{5... | collective-permute-start | bytes 1572872 | tf_op jit(solution)/shard_map/ppermute | solution.py:53
  142.1 9.9 %collective-permute-start.32 = (bf16[128,2048]{1,0:T(8,128)(2,1)S(1)}, bf16[128,2048]{1,0:T(8,128)(2,1)S(1)}, u32[]{:S(2)}, u32[]{:S(2)}) collective-permute-start(bf16[128,2048]{1,0:T(8,128)(2,1)S(1)} %collective-permute-done.26.refs_1_), channel_id=1, source_target_pairs={{0,4},{4,0},{8,12},{12,8},{16,20},{20,16},{24,28},{28,24},{1,5},{5... | collective-permute-start | bytes 1572872 | tf_op jit(solution)/shard_map/ppermute | solution.py:53
  142.5 9.5 %collective-permute-start.34 = (bf16[128,2048]{1,0:T(8,128)(2,1)S(1)}, bf16[128,2048]{1,0:T(8,128)(2,1)S(1)}, u32[]{:S(2)}, u32[]{:S(2)}) collective-permute-start(bf16[128,2048]{1,0:T(8,128)(2,1)S(1)} %collective-permute-done.28.refs_3_), channel_id=1, source_target_pairs={{0,4},{4,0},{8,12},{12,8},{16,20},{20,16},{24,28},{28,24},{1,5},{5... | collective-permute-start | bytes 1572872 | tf_op jit(solution)/shard_map/ppermute | solution.py:53
  (26 other events, 105.9 us)

commit v5 on v4

--- a/solution.py
+++ b/solution.py
@@ -33,6 +33,10 @@
         name=name,
         **kwargs,
     )
+
+
+def whole(shape):
+    return pl.BlockSpec(shape, lambda *_: (0,) * len(shape))
 
 
 def struct(shape, kind=BF16):
@@ -94,48 +98,41 @@
     )(ids, prob, tokens)
 
 
-def pack_dy_body(chips, chip_ref, sel_ref, grad_ref, dy_ref, *slice_refs):
+def pack_dy_body(sel_ref, grad_ref, dy_ref):
     dy_ref[...] = jnp.dot(sel_ref[...], grad_ref[...], preferred_element_type=F32).astype(BF16)
-    part = slice_refs[0].shape[1]
-    for key in range(chips):
-        first = pl.multiple_of((chip_ref[0] ^ key) * part, LANES)
-        slice_refs[key][...] = dy_ref[:, pl.ds(first, part)]
-
-
-def pack_dy(chip, sel, out_grad, chips):
+
+
+def pack_dy(sel, out_grad):
     rows, width = out_grad.shape
     return call(
-        functools.partial(pack_dy_body, chips),
+        pack_dy_body,
         "pack_dy",
-        [struct((LOC_CAP, width))] + [struct((LOC_CAP, width // chips))] * chips,
-        [IN_SMEM] + [IN_VMEM] * 2,
+        struct((LOC_CAP, width)),
+        [IN_VMEM] * 2,
         2 * LOC_CAP * rows * width,
         2 * rows * width,
-    )(chip, sel, out_grad)
-
-
-def join_x_body(chips, count, chip_ref, *refs):
-    blocks, x_ref, slice_refs = refs[:count], refs[count], refs[count + 1 :]
-    part = slice_refs[0].shape[1]
-    for at, block in enumerate(blocks):
-        x_ref[at * LOC_CAP : (at + 1) * LOC_CAP, :] = block[...]
+    )(sel, out_grad)
+
+
+def slice_body(chips, count, chip_ref, *refs):
+    outs = refs[count:]
+    wide = outs[0].shape[1]
     for key in range(chips):
-        first = pl.multiple_of((chip_ref[0] ^ key) * part, LANES)
-        slice_refs[key][...] = x_ref[:, pl.ds(first, part)]
-
-
-def join_x(chip, blocks, chips):
+        at = pl.multiple_of((chip_ref[0] ^ key) * wide, LANES)
+        for z in range(count):
+            outs[key][z * LOC_CAP : (z + 1) * LOC_CAP, :] = refs[z][:, pl.ds(at, wide)]
+
+
+def slices_of(chip, blocks, width, chips):
     count = len(blocks)
-    wide = blocks[0].shape[1]
     rows = count * LOC_CAP
-    part = (wide - LANES) // chips
-    return call(
-        functools.partial(join_x_body, chips, count),
-        "join_x",
-        [struct((rows, wide))] + [struct((rows, part))] * chips,
+    return call(
+        functools.partial(slice_body, chips, count),
+        "slices",
+        [struct((rows, width // chips))] * chips,
         [IN_SMEM] + [IN_VMEM] * count,
         0,
-        4 * rows * wide,
+        4 * rows * width,
     )(chip, *blocks)
 
 
@@ -158,12 +155,11 @@
         yield step
 
 
-def forward_body(
-    half, x_ref, gate_hbm, up_hbm, scaled_ref, hidden_ref, silu_ref, slope_ref, gate_ref, up_ref, sems
-):
+def forward_body(half, count, *refs):
+    blocks = refs[:count]
+    gate_hbm, up_hbm, scaled_ref, hidden_ref, silu_ref, slope_ref = refs[count : count + 6]
+    gate_ref, up_ref, sems = refs[count + 6 :]
     width, units = gate_hbm.shape
-    x = x_ref[:, :width]
-    weight = x_ref[:, width : width + 1].astype(F32)
     part = units // 2
     block = min(BLOCK, part)
     groups = []
@@ -172,6 +168,8 @@
         groups.append(
             [(gate_hbm.at[:, src], gate_ref.at[:, dst]), (up_hbm.at[:, src], up_ref.at[:, dst])]
         )
+    x = jnp.concatenate([ref[:, :width] for ref in blocks], axis=0)
+    weight = jnp.concatenate([ref[:, width : width + 1] for ref in blocks], axis=0).astype(F32)
     for step in windowed(groups, sems, 4):
         cols = slice(step * block, (step + 1) * block)
         gate = jnp.dot(x, gate_ref[:, cols], preferred_element_type=F32)
@@ -185,28 +183,37 @@
         slope_ref[:, cols] = weight * up * sig * (1.0 + gate * (1.0 - sig))
 
 
-def forward(x_all, w_gate, w_up, half):
-    rows = x_all.shape[0]
+def forward(x_blocks, w_gate, w_up, half):
+    count = len(x_blocks)
+    rows = count * LOC_CAP
     width, units = w_gate.shape
     part = units // 2
     return call(
-        functools.partial(forward_body, half),
+        functools.partial(forward_body, half, count),
         "forward",
         [struct((rows, part), kind) for kind in (BF16, BF16, F32, F32)],
-        [IN_VMEM] + [IN_HBM] * 2,
+        [IN_VMEM] * count + [IN_HBM] * 2,
         4 * rows * width * part,
         4 * width * part,
         [pltpu.VMEM((width, part), BF16)] * 2
         + [pltpu.SemaphoreType.DMA((2 * (part // min(BLOCK, part)),))],
         limit=50,
-    )(x_all, w_gate, w_up)
+    )(*x_blocks, w_gate, w_up)
 
 
 def backward_body(half, count, *refs):
     blocks = refs[:count]
-    down_hbm, hidden_ref, silu_ref, slope_ref, grad_ref, prob_ref = refs[count : count + 6]
-    down_ref, raw_ref, sems = refs[count + 6 :]
+    down_hbm, hidden_hbm, silu_hbm, slope_hbm, grad_ref, prob_ref = refs[count : count + 6]
+    down_ref, raw_ref, hidden_ref, silu_ref, slope_ref, sems, late_sems = refs[count + 6 :]
     part = hidden_ref.shape[1]
+    late = [
+        pltpu.make_async_copy(src, dst, late_sems.at[at])
+        for at, (src, dst) in enumerate(
+            ((hidden_hbm, hidden_ref), (silu_hbm, silu_ref), (slope_hbm, slope_ref))
+        )
+    ]
+    for copy in late:
+        copy.start()
     rows, width = pl.ds(half * part, part), down_hbm.shape[1]
     block = 2 * BLOCK
     spans = [pl.ds(at, block) for at in range(0, width, block)]
@@ -216,6 +223,8 @@
         dy = jnp.concatenate([ref[:, cols] for ref in blocks], axis=0)
         raw = nt_dot(dy, down_ref[:, cols])
         raw_ref[...] = raw if step == 0 else raw_ref[...] + raw
+    for copy in late:
+        copy.wait()
     raw = raw_ref[...]
     grad_ref[:, :part] = (raw * slope_ref[...]).astype(BF16)
     grad_ref[:, part:] = (raw * silu_ref[...]).astype(BF16)
@@ -230,13 +239,17 @@
         functools.partial(backward_body, half, count),
         "backward",
         [struct((rows, 2 * part)), struct((rows, 1), F32)],
-        [IN_VMEM] * count + [IN_HBM] + [IN_VMEM] * 3,
+        [IN_VMEM] * count + [IN_HBM] + [pl.BlockSpec(memory_space=pl.ANY)] * 3,
         2 * rows * width * part,
         2 * width * part + 12 * rows * part,
         [
             pltpu.VMEM((part, width), BF16),
             pltpu.VMEM((rows, part), F32),
+            pltpu.VMEM((rows, part), BF16),
+            pltpu.VMEM((rows, part), F32),
+            pltpu.VMEM((rows, part), F32),
             pltpu.SemaphoreType.DMA((width // (2 * BLOCK),)),
+            pltpu.SemaphoreType.DMA((3,)),
         ],
         limit=50,
     )(*dy_blocks, w_down, hidden, silu, slope)
@@ -339,45 +352,27 @@
         theirs_ref[:, cols] = turned[:part]
 
 
-def turn_x_body(core_ref, *refs):
+def turn_body(core_ref, *refs):
     slices, (mine_ref, theirs_ref) = refs[:-2], refs[-2:]
     rows = slices[0].shape[0]
-    for key, block in enumerate(slices):
-        split_cores(core_ref, mine_ref, theirs_ref, slice(key * rows, (key + 1) * rows), block[...])
-
-
-def turn_x(core, slices):
+    for key, ref in enumerate(slices):
+        cols = slice(key * rows, (key + 1) * rows)
+        split_cores(core_ref, mine_ref, theirs_ref, cols, ref[...])
+
+
+def turn(core, slices):
     rows, wide = slices[0].shape
     depth = rows * len(slices)
-    return call(
-        turn_x_body,
-        "turn_x",
-        [struct((wide // 2, depth))] * 2,
-        [IN_SMEM] + [IN_VMEM] * len(slices),
+    out = (wide // 2, depth)
+    return call(
+        turn_body,
+        "turn",
+        [struct(out)] * 2,
+        [IN_SMEM] + [whole(slices[0].shape)] * len(slices),
         0,
         4 * depth * wide,
-    )(core, *slices)
-
-
-def turn_dy_body(chips, core_ref, *refs):
-    slices, (mine_ref, theirs_ref) = refs[:-2], refs[-2:]
-    rows = len(slices) * LOC_CAP
-    for key in range(chips):
-        span = slice(key * LOC_CAP, (key + 1) * LOC_CAP)
-        block = jnp.concatenate([ref[span, :] for ref in slices], axis=0)
-        split_cores(core_ref, mine_ref, theirs_ref, slice(key * rows, (key + 1) * rows), block)
-
-
-def turn_dy(core, slices, chips):
-    wide = slices[0].shape[1]
-    depth = len(slices) * slices[0].shape[0]
-    return call(
-        functools.partial(turn_dy_body, chips),
-        "turn_dy",
-        [struct((wide // 2, depth))] * 2,
-        [IN_SMEM] + [IN_VMEM] * len(slices),
-        0,
-        4 * depth * wide,
+        grid=(1,),
+        out_specs=[whole(out)] * 2,
     )(core, *slices)
 
 
@@ -515,50 +510,45 @@
 
     x_pack, sel = pack_x(route_ids.T, route_prob.reshape(1, -1), tokens)
     x_blocks = [x_pack] + [shift(x_pack, step) for step in range(1, etp_ways)]
-    dy_pack, *dy_parts = pack_dy(chip, sel, out_grad, chips)
-    dy_parts = jnp.concatenate(
-        [dy_parts[0]] + [exchange(dy_parts[key], 2 * key) for key in range(1, chips)], axis=0
-    )
-    x_blocks[0] = after(x_blocks[0], dy_parts)
-    x_all, *x_parts = join_x(chip, x_blocks, chips)
-    x_slices = [x_parts[0]] + [exchange(x_parts[key], 2 * key) for key in range(1, chips)]
-    dy_pack = after(dy_pack, x_all)
+    dy_pack = after(pack_dy(sel, out_grad), *x_blocks[1:])
     dy_blocks = [dy_pack] + [shift(dy_pack, step) for step in range(1, etp_ways)]
+    width = tokens.shape[1]
+    x_slices = slices_of(chip, x_blocks, width, chips)
+    x_slices = [x_slices[0]] + [exchange(x_slices[key], 2 * key) for key in range(1, chips)]
     near = [x_slices[1 << k] for k in range(chips.bit_length() - 1)]
-    inputs = (x_all, after(x_all, *near, *dy_blocks[1:-1]))
+    inputs = (x_blocks, [after(x_pack, *near, *dy_blocks[1:]), *x_blocks[1:]])
     scaled, grads, probs, kept_halves = [], [], [], []
     for half in range(2):
         piece, *rest = forward(inputs[half], w_gate, w_up, half)
         scaled.append(chip_gather(piece, chips, half == 1))
         kept_halves.append(rest)
-    earlier = list(x_slices[1:])
-    later = []
-    for key in range(1, chips):
-        (earlier if key.bit_count() == 1 else later).extend((scaled[0][key], scaled[1][key]))
+    dy_slices = slices_of(chip, dy_blocks, width, chips)
+    dy_slices = [dy_slices[0]] + [exchange(dy_slices[key], 2 * key) for key in range(1, chips)]
+    earlier = [scaled[0][key] for key in range(chips) if key.bit_count() == 1]
+    later = [*x_slices[1:], *dy_slices[1:], *scaled[0][1:], *scaled[1][1:]]
     for half in range(2):
         hidden, silu, slope = kept_halves[half]
-        hidden = after(hidden, *earlier)
-        grad, prob = backward(dy_blocks, w_down, hidden, silu, slope, half)
+        blocks = [after(dy_blocks[0], *earlier), *dy_blocks[1:]]
+        grad, prob = backward(blocks, w_down, hidden, silu, slope, half)
         grads.append(grad)
         probs.append(prob)
         if half == 0:
             first = token_sums(w_gate, w_up, grad, 0, (), etp_ways)
             earlier = [*later, first]
     parts = [chip_gather(grads[half], chips, half == 1) for half in range(2)]
-    dy_parts = after(dy_parts, probs[1])
-    dy_slices = [dy_parts] + [shift(dy_parts, step) for step in range(1, etp_ways)]
 
     shares = token_sums(w_gate, w_up, grads[1], 1, (first, *probs), etp_ways)
-    shares = [after(share, *dy_slices[1:]) for share in shares]
+    sums_after = shares[0]
     shares = [shares[0]] + [shift(shares[step], -step) for step in range(1, etp_ways)]
     grad_tokens, grad_prob = place(shares, sel)
 
-    mine, theirs = turn_dy(core, dy_slices, chips)
-    got = exchange(theirs_sums(theirs, *scaled), 1)
-    grad_down = down_sums(mine, got, *scaled, inv)
-
-    mine, theirs = turn_x(core, x_slices)
-    far = exchange(theirs, 1)
+    x_mine, x_theirs = turn(core, x_slices)
+    dy_mine, dy_theirs = turn(core, dy_slices)
+    dy_theirs = after(dy_theirs, sums_after)
+    got = exchange(theirs_sums(dy_theirs, *scaled), 1)
+    grad_down = down_sums(dy_mine, got, *scaled, inv)
+
+    far = exchange(after(x_theirs, sums_after), 1)
     held = ()
     for half in range(2):
         others = [
@@ -566,8 +556,8 @@
             for key, part in enumerate(parts[half])
         ]
         if half == 1:
-            mine = after(mine, grad_down)
-        held = pair_sums(mine, far, parts[half], others, held, half, inv)
+            x_mine = after(x_mine, grad_down)
+        held = pair_sums(x_mine, far, parts[half], others, held, half, inv)
     grad_gate, grad_up = held
     return (grad_tokens, grad_prob.reshape(-1), grad_gate, grad_up, grad_down)
 

time: 157 us -> 158 us (level)
  local copies, waits for them, and re-layouts: 14.6 us -> 11.4 us
  starting transfers between devices: 39.7 us -> 41.7 us
  waiting for transfers between devices: 50.1 us -> 51.8 us
    ppermute x28, waiting for transfers between devices: 13.6 us -> 22.5 us  [exchange(): return lax.ppermute(block, 'dp', [(i, i ^ bits) for i in range(ways)])]
    ppermute x12 -> x9, waiting for transfers between devices: 36.4 us -> 29.3 us  [shift(): lax.ppermute(block, 'etp', [(i, (i + step) % ways) for i in range(ways)])]
    ppermute x12 -> x9, starting transfers between devices: 15.1 us -> 20.4 us  [shift(): lax.ppermute(block, 'etp', [(i, (i + step) % ways) for i in range(ways)])]
    ppermute x28, starting transfers between devices: 24.6 us -> 21.3 us  [exchange(): return lax.ppermute(block, 'dp', [(i, i ^ bits) for i in range(ways)])]
    unnamed x39 -> x48, local copies, waits for them, and re-layouts: 14 us -> 11.4 us
    pallas_call x6 -> x7, Pallas kernels: 13.4 us -> 12.3 us  [the longest x2 11.1 us: forward(): call(functools.partial(forward_body, half, count), 'forward', [struct((ro...]
  transfers between devices with their start and end apart: 40 -> 37, of which waited for: 13 -> 9; matrix products, arithmetic and copies ran while one was open for 2% -> 0% of each run, Pallas kernels for 30% -> 30%
where the time goes in v5:
time: 158 us
  Pallas kernels  52 us (33%)
  waiting for transfers between devices  51.8 us (33%)
  starting transfers between devices  41.7 us (26%)
  local copies, waits for them, and re-layouts  11.4 us (7%)
    ppermute x9, waiting for transfers between devices, shift(): lax.ppermute(block, 'etp', [(i, (i + step) % ways) for i in range(ways)])  29.3 us
    ppermute x28, waiting for transfers between devices, exchange(): return lax.ppermute(block, 'dp', [(i, i ^ bits) for i in range(ways)])  22.5 us
    ppermute x28, starting transfers between devices, exchange(): return lax.ppermute(block, 'dp', [(i, i ^ bits) for i in range(ways)])  21.3 us
    ppermute x9, starting transfers between devices, shift(): lax.ppermute(block, 'etp', [(i, (i + step) % ways) for i in range(ways)])  20.4 us
    pallas_call x2, Pallas kernels, token_sums(): call(functools.partial(token_body, half, count), 'token_sums', struct((ro...  14.1 us
    unnamed x48, local copies, waits for them, and re-layouts  11.4 us
    pallas_call x2, Pallas kernels, forward(): call(functools.partial(forward_body, half, count), 'forward', [struct((ro...  11.1 us
    pallas_call x2, Pallas kernels, pair_sums(): call(functools.partial(pair_body, inv, len(parts), steps), 'pair_sums', [...  9.1 us
  transfers between devices with their start and end apart: 37, of which 9 were waited for; matrix products, arithmetic and copies ran while one was open for 0% of the time, Pallas kernels for 30%

profile of v5, /device:TPU:0, one launch (start us, length us, event | category | flops | bytes accessed | tf_op | source)
XLA Modules:
  0.0 157.8 jit_solution(4163230983519883059)
XLA Ops:
  3.5 3.1 %collective-permute-start = (bf16[32,3200]{1,0:T(8,128)(2,1)S(1)}, bf16[32,3200]{1,0:T(8,128)(2,1)S(1)}, u32[]{:S(2)}, u32[]{:S(2)}) collective-permute-start(bf16[32,3200]{1,0:T(8,128)(2,1)S(1)} %get-tuple-element.64.refs_0_), channel_id=1, source_target_pairs={{0,1},{1,2},{2,3},{3,0},{4,5},{5,6},{6,7},{7,4},{8,9},{9,10},{10,1... | collective-permute-start | bytes 614408 | tf_op jit(solution)/shard_map/ppermute | solution.py:52
  6.5 2.6 %collective-permute-start.1 = (bf16[32,3200]{1,0:T(8,128)(2,1)S(1)}, bf16[32,3200]{1,0:T(8,128)(2,1)S(1)}, u32[]{:S(2)}, u32[]{:S(2)}) collective-permute-start(bf16[32,3200]{1,0:T(8,128)(2,1)S(1)} %get-tuple-element.64.refs_0_), channel_id=1, source_target_pairs={{0,2},{1,3},{2,0},{3,1},{4,6},{5,7},{6,4},{7,5},{8,10},{9,11},{10,... | collective-permute-start | bytes 614408 | tf_op jit(solution)/shard_map/ppermute | solution.py:52
  11.8 2.8 %collective-permute-done.refs_1_ = bf16[32,3200]{1,0:T(8,128)(2,1)S(1)} collective-permute-done((bf16[32,3200]{1,0:T(8,128)(2,1)S(1)}, bf16[32,3200]{1,0:T(8,128)(2,1)S(1)}, u32[]{:S(2)}, u32[]{:S(2)}) %collective-permute-start) | collective-permute-done | bytes 204832 | tf_op jit(solution)/shard_map/ppermute | solution.py:52
  14.6 7.9 %collective-permute-done.1.refs_2_ = bf16[32,3200]{1,0:T(8,128)(2,1)S(1)} collective-permute-done((bf16[32,3200]{1,0:T(8,128)(2,1)S(1)}, bf16[32,3200]{1,0:T(8,128)(2,1)S(1)}, u32[]{:S(2)}, u32[]{:S(2)}) %collective-permute-start.1) | collective-permute-done | bytes 204832 | tf_op jit(solution)/shard_map/ppermute | solution.py:52
  22.6 4.9 %collective-permute-start.6 = (bf16[32,3072]{1,0:T(8,128)(2,1)S(1)}, bf16[32,3072]{1,0:T(8,128)(2,1)S(1)}, u32[]{:S(2)}, u32[]{:S(2)}) collective-permute-start(bf16[32,3072]{1,0:T(8,128)(2,1)S(1)} %pack_dy.1.refs_0_), channel_id=1, source_target_pairs={{0,1},{1,2},{2,3},{3,0},{4,5},{5,6},{6,7},{7,4},{8,9},{9,10},{10,1... | collective-permute-start | bytes 589832 | tf_op jit(solution)/shard_map/ppermute | solution.py:52
  27.4 1.6 %collective-permute-start.7 = (bf16[32,3072]{1,0:T(8,128)(2,1)S(1)}, bf16[32,3072]{1,0:T(8,128)(2,1)S(1)}, u32[]{:S(2)}, u32[]{:S(2)}) collective-permute-start(bf16[32,3072]{1,0:T(8,128)(2,1)S(1)} %pack_dy.1.refs_0_), channel_id=1, source_target_pairs={{0,2},{1,3},{2,0},{3,1},{4,6},{5,7},{6,4},{7,5},{8,10},{9,11},{10,... | collective-permute-start | bytes 589832 | tf_op jit(solution)/shard_map/ppermute | solution.py:52
  32.0 1.5 collective-permute-start.4
  33.5 5.5 %forward.2 = (bf16[128,1024]{1,0:T(8,128)(2,1)S(1)}, bf16[128,1024]{1,0:T(8,128)(2,1)S(1)}, f32[128,1024]{1,0:T(8,128)S(1)}, f32[128,1024]{1,0:T(8,128)S(1)}) custom-call(bf16[32,3200]{1,0:T(8,128)(2,1)S(1)} %get-tuple-element.64.refs_0_, bf16[32,3200]{1,0:T(8,128)(2,1)S(1)} %collective-permute-done.refs_1_, ...), custom_call_target="tpu_custom_call" | custom-call | flops 1610612736 | bytes 12582912 | tf_op jit(solution)/shard_map/forward/pallas_call | solution.py:191
  41.0 1.5 collective-permute-start.13
  43.2 5.6 %forward.3 = (bf16[128,1024]{1,0:T(8,128)(2,1)S(1)}, bf16[128,1024]{1,0:T(8,128)(2,1)S(1)}, f32[128,1024]{1,0:T(8,128)S(1)}, f32[128,1024]{1,0:T(8,128)S(1)}) custom-call(bf16[32,3200]{1,0:T(8,128)(2,1)S(1)} %get-tuple-element.64.refs_0_, bf16[32,3200]{1,0:T(8,128)(2,1)S(1)} %collective-permute-done.refs_1_, ...), custom_call_target="tpu_custom_call" | custom-call | flops 1610612736 | bytes 12582912 | tf_op jit(solution)/shard_map/forward/pallas_call | solution.py:191
  49.3 2.4 %collective-permute-start.5 = (bf16[128,768]{1,0:T(8,128)(2,1)S(1)}, bf16[128,768]{1,0:T(8,128)(2,1)S(1)}, u32[]{:S(2)}, u32[]{:S(2)}) collective-permute-start(bf16[128,768]{1,0:T(8,128)(2,1)S(1)} %get-tuple-element.59), channel_id=1, source_target_pairs={{0,24},{4,28},{8,16},{12,20},{16,8},{20,12},{24,0},{28,4},{1,25},{... | collective-permute-start | bytes 589832 | tf_op jit(solution)/shard_map/ppermute | solution.py:57
  53.0 1.5 collective-permute-start.11
  54.5 4.7 %backward.2 = (bf16[128,2048]{1,0:T(8,128)(2,1)}, f32[128,1]{1,0:T(8,128)S(1)}) custom-call(bf16[32,3072]{1,0:T(8,128)(2,1)S(1)} %pack_dy.1.refs_0_, bf16[32,3072]{1,0:T(8,128)(2,1)S(1)} %collective-permute-done.6.refs_1_, bf16[32,3072]{1,0:T(8,128)(2,1)S(1)} %collective-permute-done.7.refs_2_, bf16[32,3072]{1,0:T(8,128)(2,1)S(1)} %collective-permute-done.8.refs_3_, ...), custom_call_target="tpu_custom_call" | custom-call | flops 805306368 | bytes 7864320 | tf_op jit(solution)/shard_map/backward/pallas_call | solution.py:238
  59.2 1.5 collective-permute-start.26
  61.3 8.0 %collective-permute-done.10.refs_2_ = bf16[128,768]{1,0:T(8,128)(2,1)S(1)} collective-permute-done((bf16[128,768]{1,0:T(8,128)(2,1)S(1)}, bf16[128,768]{1,0:T(8,128)(2,1)S(1)}, u32[]{:S(2)}, u32[]{:S(2)}) %collective-permute-start.10) | collective-permute-done | bytes 196640 | tf_op jit(solution)/shard_map/ppermute | solution.py:57
  69.8 1.5 collective-permute-start.17
  72.6 7.3 %token_sums.2.refs_0_ = f32[128,3072]{1,0:T(8,128)S(1)} custom-call(bf16[3072,2048]{1,0:T(8,128)(2,1)} %gate_hbm.3, bf16[3072,2048]{1,0:T(8,128)(2,1)} %up_hbm.3, bf16[128,2048]{1,0:T(8,128)(2,1)} %get-tuple-element.96.grad_ref.refs_0_), custom_call_target="tpu_custom_call" | custom-call | flops 1610612736 | bytes 12582912 | tf_op jit(solution)/shard_map/token_sums/pallas_call | solution.py:300
  79.8 7.6 %collective-permute-done.9.refs_1_ = bf16[128,768]{1,0:T(8,128)(2,1)S(1)} collective-permute-done((bf16[128,768]{1,0:T(8,128)(2,1)S(1)}, bf16[128,768]{1,0:T(8,128)(2,1)S(1)}, u32[]{:S(2)}, u32[]{:S(2)}) %collective-permute-start.9) | collective-permute-done | bytes 196640 | tf_op jit(solution)/shard_map/ppermute | solution.py:57
  87.9 4.0 %backward.3 = (bf16[128,2048]{1,0:T(8,128)(2,1)S(1)}, f32[128,1]{1,0:T(8,128)S(1)}) custom-call(bf16[32,3072]{1,0:T(8,128)(2,1)S(1)} %pack_dy.1.refs_0_, bf16[32,3072]{1,0:T(8,128)(2,1)S(1)} %collective-permute-done.6.refs_1_, bf16[32,3072]{1,0:T(8,128)(2,1)S(1)} %collective-permute-done.7.refs_2_, bf16[32,3072]{1,0:T(8,128)(2,1)S(1)} %collective-permute-done.8.refs_3_, ...), custom_call_target="tpu_custom_call" | custom-call | flops 805306368 | bytes 7864320 | tf_op jit(solution)/shard_map/backward/pallas_call | solution.py:238
  91.9 1.6 %collective-permute-start.24 = (bf16[128,2048]{1,0:T(8,128)(2,1)S(1)}, bf16[128,2048]{1,0:T(8,128)(2,1)S(1)}, u32[]{:S(2)}, u32[]{:S(2)}) collective-permute-start(bf16[128,2048]{1,0:T(8,128)(2,1)S(1)} %get-tuple-element.93.grad_ref.refs_0_), channel_id=1, source_target_pairs={{0,16},{4,20},{8,24},{12,28},{16,0},{20,4},{24,8},{28,12},{1,17},{... | collective-permute-start | bytes 1572872 | tf_op jit(solution)/shard_map/ppermute | solution.py:57
  94.0 6.9 %token_sums.3 = (bf16[32,3200]{1,0:T(8,128)(2,1)S(1)}, bf16[32,3200]{1,0:T(8,128)(2,1)}, bf16[32,3200]{1,0:T(8,128)(2,1)S(1)}, bf16[32,3200]{1,0:T(8,128)(2,1)S(1)}) custom-call(bf16[3072,2048]{1,0:T(8,128)(2,1)} %gate_hbm.3, bf16[3072,2048]{1,0:T(8,128)(2,1)} %up_hbm.3, bf16[128,2048]{1,0:T(8,128)(2,1)S(1)} %get-tuple-element.93.grad_ref.refs_0_, ...), custom_call_target="tpu_custom_call" | custom-call | flops 1610612736 | bytes 12582912 | tf_op jit(solution)/shard_map/token_sums/pallas_call | solution.py:300
  102.3 6.1 %collective-permute-start.18 = (bf16[32,3200]{1,0:T(8,128)(2,1)}, bf16[32,3200]{1,0:T(8,128)(2,1)}, u32[]{:S(2)}, u32[]{:S(2)}) collective-permute-start(bf16[32,3200]{1,0:T(8,128)(2,1)} %get-tuple-element.79), channel_id=1, source_target_pairs={{0,3},{1,0},{2,1},{3,2},{4,7},{5,4},{6,5},{7,6},{8,11},{9,8},{10,9... | collective-permute-start | bytes 614408 | tf_op jit(solution)/shard_map/ppermute | solution.py:52
  112.6 2.0 %theirs_sums.1 = bf16[384,2048]{1,0:T(8,128)(2,1)S(1)} custom-call(bf16[384,512]{1,0:T(8,128)(2,1)S(1)} %get-tuple-element.89.left_ref, bf16[128,1024]{1,0:T(8,128)(2,1)S(1)} %get-tuple-element.63.refs_0_, bf16[128,1024]{1,0:T(8,128)(2,1)S(1)} %collective-permute-done.12.refs_1_, bf16[128,1024]{1,0:T(8,128)(2,1)S(1)} %collective-permute-done.13.refs_2_, ...), custom_call_target="tpu_custom_call" | custom-call | flops 805306368 | bytes 3670016 | tf_op jit(solution)/shard_map/theirs_sums/pallas_call | solution.py:413
  114.7 1.5 collective-permute-start.23
  117.3 8.0 %collective-permute-done.19.refs_2_ = bf16[32,3200]{1,0:T(8,128)(2,1)S(1)} collective-permute-done((bf16[32,3200]{1,0:T(8,128)(2,1)S(1)}, bf16[32,3200]{1,0:T(8,128)(2,1)S(1)}, u32[]{:S(2)}, u32[]{:S(2)}) %collective-permute-start.19) | collective-permute-done | bytes 204832 | tf_op jit(solution)/shard_map/ppermute | solution.py:52
  125.4 9.2 %collective-permute-done.20.refs_3_ = bf16[32,3200]{1,0:T(8,128)(2,1)S(1)} collective-permute-done((bf16[32,3200]{1,0:T(8,128)(2,1)S(1)}, bf16[32,3200]{1,0:T(8,128)(2,1)S(1)}, u32[]{:S(2)}, u32[]{:S(2)}) %collective-permute-start.20) | collective-permute-done | bytes 204832 | tf_op jit(solution)/shard_map/ppermute | solution.py:52
  135.2 5.1 %collective-permute-done.25.refs_3_ = bf16[128,2048]{1,0:T(8,128)(2,1)S(1)} collective-permute-done((bf16[128,2048]{1,0:T(8,128)(2,1)S(1)}, bf16[128,2048]{1,0:T(8,128)(2,1)S(1)}, u32[]{:S(2)}, u32[]{:S(2)}) %collective-permute-start.25) | collective-permute-done | bytes 524320 | tf_op jit(solution)/shard_map/ppermute | solution.py:57
  141.3 1.8 %collective-permute-done.36.refs_7_ = bf16[128,2048]{1,0:T(8,128)(2,1)S(1)} collective-permute-done((bf16[128,2048]{1,0:T(8,128)(2,1)}, bf16[128,2048]{1,0:T(8,128)(2,1)S(1)}, u32[]{:S(2)}, u32[]{:S(2)}) %collective-permute-start.36) | collective-permute-done | bytes 524320 | tf_op jit(solution)/shard_map/ppermute | solution.py:57
  143.2 2.2 %place.1 = (bf16[128,3072]{1,0:T(8,128)(2,1)}, f32[1,128]{1,0:T(1,128)}) custom-call(bf16[32,3200]{1,0:T(8,128)(2,1)S(1)} %get-tuple-element.78.refs_0_, bf16[32,3200]{1,0:T(8,128)(2,1)} %collective-permute-done.18.refs_1_, bf16[32,3200]{1,0:T(8,128)(2,1)S(1)} %collective-permute-done.19.refs_2_, bf16[32,3200]{1,0:T(8,128)(2,1)S(1)} %collective-permute-done.20.refs_3_, ...), custom_call_target="tpu_custom_call" | custom-call | flops 25165824 | bytes 1572864 | tf_op jit(solution)/shard_map/place/pallas_call | solution.py:330
  145.4 5.1 %pair_sums.2 = (bf16[384,2048]{1,0:T(8,128)(2,1)}, bf16[384,2048]{1,0:T(8,128)(2,1)}) custom-call(bf16[384,512]{1,0:T(8,128)(2,1)S(1)} %get-tuple-element.90.left_ref, bf16[384,512]{1,0:T(8,128)(2,1)S(1)} %collective-permute-done.22.other_ref, bf16[128,2048]{1,0:T(8,128)(2,1)} %get-tuple-element.96.grad_ref.refs_0_, ...), custom_call_target="tpu_custom_call" | custom-call | flops 1610612736 | bytes 7340032 | tf_op jit(solution)/shard_map/pair_sums/pallas_call | solution.py:479
  150.6 3.2 %down_sums.1 = bf16[2048,384]{1,0:T(8,128)(2,1)} custom-call(bf16[384,512]{1,0:T(8,128)(2,1)S(1)} %get-tuple-element.87.left_ref, bf16[384,2048]{1,0:T(8,128)(2,1)S(1)} %collective-permute-done.21.got_ref, bf16[128,1024]{1,0:T(8,128)(2,1)S(1)} %get-tuple-element.63.refs_0_, bf16[128,1024]{1,0:T(8,128)(2,1)S(1)} %collective-permute-done.12.refs_1_, ...), custom_call_target="tpu_custom_call" | custom-call | flops 805306368 | bytes 5242880 | tf_op jit(solution)/shard_map/down_sums/pallas_call | solution.py:442
  153.8 4.0 %pair_sums.3 = (bf16[384,2048]{1,0:T(8,128)(2,1)}, bf16[384,2048]{1,0:T(8,128)(2,1)}) custom-call(bf16[384,512]{1,0:T(8,128)(2,1)S(1)} %get-tuple-element.90.left_ref, bf16[384,512]{1,0:T(8,128)(2,1)S(1)} %collective-permute-done.22.other_ref, ...), custom_call_target="tpu_custom_call", output_to_operand_aliasing={{0}: (10, {}), {1}: (11, {})} | custom-call | flops 1610612736 | bytes 7340032 | tf_op jit(solution)/shard_map/pair_sums/pallas_call | solution.py:479
  (107 shorter events, 24.7 us)
Async XLA Ops:
  3.5 11.1 %collective-permute-start = (bf16[32,3200]{1,0:T(8,128)(2,1)S(1)}, bf16[32,3200]{1,0:T(8,128)(2,1)S(1)}, u32[]{:S(2)}, u32[]{:S(2)}) collective-permute-start(bf16[32,3200]{1,0:T(8,128)(2,1)S(1)} %get-tuple-element.64.refs_0_), channel_id=1, source_target_pairs={{0,1},{1,2},{2,3},{3,0},{4,5},{5,6},{6,7},{7,4},{8,9},{9,10},{10,1... | collective-permute-start | bytes 614408 | tf_op jit(solution)/shard_map/ppermute | solution.py:52
  6.5 16.0 %collective-permute-start.1 = (bf16[32,3200]{1,0:T(8,128)(2,1)S(1)}, bf16[32,3200]{1,0:T(8,128)(2,1)S(1)}, u32[]{:S(2)}, u32[]{:S(2)}) collective-permute-start(bf16[32,3200]{1,0:T(8,128)(2,1)S(1)} %get-tuple-element.64.refs_0_), channel_id=1, source_target_pairs={{0,2},{1,3},{2,0},{3,1},{4,6},{5,7},{6,4},{7,5},{8,10},{9,11},{10,... | collective-permute-start | bytes 614408 | tf_op jit(solution)/shard_map/ppermute | solution.py:52
  9.1 13.4 %collective-permute-start.2 = (bf16[32,3200]{1,0:T(8,128)(2,1)S(1)}, bf16[32,3200]{1,0:T(8,128)(2,1)S(1)}, u32[]{:S(2)}, u32[]{:S(2)}) collective-permute-start(bf16[32,3200]{1,0:T(8,128)(2,1)S(1)} %get-tuple-element.64.refs_0_), channel_id=1, source_target_pairs={{0,3},{1,0},{2,1},{3,2},{4,7},{5,4},{6,5},{7,6},{8,11},{9,8},{10,9... | collective-permute-start | bytes 614408 | tf_op jit(solution)/shard_map/ppermute | solution.py:52
  22.6 16.5 %collective-permute-start.6 = (bf16[32,3072]{1,0:T(8,128)(2,1)S(1)}, bf16[32,3072]{1,0:T(8,128)(2,1)S(1)}, u32[]{:S(2)}, u32[]{:S(2)}) collective-permute-start(bf16[32,3072]{1,0:T(8,128)(2,1)S(1)} %pack_dy.1.refs_0_), channel_id=1, source_target_pairs={{0,1},{1,2},{2,3},{3,0},{4,5},{5,6},{6,7},{7,4},{8,9},{9,10},{10,1... | collective-permute-start | bytes 589832 | tf_op jit(solution)/shard_map/ppermute | solution.py:52
  27.4 13.6 %collective-permute-start.7 = (bf16[32,3072]{1,0:T(8,128)(2,1)S(1)}, bf16[32,3072]{1,0:T(8,128)(2,1)S(1)}, u32[]{:S(2)}, u32[]{:S(2)}) collective-permute-start(bf16[32,3072]{1,0:T(8,128)(2,1)S(1)} %pack_dy.1.refs_0_), channel_id=1, source_target_pairs={{0,2},{1,3},{2,0},{3,1},{4,6},{5,7},{6,4},{7,5},{8,10},{9,11},{10,... | collective-permute-start | bytes 589832 | tf_op jit(solution)/shard_map/ppermute | solution.py:52
  29.0 13.5 %collective-permute-start.8 = (bf16[32,3072]{1,0:T(8,128)(2,1)S(1)}, bf16[32,3072]{1,0:T(8,128)(2,1)S(1)}, u32[]{:S(2)}, u32[]{:S(2)}) collective-permute-start(bf16[32,3072]{1,0:T(8,128)(2,1)S(1)} %pack_dy.1.refs_0_), channel_id=1, source_target_pairs={{0,3},{1,0},{2,1},{3,2},{4,7},{5,4},{6,5},{7,6},{8,11},{9,8},{10,9... | collective-permute-start | bytes 589832 | tf_op jit(solution)/shard_map/ppermute | solution.py:52
  30.5 12.0 %collective-permute-start.3 = (bf16[128,768]{1,0:T(8,128)(2,1)S(1)}, bf16[128,768]{1,0:T(8,128)(2,1)S(1)}, u32[]{:S(2)}, u32[]{:S(2)}) collective-permute-start(bf16[128,768]{1,0:T(8,128)(2,1)S(1)} %get-tuple-element.57), channel_id=1, source_target_pairs={{0,8},{4,12},{8,0},{12,4},{16,24},{20,28},{24,16},{28,20},{1,9},{5... | collective-permute-start | bytes 589832 | tf_op jit(solution)/shard_map/ppermute | solution.py:57
  32.0 11.2 %collective-permute-start.4 = (bf16[128,768]{1,0:T(8,128)(2,1)S(1)}, bf16[128,768]{1,0:T(8,128)(2,1)S(1)}, u32[]{:S(2)}, u32[]{:S(2)}) collective-permute-start(bf16[128,768]{1,0:T(8,128)(2,1)S(1)} %get-tuple-element.58), channel_id=1, source_target_pairs={{0,16},{4,20},{8,24},{12,28},{16,0},{20,4},{24,8},{28,12},{1,17},{... | collective-permute-start | bytes 589832 | tf_op jit(solution)/shard_map/ppermute | solution.py:57
  39.1 14.0 %collective-permute-start.12 = (bf16[128,1024]{1,0:T(8,128)(2,1)S(1)}, bf16[128,1024]{1,0:T(8,128)(2,1)S(1)}, u32[]{:S(2)}, u32[]{:S(2)}) collective-permute-start(bf16[128,1024]{1,0:T(8,128)(2,1)S(1)} %get-tuple-element.63.refs_0_), channel_id=1, source_target_pairs={{0,8},{4,12},{8,0},{12,4},{16,24},{20,28},{24,16},{28,20},{1,9},{5... | collective-permute-start | bytes 786440 | tf_op jit(solution)/shard_map/ppermute | solution.py:57
  41.0 13.6 %collective-permute-start.13 = (bf16[128,1024]{1,0:T(8,128)(2,1)S(1)}, bf16[128,1024]{1,0:T(8,128)(2,1)S(1)}, u32[]{:S(2)}, u32[]{:S(2)}) collective-permute-start(bf16[128,1024]{1,0:T(8,128)(2,1)S(1)} %get-tuple-element.63.refs_0_), channel_id=1, source_target_pairs={{0,16},{4,20},{8,24},{12,28},{16,0},{20,4},{24,8},{28,12},{1,17},{... | collective-permute-start | bytes 786440 | tf_op jit(solution)/shard_map/ppermute | solution.py:57
  48.8 21.1 %collective-permute-start.16 = (bf16[128,1024]{1,0:T(8,128)(2,1)S(1)}, bf16[128,1024]{1,0:T(8,128)(2,1)S(1)}, u32[]{:S(2)}, u32[]{:S(2)}) collective-permute-start(bf16[128,1024]{1,0:T(8,128)(2,1)S(1)} %get-tuple-element.65.refs_4_), channel_id=1, source_target_pairs={{0,16},{4,20},{8,24},{12,28},{16,0},{20,4},{24,8},{28,12},{1,17},{... | collective-permute-start | bytes 786440 | tf_op jit(solution)/shard_map/ppermute | solution.py:57
  49.3 11.5 %collective-permute-start.5 = (bf16[128,768]{1,0:T(8,128)(2,1)S(1)}, bf16[128,768]{1,0:T(8,128)(2,1)S(1)}, u32[]{:S(2)}, u32[]{:S(2)}) collective-permute-start(bf16[128,768]{1,0:T(8,128)(2,1)S(1)} %get-tuple-element.59), channel_id=1, source_target_pairs={{0,24},{4,28},{8,16},{12,20},{16,8},{20,12},{24,0},{28,4},{1,25},{... | collective-permute-start | bytes 589832 | tf_op jit(solution)/shard_map/ppermute | solution.py:57
  52.5 16.8 %collective-permute-start.10 = (bf16[128,768]{1,0:T(8,128)(2,1)S(1)}, bf16[128,768]{1,0:T(8,128)(2,1)S(1)}, u32[]{:S(2)}, u32[]{:S(2)}) collective-permute-start(bf16[128,768]{1,0:T(8,128)(2,1)S(1)} %get-tuple-element.61), channel_id=1, source_target_pairs={{0,16},{4,20},{8,24},{12,28},{16,0},{20,4},{24,8},{28,12},{1,17},{... | collective-permute-start | bytes 589832 | tf_op jit(solution)/shard_map/ppermute | solution.py:57
  53.0 18.3 %collective-permute-start.11 = (bf16[128,768]{1,0:T(8,128)(2,1)S(1)}, bf16[128,768]{1,0:T(8,128)(2,1)S(1)}, u32[]{:S(2)}, u32[]{:S(2)}) collective-permute-start(bf16[128,768]{1,0:T(8,128)(2,1)S(1)} %get-tuple-element.62), channel_id=1, source_target_pairs={{0,24},{4,28},{8,16},{12,20},{16,8},{20,12},{24,0},{28,4},{1,25},{... | collective-permute-start | bytes 589832 | tf_op jit(solution)/shard_map/ppermute | solution.py:57
  59.2 34.3 %collective-permute-start.26 = (bf16[128,2048]{1,0:T(8,128)(2,1)}, bf16[128,2048]{1,0:T(8,128)(2,1)}, u32[]{:S(2)}, u32[]{:S(2)}) collective-permute-start(bf16[128,2048]{1,0:T(8,128)(2,1)} %get-tuple-element.96.grad_ref.refs_0_), channel_id=1, source_target_pairs={{0,8},{4,12},{8,0},{12,4},{16,24},{20,28},{24,16},{28,20},{1,9},{5... | collective-permute-start | bytes 1572872 | tf_op jit(solution)/shard_map/ppermute | solution.py:57
  60.8 27.1 %collective-permute-start.15 = (bf16[128,1024]{1,0:T(8,128)(2,1)S(1)}, bf16[128,1024]{1,0:T(8,128)(2,1)S(1)}, u32[]{:S(2)}, u32[]{:S(2)}) collective-permute-start(bf16[128,1024]{1,0:T(8,128)(2,1)S(1)} %get-tuple-element.65.refs_4_), channel_id=1, source_target_pairs={{0,8},{4,12},{8,0},{12,4},{16,24},{20,28},{24,16},{28,20},{1,9},{5... | collective-permute-start | bytes 786440 | tf_op jit(solution)/shard_map/ppermute | solution.py:57
  69.3 18.6 %collective-permute-start.14 = (bf16[128,1024]{1,0:T(8,128)(2,1)S(1)}, bf16[128,1024]{1,0:T(8,128)(2,1)S(1)}, u32[]{:S(2)}, u32[]{:S(2)}) collective-permute-start(bf16[128,1024]{1,0:T(8,128)(2,1)S(1)} %collective-permute-done.12.refs_1_), channel_id=1, source_target_pairs={{0,16},{4,20},{8,24},{12,28},{16,0},{20,4},{24,8},{28,12},{1,17},{... | collective-permute-start | bytes 786440 | tf_op jit(solution)/shard_map/ppermute | solution.py:57
  69.8 18.1 %collective-permute-start.17 = (bf16[128,1024]{1,0:T(8,128)(2,1)S(1)}, bf16[128,1024]{1,0:T(8,128)(2,1)S(1)}, u32[]{:S(2)}, u32[]{:S(2)}) collective-permute-start(bf16[128,1024]{1,0:T(8,128)(2,1)S(1)} %collective-permute-done.16.refs_6_), channel_id=1, source_target_pairs={{0,8},{4,12},{8,0},{12,4},{16,24},{20,28},{24,16},{28,20},{1,9},{5... | collective-permute-start | bytes 786440 | tf_op jit(solution)/shard_map/ppermute | solution.py:57
  72.0 15.4 %collective-permute-start.9 = (bf16[128,768]{1,0:T(8,128)(2,1)S(1)}, bf16[128,768]{1,0:T(8,128)(2,1)S(1)}, u32[]{:S(2)}, u32[]{:S(2)}) collective-permute-start(bf16[128,768]{1,0:T(8,128)(2,1)S(1)} %get-tuple-element.60), channel_id=1, source_target_pairs={{0,8},{4,12},{8,0},{12,4},{16,24},{20,28},{24,16},{28,20},{1,9},{5... | collective-permute-start | bytes 589832 | tf_op jit(solution)/shard_map/ppermute | solution.py:57
  87.4 27.2 %collective-permute-start.32 = (bf16[128,2048]{1,0:T(8,128)(2,1)}, bf16[128,2048]{1,0:T(8,128)(2,1)}, u32[]{:S(2)}, u32[]{:S(2)}) collective-permute-start(bf16[128,2048]{1,0:T(8,128)(2,1)} %get-tuple-element.96.grad_ref.refs_0_), channel_id=1, source_target_pairs={{0,16},{4,20},{8,24},{12,28},{16,0},{20,4},{24,8},{28,12},{1,17},{... | collective-permute-start | bytes 1572872 | tf_op jit(solution)/shard_map/ppermute | solution.py:57
  91.9 24.3 %collective-permute-start.24 = (bf16[128,2048]{1,0:T(8,128)(2,1)S(1)}, bf16[128,2048]{1,0:T(8,128)(2,1)S(1)}, u32[]{:S(2)}, u32[]{:S(2)}) collective-permute-start(bf16[128,2048]{1,0:T(8,128)(2,1)S(1)} %get-tuple-element.93.grad_ref.refs_0_), channel_id=1, source_target_pairs={{0,16},{4,20},{8,24},{12,28},{16,0},{20,4},{24,8},{28,12},{1,17},{... | collective-permute-start | bytes 1572872 | tf_op jit(solution)/shard_map/ppermute | solution.py:57
  93.5 31.9 %collective-permute-start.27 = (bf16[128,2048]{1,0:T(8,128)(2,1)}, bf16[128,2048]{1,0:T(8,128)(2,1)}, u32[]{:S(2)}, u32[]{:S(2)}) collective-permute-start(bf16[128,2048]{1,0:T(8,128)(2,1)} %collective-permute-done.26.refs_1_), channel_id=1, source_target_pairs={{0,16},{4,20},{8,24},{12,28},{16,0},{20,4},{24,8},{28,12},{1,17},{... | collective-permute-start | bytes 1572872 | tf_op jit(solution)/shard_map/ppermute | solution.py:57
  102.3 12.4 %collective-permute-start.18 = (bf16[32,3200]{1,0:T(8,128)(2,1)}, bf16[32,3200]{1,0:T(8,128)(2,1)}, u32[]{:S(2)}, u32[]{:S(2)}) collective-permute-start(bf16[32,3200]{1,0:T(8,128)(2,1)} %get-tuple-element.79), channel_id=1, source_target_pairs={{0,3},{1,0},{2,1},{3,2},{4,7},{5,4},{6,5},{7,6},{8,11},{9,8},{10,9... | collective-permute-start | bytes 614408 | tf_op jit(solution)/shard_map/ppermute | solution.py:52
  114.5 36.0 %collective-permute-start.21 = (bf16[384,2048]{1,0:T(8,128)(2,1)S(1)}, bf16[384,2048]{1,0:T(8,128)(2,1)S(1)}, u32[]{:S(2)}, u32[]{:S(2)}) collective-permute-start(bf16[384,2048]{1,0:T(8,128)(2,1)S(1)} %theirs_sums.1), channel_id=1, source_target_pairs={{0,4},{4,0},{8,12},{12,8},{16,20},{20,16},{24,28},{28,24},{1,5},{5... | collective-permute-start | bytes 4718600 | tf_op jit(solution)/shard_map/ppermute | solution.py:57
  114.6 10.7 %collective-permute-start.19 = (bf16[32,3200]{1,0:T(8,128)(2,1)S(1)}, bf16[32,3200]{1,0:T(8,128)(2,1)S(1)}, u32[]{:S(2)}, u32[]{:S(2)}) collective-permute-start(bf16[32,3200]{1,0:T(8,128)(2,1)S(1)} %copy-done.23), channel_id=1, source_target_pairs={{0,2},{1,3},{2,0},{3,1},{4,6},{5,7},{6,4},{7,5},{8,10},{9,11},{10,... | collective-permute-start | bytes 614408 | tf_op jit(solution)/shard_map/ppermute | solution.py:52
  114.7 20.4 %collective-permute-start.23 = (bf16[128,2048]{1,0:T(8,128)(2,1)S(1)}, bf16[128,2048]{1,0:T(8,128)(2,1)S(1)}, u32[]{:S(2)}, u32[]{:S(2)}) collective-permute-start(bf16[128,2048]{1,0:T(8,128)(2,1)S(1)} %get-tuple-element.93.grad_ref.refs_0_), channel_id=1, source_target_pairs={{0,8},{4,12},{8,0},{12,4},{16,24},{20,28},{24,16},{28,20},{1,9},{5... | collective-permute-start | bytes 1572872 | tf_op jit(solution)/shard_map/ppermute | solution.py:57
  116.3 24.0 %collective-permute-start.25 = (bf16[128,2048]{1,0:T(8,128)(2,1)S(1)}, bf16[128,2048]{1,0:T(8,128)(2,1)S(1)}, u32[]{:S(2)}, u32[]{:S(2)}) collective-permute-start(bf16[128,2048]{1,0:T(8,128)(2,1)S(1)} %collective-permute-done.24.refs_2_), channel_id=1, source_target_pairs={{0,8},{4,12},{8,0},{12,4},{16,24},{20,28},{24,16},{28,20},{1,9},{5... | collective-permute-start | bytes 1572872 | tf_op jit(solution)/shard_map/ppermute | solution.py:57
  125.3 9.3 %collective-permute-start.22 = (bf16[384,512]{1,0:T(8,128)(2,1)S(1)}, bf16[384,512]{1,0:T(8,128)(2,1)S(1)}, u32[]{:S(2)}, u32[]{:S(2)}) collective-permute-start(bf16[384,512]{1,0:T(8,128)(2,1)S(1)} %get-tuple-element.92), channel_id=1, source_target_pairs={{0,4},{4,0},{8,12},{12,8},{16,20},{20,16},{24,28},{28,24},{1,5},{5... | collective-permute-start | bytes 1179656 | tf_op jit(solution)/shard_map/ppermute | solution.py:57
  140.3 13.5 %collective-permute-start.29 = (bf16[128,2048]{1,0:T(8,128)(2,1)S(1)}, bf16[128,2048]{1,0:T(8,128)(2,1)S(1)}, u32[]{:S(2)}, u32[]{:S(2)}) collective-permute-start(bf16[128,2048]{1,0:T(8,128)(2,1)S(1)} %collective-permute-done.23.refs_1_), channel_id=1, source_target_pairs={{0,4},{4,0},{8,12},{12,8},{16,20},{20,16},{24,28},{28,24},{1,5},{5... | collective-permute-start | bytes 1572872 | tf_op jit(solution)/shard_map/ppermute | solution.py:57
  140.8 13.0 %collective-permute-start.30 = (bf16[128,2048]{1,0:T(8,128)(2,1)S(1)}, bf16[128,2048]{1,0:T(8,128)(2,1)S(1)}, u32[]{:S(2)}, u32[]{:S(2)}) collective-permute-start(bf16[128,2048]{1,0:T(8,128)(2,1)S(1)} %collective-permute-done.24.refs_2_), channel_id=1, source_target_pairs={{0,4},{4,0},{8,12},{12,8},{16,20},{20,16},{24,28},{28,24},{1,5},{5... | collective-permute-start | bytes 1572872 | tf_op jit(solution)/shard_map/ppermute | solution.py:57
  140.9 12.9 %collective-permute-start.28 = (bf16[128,2048]{1,0:T(8,128)(2,1)S(1)}, bf16[128,2048]{1,0:T(8,128)(2,1)S(1)}, u32[]{:S(2)}, u32[]{:S(2)}) collective-permute-start(bf16[128,2048]{1,0:T(8,128)(2,1)S(1)} %get-tuple-element.93.grad_ref.refs_0_), channel_id=1, source_target_pairs={{0,4},{4,0},{8,12},{12,8},{16,20},{20,16},{24,28},{28,24},{1,5},{5... | collective-permute-start | bytes 1572872 | tf_op jit(solution)/shard_map/ppermute | solution.py:57
  143.1 10.7 %collective-permute-start.31 = (bf16[128,2048]{1,0:T(8,128)(2,1)S(1)}, bf16[128,2048]{1,0:T(8,128)(2,1)S(1)}, u32[]{:S(2)}, u32[]{:S(2)}) collective-permute-start(bf16[128,2048]{1,0:T(8,128)(2,1)S(1)} %collective-permute-done.25.refs_3_), channel_id=1, source_target_pairs={{0,4},{4,0},{8,12},{12,8},{16,20},{20,16},{24,28},{28,24},{1,5},{5... | collective-permute-start | bytes 1572872 | tf_op jit(solution)/shard_map/ppermute | solution.py:57
  (29 other events, 112.9 us)

commit v6 on v5

--- a/solution.py
+++ b/solution.py
@@ -114,26 +114,29 @@
     )(sel, out_grad)
 
 
-def slice_body(chips, count, chip_ref, *refs):
-    outs = refs[count:]
-    wide = outs[0].shape[1]
-    for key in range(chips):
-        at = pl.multiple_of((chip_ref[0] ^ key) * wide, LANES)
+def slice_body(chips, count, *refs):
+    out_ref = refs[-1]
+    wide = out_ref.shape[2] // 2
+    for chip in range(chips):
+        span = slice(chip * wide, (chip + 1) * wide)
         for z in range(count):
-            outs[key][z * LOC_CAP : (z + 1) * LOC_CAP, :] = refs[z][:, pl.ds(at, wide)]
-
-
-def slices_of(chip, blocks, width, chips):
-    count = len(blocks)
+            rows = slice(z * LOC_CAP, (z + 1) * LOC_CAP)
+            out_ref[chip, rows, :wide] = refs[z][:, span]
+            out_ref[chip, rows, wide:] = refs[count + z][:, span]
+
+
+def slices_of(x_blocks, dy_blocks, chips):
+    count = len(x_blocks)
     rows = count * LOC_CAP
+    width = dy_blocks[0].shape[1]
     return call(
         functools.partial(slice_body, chips, count),
         "slices",
-        [struct((rows, width // chips))] * chips,
-        [IN_SMEM] + [IN_VMEM] * count,
+        struct((chips, rows, 2 * width // chips)),
+        [IN_VMEM] * (2 * count),
         0,
-        4 * rows * width,
-    )(chip, *blocks)
+        8 * rows * width,
+    )(*x_blocks, *dy_blocks)
 
 
 def windowed(groups, sems, ahead):
@@ -352,28 +355,28 @@
         theirs_ref[:, cols] = turned[:part]
 
 
-def turn_body(core_ref, *refs):
-    slices, (mine_ref, theirs_ref) = refs[:-2], refs[-2:]
-    rows = slices[0].shape[0]
-    for key, ref in enumerate(slices):
+def turn_body(chip_ref, core_ref, slices_ref, x_mine, x_theirs, dy_mine, dy_theirs):
+    chips, rows, wide = slices_ref.shape
+    for key in range(chips):
         cols = slice(key * rows, (key + 1) * rows)
-        split_cores(core_ref, mine_ref, theirs_ref, cols, ref[...])
-
-
-def turn(core, slices):
-    rows, wide = slices[0].shape
-    depth = rows * len(slices)
-    out = (wide // 2, depth)
+        at = chip_ref[0] ^ key
+        split_cores(core_ref, x_mine, x_theirs, cols, slices_ref[at, :, : wide // 2])
+        split_cores(core_ref, dy_mine, dy_theirs, cols, slices_ref[at, :, wide // 2 :])
+
+
+def turn(chip, core, slices):
+    chips, rows, wide = slices.shape
+    out = (wide // 4, chips * rows)
     return call(
         turn_body,
         "turn",
-        [struct(out)] * 2,
-        [IN_SMEM] + [whole(slices[0].shape)] * len(slices),
+        [struct(out)] * 4,
+        [IN_SMEM] * 2 + [whole(slices.shape)],
         0,
-        4 * depth * wide,
+        2 * slices.size,
         grid=(1,),
-        out_specs=[whole(out)] * 2,
-    )(core, *slices)
+        out_specs=[whole(out)] * 4,
+    )(chip, core, slices)
 
 
 def stacked(refs):
@@ -512,47 +515,50 @@
     x_blocks = [x_pack] + [shift(x_pack, step) for step in range(1, etp_ways)]
     dy_pack = after(pack_dy(sel, out_grad), *x_blocks[1:])
     dy_blocks = [dy_pack] + [shift(dy_pack, step) for step in range(1, etp_ways)]
-    width = tokens.shape[1]
-    x_slices = slices_of(chip, x_blocks, width, chips)
-    x_slices = [x_slices[0]] + [exchange(x_slices[key], 2 * key) for key in range(1, chips)]
-    near = [x_slices[1 << k] for k in range(chips.bit_length() - 1)]
-    inputs = (x_blocks, [after(x_pack, *near, *dy_blocks[1:]), *x_blocks[1:]])
+    inputs = (x_blocks, [after(x_pack, *dy_blocks[1:]), *x_blocks[1:]])
     scaled, grads, probs, kept_halves = [], [], [], []
     for half in range(2):
         piece, *rest = forward(inputs[half], w_gate, w_up, half)
         scaled.append(chip_gather(piece, chips, half == 1))
         kept_halves.append(rest)
-    dy_slices = slices_of(chip, dy_blocks, width, chips)
-    dy_slices = [dy_slices[0]] + [exchange(dy_slices[key], 2 * key) for key in range(1, chips)]
-    earlier = [scaled[0][key] for key in range(chips) if key.bit_count() == 1]
-    later = [*x_slices[1:], *dy_slices[1:], *scaled[0][1:], *scaled[1][1:]]
+    slices = lax.all_to_all(
+        slices_of(x_blocks, dy_blocks, chips),
+        "dp",
+        split_axis=0,
+        concat_axis=0,
+        tiled=True,
+        axis_index_groups=[[2 * k + at for k in range(chips)] for at in range(2)],
+    )
+    earlier, later = [], []
+    for key in range(1, chips):
+        (earlier if key.bit_count() == 1 else later).extend((scaled[0][key], scaled[1][key]))
+    parts = []
     for half in range(2):
         hidden, silu, slope = kept_halves[half]
         blocks = [after(dy_blocks[0], *earlier), *dy_blocks[1:]]
         grad, prob = backward(blocks, w_down, hidden, silu, slope, half)
         grads.append(grad)
         probs.append(prob)
+        parts.append(chip_gather(grad, chips, half == 1))
         if half == 0:
             first = token_sums(w_gate, w_up, grad, 0, (), etp_ways)
-            earlier = [*later, first]
-    parts = [chip_gather(grads[half], chips, half == 1) for half in range(2)]
-
+            earlier = [*later, first, parts[0][1], parts[0][chips // 2]]
+
+    probs[0] = after(probs[0], slices)
     shares = token_sums(w_gate, w_up, grads[1], 1, (first, *probs), etp_ways)
-    sums_after = shares[0]
     shares = [shares[0]] + [shift(shares[step], -step) for step in range(1, etp_ways)]
     grad_tokens, grad_prob = place(shares, sel)
 
-    x_mine, x_theirs = turn(core, x_slices)
-    dy_mine, dy_theirs = turn(core, dy_slices)
-    dy_theirs = after(dy_theirs, sums_after)
+    x_mine, x_theirs, dy_mine, dy_theirs = turn(chip, core, slices)
+    dy_theirs = after(dy_theirs, *shares[1:], *parts[0][1:], *parts[1][1:])
     got = exchange(theirs_sums(dy_theirs, *scaled), 1)
     grad_down = down_sums(dy_mine, got, *scaled, inv)
 
-    far = exchange(after(x_theirs, sums_after), 1)
+    far = exchange(after(x_theirs, *shares[1:]), 1)
     held = ()
     for half in range(2):
         others = [
-            exchange(after(part, parts[0][-1]) if key.bit_count() < 2 else part, 1)
+            exchange(after(part, parts[half][-1]) if key.bit_count() < 2 else part, 1)
             for key, part in enumerate(parts[half])
         ]
         if half == 1:

time: 158 us -> 180 us (1.14)
  waiting for transfers between devices: 51.8 us -> 67 us
  Pallas kernels: 52 us -> 59 us
    ppermute x28 -> x22, waiting for transfers between devices: 22.5 us -> 42.8 us  [exchange(): return lax.ppermute(block, 'dp', [(i, i ^ bits) for i in range(ways)])]
    ppermute x9, waiting for transfers between devices: 29.3 us -> 24.2 us  [shift(): lax.ppermute(block, 'etp', [(i, (i + step) % ways) for i in range(ways)])]
    ppermute x28 -> x22, starting transfers between devices: 21.3 us -> 16.2 us  [exchange(): return lax.ppermute(block, 'dp', [(i, i ^ bits) for i in range(ways)])]
    all_to_all x0 -> x1, starting transfers between devices: none -> 3.74 us  [shards(): lax.all_to_all(slices_of(x_blocks, dy_blocks, chips), 'dp', split_axis=0,...]
    unnamed x48 -> x64, local copies, waits for them, and re-layouts: 11.4 us -> 11.7 us
  transfers between devices with their start and end apart: 37 -> 32, of which waited for: 9 -> 14; matrix products, arithmetic and copies ran while one was open for 0% -> 0% of each run, Pallas kernels for 30% -> 25%
where the time goes in v6:
time: 180 us; the launch traced here: 179 us
  waiting for transfers between devices  67 us (37%)
  Pallas kernels  59 us (33%)
  starting transfers between devices  40.6 us (23%)
  local copies, waits for them, and re-layouts  11.7 us (6%)
    ppermute x22, waiting for transfers between devices, exchange(): return lax.ppermute(block, 'dp', [(i, i ^ bits) for i in range(ways)])  42.8 us
    ppermute x9, waiting for transfers between devices, shift(): lax.ppermute(block, 'etp', [(i, (i + step) % ways) for i in range(ways)])  24.2 us
    ppermute x9, starting transfers between devices, shift(): lax.ppermute(block, 'etp', [(i, (i + step) % ways) for i in range(ways)])  20.6 us
    ppermute x22, starting transfers between devices, exchange(): return lax.ppermute(block, 'dp', [(i, i ^ bits) for i in range(ways)])  16.2 us
    pallas_call x2, Pallas kernels, token_sums(): call(functools.partial(token_body, half, count), 'token_sums', struct((ro...  15.3 us
    unnamed x64, local copies, waits for them, and re-layouts  11.7 us
    pallas_call x2, Pallas kernels, forward(): call(functools.partial(forward_body, half, count), 'forward', [struct((ro...  11.1 us
    pallas_call x2, Pallas kernels, pair_sums(): call(functools.partial(pair_body, inv, len(parts), steps), 'pair_sums', [...  10.3 us
  transfers between devices with their start and end apart: 32, of which 14 were waited for; matrix products, arithmetic and copies ran while one was open for 0% of the time, Pallas kernels for 25%

profile of v6, /device:TPU:0, one launch (start us, length us, event | category | flops | bytes accessed | tf_op | source)
XLA Modules:
  0.0 179.2 jit_solution(15514994857770145445)
XLA Ops:
  3.5 3.1 %collective-permute-start = (bf16[32,3200]{1,0:T(8,128)(2,1)S(1)}, bf16[32,3200]{1,0:T(8,128)(2,1)S(1)}, u32[]{:S(2)}, u32[]{:S(2)}) collective-permute-start(bf16[32,3200]{1,0:T(8,128)(2,1)S(1)} %get-tuple-element.51.refs_0_), channel_id=1, source_target_pairs={{0,1},{1,2},{2,3},{3,0},{4,5},{5,6},{6,7},{7,4},{8,9},{9,10},{10,1... | collective-permute-start | bytes 614408 | tf_op jit(solution)/shard_map/ppermute | solution.py:52
  6.5 2.6 %collective-permute-start.1 = (bf16[32,3200]{1,0:T(8,128)(2,1)S(1)}, bf16[32,3200]{1,0:T(8,128)(2,1)S(1)}, u32[]{:S(2)}, u32[]{:S(2)}) collective-permute-start(bf16[32,3200]{1,0:T(8,128)(2,1)S(1)} %get-tuple-element.51.refs_0_), channel_id=1, source_target_pairs={{0,2},{1,3},{2,0},{3,1},{4,6},{5,7},{6,4},{7,5},{8,10},{9,11},{10,... | collective-permute-start | bytes 614408 | tf_op jit(solution)/shard_map/ppermute | solution.py:52
  11.9 2.8 %collective-permute-done.refs_1_ = bf16[32,3200]{1,0:T(8,128)(2,1)S(1)} collective-permute-done((bf16[32,3200]{1,0:T(8,128)(2,1)S(1)}, bf16[32,3200]{1,0:T(8,128)(2,1)S(1)}, u32[]{:S(2)}, u32[]{:S(2)}) %collective-permute-start) | collective-permute-done | bytes 204832 | tf_op jit(solution)/shard_map/ppermute | solution.py:52
  14.6 7.9 %collective-permute-done.1.refs_2_ = bf16[32,3200]{1,0:T(8,128)(2,1)S(1)} collective-permute-done((bf16[32,3200]{1,0:T(8,128)(2,1)S(1)}, bf16[32,3200]{1,0:T(8,128)(2,1)S(1)}, u32[]{:S(2)}, u32[]{:S(2)}) %collective-permute-start.1) | collective-permute-done | bytes 204832 | tf_op jit(solution)/shard_map/ppermute | solution.py:52
  22.6 4.9 %collective-permute-start.5 = (bf16[32,3072]{1,0:T(8,128)(2,1)S(1)}, bf16[32,3072]{1,0:T(8,128)(2,1)S(1)}, u32[]{:S(2)}, u32[]{:S(2)}) collective-permute-start(bf16[32,3072]{1,0:T(8,128)(2,1)S(1)} %pack_dy.1.refs_0_.refs_4_), channel_id=1, source_target_pairs={{0,1},{1,2},{2,3},{3,0},{4,5},{5,6},{6,7},{7,4},{8,9},{9,10},{10,1... | collective-permute-start | bytes 589832 | tf_op jit(solution)/shard_map/ppermute | solution.py:52
  27.4 1.6 collective-permute-start.6
  29.8 5.5 %forward.2 = (bf16[128,1024]{1,0:T(8,128)(2,1)S(1)}, bf16[128,1024]{1,0:T(8,128)(2,1)S(1)}, f32[128,1024]{1,0:T(8,128)S(1)}, f32[128,1024]{1,0:T(8,128)S(1)}) custom-call(bf16[32,3200]{1,0:T(8,128)(2,1)S(1)} %get-tuple-element.51.refs_0_, bf16[32,3200]{1,0:T(8,128)(2,1)S(1)} %collective-permute-done.refs_1_, ...), custom_call_target="tpu_custom_call" | custom-call | flops 1610612736 | bytes 12582912 | tf_op jit(solution)/shard_map/forward/pallas_call | solution.py:194
  35.3 1.5 collective-permute-start.3
  36.9 1.5 collective-permute-start.11
  38.4 2.6 %collective-permute-done.6.refs_2_.refs_6_ = bf16[32,3072]{1,0:T(8,128)(2,1)S(1)} collective-permute-done((bf16[32,3072]{1,0:T(8,128)(2,1)S(1)}, bf16[32,3072]{1,0:T(8,128)(2,1)S(1)}, u32[]{:S(2)}, u32[]{:S(2)}) %collective-permute-start.6) | collective-permute-done | bytes 196640 | tf_op jit(solution)/shard_map/ppermute | solution.py:52
  41.0 5.6 %forward.3 = (bf16[128,1024]{1,0:T(8,128)(2,1)S(1)}, bf16[128,1024]{1,0:T(8,128)(2,1)S(1)}, f32[128,1024]{1,0:T(8,128)S(1)}, f32[128,1024]{1,0:T(8,128)S(1)}) custom-call(bf16[32,3200]{1,0:T(8,128)(2,1)S(1)} %get-tuple-element.51.refs_0_, bf16[32,3200]{1,0:T(8,128)(2,1)S(1)} %collective-permute-done.refs_1_, ...), custom_call_target="tpu_custom_call" | custom-call | flops 1610612736 | bytes 12582912 | tf_op jit(solution)/shard_map/forward/pallas_call | solution.py:194
  48.9 1.5 collective-permute-start.8
  50.5 1.5 collective-permute-start.10
  52.6 4.5 %collective-permute-done.8.refs_6_ = bf16[128,1024]{1,0:T(8,128)(2,1)} collective-permute-done((bf16[128,1024]{1,0:T(8,128)(2,1)S(1)}, bf16[128,1024]{1,0:T(8,128)(2,1)}, u32[]{:S(2)}, u32[]{:S(2)}) %collective-permute-start.8) | collective-permute-done | bytes 262176 | tf_op jit(solution)/shard_map/ppermute | solution.py:57
  59.0 4.8 %backward.2 = (bf16[128,2048]{1,0:T(8,128)(2,1)}, f32[128,1]{1,0:T(8,128)S(1)}) custom-call(bf16[32,3072]{1,0:T(8,128)(2,1)S(1)} %pack_dy.1.refs_0_.refs_4_, bf16[32,3072]{1,0:T(8,128)(2,1)S(1)} %collective-permute-done.5.refs_1_.refs_5_, bf16[32,3072]{1,0:T(8,128)(2,1)S(1)} %collective-permute-done.6.refs_2_.refs_6_, ...), custom_call_target="tpu_custom_call" | custom-call | flops 805306368 | bytes 7864320 | tf_op jit(solution)/shard_map/backward/pallas_call | solution.py:241
  64.4 1.5 collective-permute-start.12
  67.7 3.7 %all-to-all-start = ((bf16[4,128,1536]{2,1,0:T(8,128)(2,1)}), bf16[4,128,1536]{2,1,0:T(8,128)(2,1)S(1)}, u32[]{:S(2)}, u32[]{:S(2)}) async-start(bf16[4,128,1536]{2,1,0:T(8,128)(2,1)} %slices.1), calls=%async_computation | async-start | bytes 3145728 | tf_op jit(solution)/shard_map/all_to_all | solution.py:524
  71.5 1.8 %collective-permute-start.4 = (bf16[128,1024]{1,0:T(8,128)(2,1)}, bf16[128,1024]{1,0:T(8,128)(2,1)S(1)}, u32[]{:S(2)}, u32[]{:S(2)}) collective-permute-start(bf16[128,1024]{1,0:T(8,128)(2,1)} %collective-permute-done.3.refs_1_), channel_id=1, source_target_pairs={{0,16},{4,20},{8,24},{12,28},{16,0},{20,4},{24,8},{28,12},{1,17},{... | collective-permute-start | bytes 786440 | tf_op jit(solution)/shard_map/ppermute | solution.py:57
  74.8 7.2 %token_sums.2.refs_0_ = f32[128,3072]{1,0:T(8,128)S(1)} custom-call(bf16[3072,2048]{1,0:T(8,128)(2,1)} %gate_hbm.3, bf16[3072,2048]{1,0:T(8,128)(2,1)} %up_hbm.3, bf16[128,2048]{1,0:T(8,128)(2,1)} %get-tuple-element.82.grad_ref.refs_0_), custom_call_target="tpu_custom_call" | custom-call | flops 1610612736 | bytes 12582912 | tf_op jit(solution)/shard_map/token_sums/pallas_call | solution.py:303
  82.0 19.0 %collective-permute-done.4.refs_3_ = bf16[128,1024]{1,0:T(8,128)(2,1)S(1)} collective-permute-done((bf16[128,1024]{1,0:T(8,128)(2,1)}, bf16[128,1024]{1,0:T(8,128)(2,1)S(1)}, u32[]{:S(2)}, u32[]{:S(2)}) %collective-permute-start.4) | collective-permute-done | bytes 262176 | tf_op jit(solution)/shard_map/ppermute | solution.py:57
  102.4 4.7 %backward.3 = (bf16[128,2048]{1,0:T(8,128)(2,1)}, f32[128,1]{1,0:T(8,128)S(1)}) custom-call(bf16[32,3072]{1,0:T(8,128)(2,1)S(1)} %pack_dy.1.refs_0_.refs_4_, bf16[32,3072]{1,0:T(8,128)(2,1)S(1)} %collective-permute-done.5.refs_1_.refs_5_, bf16[32,3072]{1,0:T(8,128)(2,1)S(1)} %copy-done.1, bf16[32,3072]{1,0:T(8,128)(2,1)S(1)} %copy-done.3, ...), custom_call_target="tpu_custom_call" | custom-call | flops 805306368 | bytes 7864320 | tf_op jit(solution)/shard_map/backward/pallas_call | solution.py:241
  110.3 12.6 %collective-permute-done.19.refs_2_ = bf16[128,2048]{1,0:T(8,128)(2,1)} collective-permute-done((bf16[128,2048]{1,0:T(8,128)(2,1)}, bf16[128,2048]{1,0:T(8,128)(2,1)}, u32[]{:S(2)}, u32[]{:S(2)}) %collective-permute-start.19) | collective-permute-done | bytes 524320 | tf_op jit(solution)/shard_map/ppermute | solution.py:57
  125.2 8.0 %token_sums.3 = (bf16[32,3200]{1,0:T(8,128)(2,1)S(1)}, bf16[32,3200]{1,0:T(8,128)(2,1)}, bf16[32,3200]{1,0:T(8,128)(2,1)}, bf16[32,3200]{1,0:T(8,128)(2,1)}) custom-call(bf16[3072,2048]{1,0:T(8,128)(2,1)} %gate_hbm.3, bf16[3072,2048]{1,0:T(8,128)(2,1)} %up_hbm.3, bf16[128,2048]{1,0:T(8,128)(2,1)} %get-tuple-element.79.grad_ref.refs_0_, ...), custom_call_target="tpu_custom_call" | custom-call | flops 1610612736 | bytes 12582912 | tf_op jit(solution)/shard_map/token_sums/pallas_call | solution.py:303
  133.3 5.7 %collective-permute-start.14 = (bf16[32,3200]{1,0:T(8,128)(2,1)}, bf16[32,3200]{1,0:T(8,128)(2,1)S(1)}, u32[]{:S(2)}, u32[]{:S(2)}) collective-permute-start(bf16[32,3200]{1,0:T(8,128)(2,1)} %get-tuple-element.67), channel_id=1, source_target_pairs={{0,3},{1,0},{2,1},{3,2},{4,7},{5,4},{6,5},{7,6},{8,11},{9,8},{10,9... | collective-permute-start | bytes 614408 | tf_op jit(solution)/shard_map/ppermute | solution.py:52
  140.5 3.5 %collective-permute-done.14.refs_1_ = bf16[32,3200]{1,0:T(8,128)(2,1)S(1)} collective-permute-done((bf16[32,3200]{1,0:T(8,128)(2,1)}, bf16[32,3200]{1,0:T(8,128)(2,1)S(1)}, u32[]{:S(2)}, u32[]{:S(2)}) %collective-permute-start.14) | collective-permute-done | bytes 204832 | tf_op jit(solution)/shard_map/ppermute | solution.py:52
  144.0 7.4 %collective-permute-done.15.refs_2_ = bf16[32,3200]{1,0:T(8,128)(2,1)} collective-permute-done((bf16[32,3200]{1,0:T(8,128)(2,1)}, bf16[32,3200]{1,0:T(8,128)(2,1)}, u32[]{:S(2)}, u32[]{:S(2)}) %collective-permute-start.15) | collective-permute-done | bytes 204832 | tf_op jit(solution)/shard_map/ppermute | solution.py:52
  151.5 3.3 %theirs_sums.1 = bf16[384,2048]{1,0:T(8,128)(2,1)S(1)} custom-call(bf16[384,512]{1,0:T(8,128)(2,1)S(1)} %get-tuple-element.75.left_ref, bf16[128,1024]{1,0:T(8,128)(2,1)S(1)} %copy-done.5, bf16[128,1024]{1,0:T(8,128)(2,1)} %collective-permute-done.3.refs_1_, bf16[128,1024]{1,0:T(8,128)(2,1)S(1)} %copy-done.7, bf16[128,1024]{1,0:T(8,128)(2,1)S(1)} %copy-done.13, ...), custom_call_target="tpu_custom_call" | custom-call | flops 805306368 | bytes 3670016 | tf_op jit(solution)/shard_map/theirs_sums/pallas_call | solution.py:416
  155.9 3.4 %collective-permute-done.22.other_ref = bf16[384,512]{1,0:T(8,128)(2,1)S(1)} collective-permute-done((bf16[384,512]{1,0:T(8,128)(2,1)S(1)}, bf16[384,512]{1,0:T(8,128)(2,1)S(1)}, u32[]{:S(2)}, u32[]{:S(2)}) %collective-permute-start.22) | collective-permute-done | bytes 393248 | tf_op jit(solution)/shard_map/ppermute | solution.py:57
  162.1 2.3 %place.1 = (bf16[128,3072]{1,0:T(8,128)(2,1)}, f32[1,128]{1,0:T(1,128)}) custom-call(bf16[32,3200]{1,0:T(8,128)(2,1)S(1)} %get-tuple-element.66.refs_0_, bf16[32,3200]{1,0:T(8,128)(2,1)S(1)} %collective-permute-done.14.refs_1_, bf16[32,3200]{1,0:T(8,128)(2,1)} %collective-permute-done.15.refs_2_, bf16[32,3200]{1,0:T(8,128)(2,1)} %collective-permute-done.16.refs_3_, ...), custom_call_target="tpu_custom_call" | custom-call | flops 25165824 | bytes 1572864 | tf_op jit(solution)/shard_map/place/pallas_call | solution.py:333
  164.5 5.2 %pair_sums.2 = (bf16[384,2048]{1,0:T(8,128)(2,1)}, bf16[384,2048]{1,0:T(8,128)(2,1)}) custom-call(bf16[384,512]{1,0:T(8,128)(2,1)S(1)} %get-tuple-element.76.left_ref, bf16[384,512]{1,0:T(8,128)(2,1)S(1)} %collective-permute-done.22.other_ref, bf16[128,2048]{1,0:T(8,128)(2,1)} %get-tuple-element.82.grad_ref.refs_0_, ...), custom_call_target="tpu_custom_call" | custom-call | flops 1610612736 | bytes 7340032 | tf_op jit(solution)/shard_map/pair_sums/pallas_call | solution.py:482
  169.6 4.4 %down_sums.1 = bf16[2048,384]{1,0:T(8,128)(2,1)} custom-call(bf16[384,512]{1,0:T(8,128)(2,1)S(1)} %get-tuple-element.73.left_ref, bf16[384,2048]{1,0:T(8,128)(2,1)S(1)} %collective-permute-done.21.got_ref, bf16[128,1024]{1,0:T(8,128)(2,1)S(1)} %copy-done.5, bf16[128,1024]{1,0:T(8,128)(2,1)} %collective-permute-done.3.refs_1_, ...), custom_call_target="tpu_custom_call" | custom-call | flops 805306368 | bytes 5242880 | tf_op jit(solution)/shard_map/down_sums/pallas_call | solution.py:445
  174.1 5.2 %pair_sums.3 = (bf16[384,2048]{1,0:T(8,128)(2,1)}, bf16[384,2048]{1,0:T(8,128)(2,1)}) custom-call(bf16[384,512]{1,0:T(8,128)(2,1)S(1)} %get-tuple-element.76.left_ref, bf16[384,512]{1,0:T(8,128)(2,1)S(1)} %collective-permute-done.22.other_ref, bf16[128,2048]{1,0:T(8,128)(2,1)} %get-tuple-element.79.grad_ref.refs_0_, ...), custom_call_target="tpu_custom_call", output_to_operand_aliasing={{0}: (10, {}), {1}: (11, {})} | custom-call | flops 1610612736 | bytes 7340032 | tf_op jit(solution)/shard_map/pair_sums/pallas_call | solution.py:482
  (111 shorter events, 27.3 us)
Async XLA Ops:
  3.5 11.1 %collective-permute-start = (bf16[32,3200]{1,0:T(8,128)(2,1)S(1)}, bf16[32,3200]{1,0:T(8,128)(2,1)S(1)}, u32[]{:S(2)}, u32[]{:S(2)}) collective-permute-start(bf16[32,3200]{1,0:T(8,128)(2,1)S(1)} %get-tuple-element.51.refs_0_), channel_id=1, source_target_pairs={{0,1},{1,2},{2,3},{3,0},{4,5},{5,6},{6,7},{7,4},{8,9},{9,10},{10,1... | collective-permute-start | bytes 614408 | tf_op jit(solution)/shard_map/ppermute | solution.py:52
  6.5 16.0 %collective-permute-start.1 = (bf16[32,3200]{1,0:T(8,128)(2,1)S(1)}, bf16[32,3200]{1,0:T(8,128)(2,1)S(1)}, u32[]{:S(2)}, u32[]{:S(2)}) collective-permute-start(bf16[32,3200]{1,0:T(8,128)(2,1)S(1)} %get-tuple-element.51.refs_0_), channel_id=1, source_target_pairs={{0,2},{1,3},{2,0},{3,1},{4,6},{5,7},{6,4},{7,5},{8,10},{9,11},{10,... | collective-permute-start | bytes 614408 | tf_op jit(solution)/shard_map/ppermute | solution.py:52
  9.1 13.4 %collective-permute-start.2 = (bf16[32,3200]{1,0:T(8,128)(2,1)S(1)}, bf16[32,3200]{1,0:T(8,128)(2,1)S(1)}, u32[]{:S(2)}, u32[]{:S(2)}) collective-permute-start(bf16[32,3200]{1,0:T(8,128)(2,1)S(1)} %get-tuple-element.51.refs_0_), channel_id=1, source_target_pairs={{0,3},{1,0},{2,1},{3,2},{4,7},{5,4},{6,5},{7,6},{8,11},{9,8},{10,9... | collective-permute-start | bytes 614408 | tf_op jit(solution)/shard_map/ppermute | solution.py:52
  22.6 15.8 %collective-permute-start.5 = (bf16[32,3072]{1,0:T(8,128)(2,1)S(1)}, bf16[32,3072]{1,0:T(8,128)(2,1)S(1)}, u32[]{:S(2)}, u32[]{:S(2)}) collective-permute-start(bf16[32,3072]{1,0:T(8,128)(2,1)S(1)} %pack_dy.1.refs_0_.refs_4_), channel_id=1, source_target_pairs={{0,1},{1,2},{2,3},{3,0},{4,5},{5,6},{6,7},{7,4},{8,9},{9,10},{10,1... | collective-permute-start | bytes 589832 | tf_op jit(solution)/shard_map/ppermute | solution.py:52
  27.4 13.6 %collective-permute-start.6 = (bf16[32,3072]{1,0:T(8,128)(2,1)S(1)}, bf16[32,3072]{1,0:T(8,128)(2,1)S(1)}, u32[]{:S(2)}, u32[]{:S(2)}) collective-permute-start(bf16[32,3072]{1,0:T(8,128)(2,1)S(1)} %pack_dy.1.refs_0_.refs_4_), channel_id=1, source_target_pairs={{0,2},{1,3},{2,0},{3,1},{4,6},{5,7},{6,4},{7,5},{8,10},{9,11},{10,... | collective-permute-start | bytes 589832 | tf_op jit(solution)/shard_map/ppermute | solution.py:52
  29.0 12.0 %collective-permute-start.7 = (bf16[32,3072]{1,0:T(8,128)(2,1)S(1)}, bf16[32,3072]{1,0:T(8,128)(2,1)S(1)}, u32[]{:S(2)}, u32[]{:S(2)}) collective-permute-start(bf16[32,3072]{1,0:T(8,128)(2,1)S(1)} %pack_dy.1.refs_0_.refs_4_), channel_id=1, source_target_pairs={{0,3},{1,0},{2,1},{3,2},{4,7},{5,4},{6,5},{7,6},{8,11},{9,8},{10,9... | collective-permute-start | bytes 589832 | tf_op jit(solution)/shard_map/ppermute | solution.py:52
  35.3 17.3 %collective-permute-start.3 = (bf16[128,1024]{1,0:T(8,128)(2,1)S(1)}, bf16[128,1024]{1,0:T(8,128)(2,1)}, u32[]{:S(2)}, u32[]{:S(2)}) collective-permute-start(bf16[128,1024]{1,0:T(8,128)(2,1)S(1)} %get-tuple-element.50.refs_0_), channel_id=1, source_target_pairs={{0,8},{4,12},{8,0},{12,4},{16,24},{20,28},{24,16},{28,20},{1,9},{5... | collective-permute-start | bytes 786440 | tf_op jit(solution)/shard_map/ppermute | solution.py:57
  36.9 15.8 %collective-permute-start.11 = (bf16[128,1024]{1,0:T(8,128)(2,1)S(1)}, bf16[128,1024]{1,0:T(8,128)(2,1)S(1)}, u32[]{:S(2)}, u32[]{:S(2)}) collective-permute-start(bf16[128,1024]{1,0:T(8,128)(2,1)S(1)} %get-tuple-element.50.refs_0_), channel_id=1, source_target_pairs={{0,16},{4,20},{8,24},{12,28},{16,0},{20,4},{24,8},{28,12},{1,17},{... | collective-permute-start | bytes 786440 | tf_op jit(solution)/shard_map/ppermute | solution.py:57
  48.9 8.2 %collective-permute-start.8 = (bf16[128,1024]{1,0:T(8,128)(2,1)S(1)}, bf16[128,1024]{1,0:T(8,128)(2,1)}, u32[]{:S(2)}, u32[]{:S(2)}) collective-permute-start(bf16[128,1024]{1,0:T(8,128)(2,1)S(1)} %get-tuple-element.52.refs_4_), channel_id=1, source_target_pairs={{0,16},{4,20},{8,24},{12,28},{16,0},{20,4},{24,8},{28,12},{1,17},{... | collective-permute-start | bytes 786440 | tf_op jit(solution)/shard_map/ppermute | solution.py:57
  50.5 7.8 %collective-permute-start.10 = (bf16[128,1024]{1,0:T(8,128)(2,1)S(1)}, bf16[128,1024]{1,0:T(8,128)(2,1)S(1)}, u32[]{:S(2)}, u32[]{:S(2)}) collective-permute-start(bf16[128,1024]{1,0:T(8,128)(2,1)S(1)} %get-tuple-element.52.refs_4_), channel_id=1, source_target_pairs={{0,8},{4,12},{8,0},{12,4},{16,24},{20,28},{24,16},{28,20},{1,9},{5... | collective-permute-start | bytes 786440 | tf_op jit(solution)/shard_map/ppermute | solution.py:57
  64.4 38.0 %collective-permute-start.12 = (bf16[128,2048]{1,0:T(8,128)(2,1)}, bf16[128,2048]{1,0:T(8,128)(2,1)}, u32[]{:S(2)}, u32[]{:S(2)}) collective-permute-start(bf16[128,2048]{1,0:T(8,128)(2,1)} %get-tuple-element.82.grad_ref.refs_0_), channel_id=1, source_target_pairs={{0,8},{4,12},{8,0},{12,4},{16,24},{20,28},{24,16},{28,20},{1,9},{5... | collective-permute-start | bytes 1572872 | tf_op jit(solution)/shard_map/ppermute | solution.py:57
  65.9 36.5 %collective-permute-start.13 = (bf16[128,2048]{1,0:T(8,128)(2,1)}, bf16[128,2048]{1,0:T(8,128)(2,1)}, u32[]{:S(2)}, u32[]{:S(2)}) collective-permute-start(bf16[128,2048]{1,0:T(8,128)(2,1)} %get-tuple-element.82.grad_ref.refs_0_), channel_id=1, source_target_pairs={{0,16},{4,20},{8,24},{12,28},{16,0},{20,4},{24,8},{28,12},{1,17},{... | collective-permute-start | bytes 1572872 | tf_op jit(solution)/shard_map/ppermute | solution.py:57
  67.7 55.8 %all-to-all-start = ((bf16[4,128,1536]{2,1,0:T(8,128)(2,1)}), bf16[4,128,1536]{2,1,0:T(8,128)(2,1)S(1)}, u32[]{:S(2)}, u32[]{:S(2)}) async-start(bf16[4,128,1536]{2,1,0:T(8,128)(2,1)} %slices.1), calls=%async_computation | async-start | bytes 3145728 | tf_op jit(solution)/shard_map/all_to_all | solution.py:524
  71.5 29.5 %collective-permute-start.4 = (bf16[128,1024]{1,0:T(8,128)(2,1)}, bf16[128,1024]{1,0:T(8,128)(2,1)S(1)}, u32[]{:S(2)}, u32[]{:S(2)}) collective-permute-start(bf16[128,1024]{1,0:T(8,128)(2,1)} %collective-permute-done.3.refs_1_), channel_id=1, source_target_pairs={{0,16},{4,20},{8,24},{12,28},{16,0},{20,4},{24,8},{28,12},{1,17},{... | collective-permute-start | bytes 786440 | tf_op jit(solution)/shard_map/ppermute | solution.py:57
  73.3 28.4 %collective-permute-start.9 = (bf16[128,1024]{1,0:T(8,128)(2,1)}, bf16[128,1024]{1,0:T(8,128)(2,1)S(1)}, u32[]{:S(2)}, u32[]{:S(2)}) collective-permute-start(bf16[128,1024]{1,0:T(8,128)(2,1)} %collective-permute-done.8.refs_6_), channel_id=1, source_target_pairs={{0,8},{4,12},{8,0},{12,4},{16,24},{20,28},{24,16},{28,20},{1,9},{5... | collective-permute-start | bytes 786440 | tf_op jit(solution)/shard_map/ppermute | solution.py:57
  107.8 15.2 %collective-permute-start.19 = (bf16[128,2048]{1,0:T(8,128)(2,1)}, bf16[128,2048]{1,0:T(8,128)(2,1)}, u32[]{:S(2)}, u32[]{:S(2)}) collective-permute-start(bf16[128,2048]{1,0:T(8,128)(2,1)} %get-tuple-element.79.grad_ref.refs_0_), channel_id=1, source_target_pairs={{0,16},{4,20},{8,24},{12,28},{16,0},{20,4},{24,8},{28,12},{1,17},{... | collective-permute-start | bytes 1572872 | tf_op jit(solution)/shard_map/ppermute | solution.py:57
  108.4 31.2 %collective-permute-start.17 = (bf16[128,2048]{1,0:T(8,128)(2,1)}, bf16[128,2048]{1,0:T(8,128)(2,1)}, u32[]{:S(2)}, u32[]{:S(2)}) collective-permute-start(bf16[128,2048]{1,0:T(8,128)(2,1)} %collective-permute-done.12.refs_1_), channel_id=1, source_target_pairs={{0,16},{4,20},{8,24},{12,28},{16,0},{20,4},{24,8},{28,12},{1,17},{... | collective-permute-start | bytes 1572872 | tf_op jit(solution)/shard_map/ppermute | solution.py:57
  109.8 30.7 %collective-permute-start.18 = (bf16[128,2048]{1,0:T(8,128)(2,1)}, bf16[128,2048]{1,0:T(8,128)(2,1)}, u32[]{:S(2)}, u32[]{:S(2)}) collective-permute-start(bf16[128,2048]{1,0:T(8,128)(2,1)} %get-tuple-element.79.grad_ref.refs_0_), channel_id=1, source_target_pairs={{0,8},{4,12},{8,0},{12,4},{16,24},{20,28},{24,16},{28,20},{1,9},{5... | collective-permute-start | bytes 1572872 | tf_op jit(solution)/shard_map/ppermute | solution.py:57
  123.0 28.4 %collective-permute-start.20 = (bf16[128,2048]{1,0:T(8,128)(2,1)}, bf16[128,2048]{1,0:T(8,128)(2,1)}, u32[]{:S(2)}, u32[]{:S(2)}) collective-permute-start(bf16[128,2048]{1,0:T(8,128)(2,1)} %collective-permute-done.19.refs_2_), channel_id=1, source_target_pairs={{0,8},{4,12},{8,0},{12,4},{16,24},{20,28},{24,16},{28,20},{1,9},{5... | collective-permute-start | bytes 1572872 | tf_op jit(solution)/shard_map/ppermute | solution.py:57
  133.3 10.7 %collective-permute-start.14 = (bf16[32,3200]{1,0:T(8,128)(2,1)}, bf16[32,3200]{1,0:T(8,128)(2,1)S(1)}, u32[]{:S(2)}, u32[]{:S(2)}) collective-permute-start(bf16[32,3200]{1,0:T(8,128)(2,1)} %get-tuple-element.67), channel_id=1, source_target_pairs={{0,3},{1,0},{2,1},{3,2},{4,7},{5,4},{6,5},{7,6},{8,11},{9,8},{10,9... | collective-permute-start | bytes 614408 | tf_op jit(solution)/shard_map/ppermute | solution.py:52
  138.9 12.5 %collective-permute-start.15 = (bf16[32,3200]{1,0:T(8,128)(2,1)}, bf16[32,3200]{1,0:T(8,128)(2,1)}, u32[]{:S(2)}, u32[]{:S(2)}) collective-permute-start(bf16[32,3200]{1,0:T(8,128)(2,1)} %get-tuple-element.68), channel_id=1, source_target_pairs={{0,2},{1,3},{2,0},{3,1},{4,6},{5,7},{6,4},{7,5},{8,10},{9,11},{10,... | collective-permute-start | bytes 614408 | tf_op jit(solution)/shard_map/ppermute | solution.py:52
  139.6 11.8 %collective-permute-start.16 = (bf16[32,3200]{1,0:T(8,128)(2,1)}, bf16[32,3200]{1,0:T(8,128)(2,1)}, u32[]{:S(2)}, u32[]{:S(2)}) collective-permute-start(bf16[32,3200]{1,0:T(8,128)(2,1)} %get-tuple-element.69), channel_id=1, source_target_pairs={{0,1},{1,2},{2,3},{3,0},{4,5},{5,6},{6,7},{7,4},{8,9},{9,10},{10,1... | collective-permute-start | bytes 614408 | tf_op jit(solution)/shard_map/ppermute | solution.py:52
  154.8 14.9 %collective-permute-start.21 = (bf16[384,2048]{1,0:T(8,128)(2,1)S(1)}, bf16[384,2048]{1,0:T(8,128)(2,1)S(1)}, u32[]{:S(2)}, u32[]{:S(2)}) collective-permute-start(bf16[384,2048]{1,0:T(8,128)(2,1)S(1)} %theirs_sums.1), channel_id=1, source_target_pairs={{0,4},{4,0},{8,12},{12,8},{16,20},{20,16},{24,28},{28,24},{1,5},{5... | collective-permute-start | bytes 4718600 | tf_op jit(solution)/shard_map/ppermute | solution.py:57
  154.8 4.5 %collective-permute-start.22 = (bf16[384,512]{1,0:T(8,128)(2,1)S(1)}, bf16[384,512]{1,0:T(8,128)(2,1)S(1)}, u32[]{:S(2)}, u32[]{:S(2)}) collective-permute-start(bf16[384,512]{1,0:T(8,128)(2,1)S(1)} %get-tuple-element.78), channel_id=1, source_target_pairs={{0,4},{4,0},{8,12},{12,8},{16,20},{20,16},{24,28},{28,24},{1,5},{5... | collective-permute-start | bytes 1179656 | tf_op jit(solution)/shard_map/ppermute | solution.py:57
  155.3 4.4 %collective-permute-start.28 = (bf16[128,2048]{1,0:T(8,128)(2,1)}, bf16[128,2048]{1,0:T(8,128)(2,1)S(1)}, u32[]{:S(2)}, u32[]{:S(2)}) collective-permute-start(bf16[128,2048]{1,0:T(8,128)(2,1)} %collective-permute-done.12.refs_1_), channel_id=1, source_target_pairs={{0,4},{4,0},{8,12},{12,8},{16,20},{20,16},{24,28},{28,24},{1,5},{5... | collective-permute-start | bytes 1572872 | tf_op jit(solution)/shard_map/ppermute | solution.py:57
  155.4 5.1 %collective-permute-start.29 = (bf16[128,2048]{1,0:T(8,128)(2,1)}, bf16[128,2048]{1,0:T(8,128)(2,1)S(1)}, u32[]{:S(2)}, u32[]{:S(2)}) collective-permute-start(bf16[128,2048]{1,0:T(8,128)(2,1)} %collective-permute-done.13.refs_2_), channel_id=1, source_target_pairs={{0,4},{4,0},{8,12},{12,8},{16,20},{20,16},{24,28},{28,24},{1,5},{5... | collective-permute-start | bytes 1572872 | tf_op jit(solution)/shard_map/ppermute | solution.py:57
  155.8 5.4 %collective-permute-start.27 = (bf16[128,2048]{1,0:T(8,128)(2,1)}, bf16[128,2048]{1,0:T(8,128)(2,1)S(1)}, u32[]{:S(2)}, u32[]{:S(2)}) collective-permute-start(bf16[128,2048]{1,0:T(8,128)(2,1)} %get-tuple-element.82.grad_ref.refs_0_), channel_id=1, source_target_pairs={{0,4},{4,0},{8,12},{12,8},{16,20},{20,16},{24,28},{28,24},{1,5},{5... | collective-permute-start | bytes 1572872 | tf_op jit(solution)/shard_map/ppermute | solution.py:57
  159.4 2.6 %collective-permute-start.30 = (bf16[128,2048]{1,0:T(8,128)(2,1)}, bf16[128,2048]{1,0:T(8,128)(2,1)S(1)}, u32[]{:S(2)}, u32[]{:S(2)}) collective-permute-start(bf16[128,2048]{1,0:T(8,128)(2,1)} %collective-permute-done.17.refs_3_), channel_id=1, source_target_pairs={{0,4},{4,0},{8,12},{12,8},{16,20},{20,16},{24,28},{28,24},{1,5},{5... | collective-permute-start | bytes 1572872 | tf_op jit(solution)/shard_map/ppermute | solution.py:57
  159.8 14.3 %collective-permute-start.24 = (bf16[128,2048]{1,0:T(8,128)(2,1)}, bf16[128,2048]{1,0:T(8,128)(2,1)S(1)}, u32[]{:S(2)}, u32[]{:S(2)}) collective-permute-start(bf16[128,2048]{1,0:T(8,128)(2,1)} %collective-permute-done.18.refs_1_), channel_id=1, source_target_pairs={{0,4},{4,0},{8,12},{12,8},{16,20},{20,16},{24,28},{28,24},{1,5},{5... | collective-permute-start | bytes 1572872 | tf_op jit(solution)/shard_map/ppermute | solution.py:57
  160.5 13.5 %collective-permute-start.25 = (bf16[128,2048]{1,0:T(8,128)(2,1)}, bf16[128,2048]{1,0:T(8,128)(2,1)S(1)}, u32[]{:S(2)}, u32[]{:S(2)}) collective-permute-start(bf16[128,2048]{1,0:T(8,128)(2,1)} %collective-permute-done.19.refs_2_), channel_id=1, source_target_pairs={{0,4},{4,0},{8,12},{12,8},{16,20},{20,16},{24,28},{28,24},{1,5},{5... | collective-permute-start | bytes 1572872 | tf_op jit(solution)/shard_map/ppermute | solution.py:57
  161.3 12.8 %collective-permute-start.23 = (bf16[128,2048]{1,0:T(8,128)(2,1)}, bf16[128,2048]{1,0:T(8,128)(2,1)S(1)}, u32[]{:S(2)}, u32[]{:S(2)}) collective-permute-start(bf16[128,2048]{1,0:T(8,128)(2,1)} %get-tuple-element.79.grad_ref.refs_0_), channel_id=1, source_target_pairs={{0,4},{4,0},{8,12},{12,8},{16,20},{20,16},{24,28},{28,24},{1,5},{5... | collective-permute-start | bytes 1572872 | tf_op jit(solution)/shard_map/ppermute | solution.py:57
  162.0 12.0 %collective-permute-start.26 = (bf16[128,2048]{1,0:T(8,128)(2,1)}, bf16[128,2048]{1,0:T(8,128)(2,1)S(1)}, u32[]{:S(2)}, u32[]{:S(2)}) collective-permute-start(bf16[128,2048]{1,0:T(8,128)(2,1)} %collective-permute-done.20.refs_3_), channel_id=1, source_target_pairs={{0,4},{4,0},{8,12},{12,8},{16,20},{20,16},{24,28},{28,24},{1,5},{5... | collective-permute-start | bytes 1572872 | tf_op jit(solution)/shard_map/ppermute | solution.py:57
  (32 other events, 385.1 us)

commit v7 on v5

--- a/solution.py
+++ b/solution.py
@@ -57,12 +57,12 @@
     return lax.ppermute(block, "dp", [(i, i ^ bits) for i in range(ways)])
 
 
-def chip_gather(piece, chips, turned):
+def chip_gather(piece, chips, turned, hold=()):
     bits = [1 << k for k in range(chips.bit_length() - 1)]
     held = {0: piece}
     for bit in bits[::-1] if turned else bits:
         for key in sorted(held):
-            held[key ^ bit] = exchange(held[key], 2 * bit)
+            held[key ^ bit] = exchange(after(held[key], *hold) if key else held[key], 2 * bit)
     return [held[key] for key in range(chips)]
 
 
@@ -134,6 +134,28 @@
         0,
         4 * rows * width,
     )(chip, *blocks)
+
+
+def columns_body(count, *refs):
+    out_ref = refs[-1]
+    wide = out_ref.shape[2]
+    for chip in range(out_ref.shape[0]):
+        for z in range(count):
+            out_ref[chip, z * LOC_CAP : (z + 1) * LOC_CAP, :] = refs[z][:, chip * wide : (chip + 1) * wide]
+
+
+def columns_of(blocks, chips):
+    count = len(blocks)
+    rows = count * LOC_CAP
+    width = blocks[0].shape[1]
+    return call(
+        functools.partial(columns_body, count),
+        "columns",
+        struct((chips, rows, width // chips)),
+        [IN_VMEM] * count,
+        0,
+        4 * rows * width,
+    )(*blocks)
 
 
 def windowed(groups, sems, ahead):
@@ -376,6 +398,28 @@
     )(core, *slices)
 
 
+def turn_columns_body(chip_ref, core_ref, columns_ref, mine_ref, theirs_ref):
+    chips, rows, _ = columns_ref.shape
+    for key in range(chips):
+        cols = slice(key * rows, (key + 1) * rows)
+        split_cores(core_ref, mine_ref, theirs_ref, cols, columns_ref[chip_ref[0] ^ key])
+
+
+def turn_columns(chip, core, columns):
+    chips, rows, wide = columns.shape
+    out = (wide // 2, chips * rows)
+    return call(
+        turn_columns_body,
+        "turn_columns",
+        [struct(out)] * 2,
+        [IN_SMEM] * 2 + [whole(columns.shape)],
+        0,
+        2 * columns.size,
+        grid=(1,),
+        out_specs=[whole(out)] * 2,
+    )(chip, core, columns)
+
+
 def stacked(refs):
     return jnp.concatenate([ref[...] for ref in refs], axis=0)
 
@@ -522,10 +566,10 @@
         piece, *rest = forward(inputs[half], w_gate, w_up, half)
         scaled.append(chip_gather(piece, chips, half == 1))
         kept_halves.append(rest)
-    dy_slices = slices_of(chip, dy_blocks, width, chips)
-    dy_slices = [dy_slices[0]] + [exchange(dy_slices[key], 2 * key) for key in range(1, chips)]
-    earlier = [scaled[0][key] for key in range(chips) if key.bit_count() == 1]
-    later = [*x_slices[1:], *dy_slices[1:], *scaled[0][1:], *scaled[1][1:]]
+    earlier = [*x_slices[1:], *scaled[0][1:]]
+    earlier += [scaled[1][key] for key in range(1, chips) if key.bit_count() == 1]
+    later = [scaled[1][key] for key in range(1, chips) if key.bit_count() > 1]
+    parts = []
     for half in range(2):
         hidden, silu, slope = kept_halves[half]
         blocks = [after(dy_blocks[0], *earlier), *dy_blocks[1:]]
@@ -534,25 +578,33 @@
         probs.append(prob)
         if half == 0:
             first = token_sums(w_gate, w_up, grad, 0, (), etp_ways)
-            earlier = [*later, first]
-    parts = [chip_gather(grads[half], chips, half == 1) for half in range(2)]
+            parts.append(chip_gather(grad, chips, False, (first,)))
+            earlier = [*later, first, parts[0][1], parts[0][chips // 2]]
+    dy_columns = lax.all_to_all(
+        columns_of([after(dy_blocks[0], probs[0]), *dy_blocks[1:]], chips),
+        "dp",
+        split_axis=0,
+        concat_axis=0,
+        tiled=True,
+        axis_index_groups=[[2 * k + at for k in range(chips)] for at in range(2)],
+    )
 
     shares = token_sums(w_gate, w_up, grads[1], 1, (first, *probs), etp_ways)
-    sums_after = shares[0]
+    parts.append(chip_gather(grads[1], chips, True, (shares[0],)))
     shares = [shares[0]] + [shift(shares[step], -step) for step in range(1, etp_ways)]
     grad_tokens, grad_prob = place(shares, sel)
 
     x_mine, x_theirs = turn(core, x_slices)
-    dy_mine, dy_theirs = turn(core, dy_slices)
-    dy_theirs = after(dy_theirs, sums_after)
+    dy_mine, dy_theirs = turn_columns(chip, core, dy_columns)
+    dy_theirs = after(dy_theirs, *shares[1:], *parts[0][1:], *parts[1][1:])
     got = exchange(theirs_sums(dy_theirs, *scaled), 1)
     grad_down = down_sums(dy_mine, got, *scaled, inv)
 
-    far = exchange(after(x_theirs, sums_after), 1)
+    far = exchange(after(x_theirs, *shares[1:]), 1)
     held = ()
     for half in range(2):
         others = [
-            exchange(after(part, parts[0][-1]) if key.bit_count() < 2 else part, 1)
+            exchange(after(part, parts[half][-1]) if key.bit_count() < 2 else part, 1)
             for key, part in enumerate(parts[half])
         ]
         if half == 1:

time: 158 us -> 168 us (1.063)
  starting transfers between devices: 41.7 us -> 48.4 us
  local copies, waits for them, and re-layouts: 11.4 us -> 16 us
    ppermute x9, waiting for transfers between devices: 29.3 us -> 23.8 us  [shift(): lax.ppermute(block, 'etp', [(i, (i + step) % ways) for i in range(ways)])]
    unnamed x48 -> x88, local copies, waits for them, and re-layouts: 11.4 us -> 16 us
    ppermute x28 -> x25, waiting for transfers between devices: 22.5 us -> 26.5 us  [exchange(): return lax.ppermute(block, 'dp', [(i, i ^ bits) for i in range(ways)])]
    all_to_all x0 -> x1, starting transfers between devices: none -> 3.67 us  [shards(): lax.all_to_all(columns_of([after(dy_blocks[0], probs[0]), *dy_blocks[1:]]...]
    ppermute x9, starting transfers between devices: 20.4 us -> 23.5 us  [shift(): lax.ppermute(block, 'etp', [(i, (i + step) % ways) for i in range(ways)])]
    ppermute x28 -> x25, starting transfers between devices: 21.3 us -> 21.3 us  [exchange(): return lax.ppermute(block, 'dp', [(i, i ^ bits) for i in range(ways)])]
  transfers between devices with their start and end apart: 37 -> 35, of which waited for: 9 -> 15; matrix products, arithmetic and copies ran while one was open for 0% -> 0% of each run, Pallas kernels for 30% -> 21%
where the time goes in v7:
time: 168 us; the launch traced here: 167 us
  Pallas kernels  51.4 us (31%)
  waiting for transfers between devices  50.2 us (30%)
  starting transfers between devices  48.4 us (29%)
  local copies, waits for them, and re-layouts  16 us (10%)
    ppermute x25, waiting for transfers between devices, exchange(): return lax.ppermute(block, 'dp', [(i, i ^ bits) for i in range(ways)])  26.5 us
    ppermute x9, waiting for transfers between devices, shift(): lax.ppermute(block, 'etp', [(i, (i + step) % ways) for i in range(ways)])  23.8 us
    ppermute x9, starting transfers between devices, shift(): lax.ppermute(block, 'etp', [(i, (i + step) % ways) for i in range(ways)])  23.5 us
    ppermute x25, starting transfers between devices, exchange(): return lax.ppermute(block, 'dp', [(i, i ^ bits) for i in range(ways)])  21.3 us
    unnamed x88, local copies, waits for them, and re-layouts  16 us
    pallas_call x2, Pallas kernels, token_sums(): call(functools.partial(token_body, half, count), 'token_sums', struct((ro...  13.3 us
    pallas_call x2, Pallas kernels, forward(): call(functools.partial(forward_body, half, count), 'forward', [struct((ro...  11.1 us
    pallas_call x2, Pallas kernels, pair_sums(): call(functools.partial(pair_body, inv, len(parts), steps), 'pair_sums', [...  9.86 us
  transfers between devices with their start and end apart: 35, of which 15 were waited for; matrix products, arithmetic and copies ran while one was open for 0% of the time, Pallas kernels for 21%

profile of v7, /device:TPU:0, one launch (start us, length us, event | category | flops | bytes accessed | tf_op | source)
XLA Modules:
  0.0 167.1 jit_solution(14796680452756321957)
XLA Ops:
  3.5 3.1 %collective-permute-start = (bf16[32,3200]{1,0:T(8,128)(2,1)S(1)}, bf16[32,3200]{1,0:T(8,128)(2,1)S(1)}, u32[]{:S(2)}, u32[]{:S(2)}) collective-permute-start(bf16[32,3200]{1,0:T(8,128)(2,1)S(1)} %get-tuple-element.58.refs_0_), channel_id=1, source_target_pairs={{0,1},{1,2},{2,3},{3,0},{4,5},{5,6},{6,7},{7,4},{8,9},{9,10},{10,1... | collective-permute-start | bytes 614408 | tf_op jit(solution)/shard_map/ppermute | solution.py:52
  6.5 2.6 %collective-permute-start.1 = (bf16[32,3200]{1,0:T(8,128)(2,1)S(1)}, bf16[32,3200]{1,0:T(8,128)(2,1)S(1)}, u32[]{:S(2)}, u32[]{:S(2)}) collective-permute-start(bf16[32,3200]{1,0:T(8,128)(2,1)S(1)} %get-tuple-element.58.refs_0_), channel_id=1, source_target_pairs={{0,2},{1,3},{2,0},{3,1},{4,6},{5,7},{6,4},{7,5},{8,10},{9,11},{10,... | collective-permute-start | bytes 614408 | tf_op jit(solution)/shard_map/ppermute | solution.py:52
  10.5 4.1 %collective-permute-done.refs_1_ = bf16[32,3200]{1,0:T(8,128)(2,1)S(1)} collective-permute-done((bf16[32,3200]{1,0:T(8,128)(2,1)S(1)}, bf16[32,3200]{1,0:T(8,128)(2,1)S(1)}, u32[]{:S(2)}, u32[]{:S(2)}) %collective-permute-start) | collective-permute-done | bytes 204832 | tf_op jit(solution)/shard_map/ppermute | solution.py:52
  14.6 7.9 %collective-permute-done.1.refs_2_ = bf16[32,3200]{1,0:T(8,128)(2,1)S(1)} collective-permute-done((bf16[32,3200]{1,0:T(8,128)(2,1)S(1)}, bf16[32,3200]{1,0:T(8,128)(2,1)S(1)}, u32[]{:S(2)}, u32[]{:S(2)}) %collective-permute-start.1) | collective-permute-done | bytes 204832 | tf_op jit(solution)/shard_map/ppermute | solution.py:52
  22.6 1.5 collective-permute-start.3
  24.4 4.9 %collective-permute-start.5 = (bf16[32,3072]{1,0:T(8,128)(2,1)S(1)}, bf16[32,3072]{1,0:T(8,128)(2,1)S(1)}, u32[]{:S(2)}, u32[]{:S(2)}) collective-permute-start(bf16[32,3072]{1,0:T(8,128)(2,1)S(1)} %pack_dy.1.refs_0_), channel_id=1, source_target_pairs={{0,1},{1,2},{2,3},{3,0},{4,5},{5,6},{6,7},{7,4},{8,9},{9,10},{10,1... | collective-permute-start | bytes 589832 | tf_op jit(solution)/shard_map/ppermute | solution.py:52
  29.3 1.6 collective-permute-start.6
  33.3 5.5 %forward.3 = (bf16[128,1024]{1,0:T(8,128)(2,1)S(1)}, bf16[128,1024]{1,0:T(8,128)(2,1)S(1)}, f32[128,1024]{1,0:T(8,128)S(1)}, f32[128,1024]{1,0:T(8,128)S(1)}) custom-call(bf16[32,3200]{1,0:T(8,128)(2,1)S(1)} %get-tuple-element.58.refs_0_, bf16[32,3200]{1,0:T(8,128)(2,1)S(1)} %collective-permute-done.refs_1_, ...), custom_call_target="tpu_custom_call" | custom-call | flops 1610612736 | bytes 12582912 | tf_op jit(solution)/shard_map/forward/pallas_call | solution.py:213
  40.6 2.1 %collective-permute-done.6.refs_2_ = bf16[32,3072]{1,0:T(8,128)(2,1)S(1)} collective-permute-done((bf16[32,3072]{1,0:T(8,128)(2,1)S(1)}, bf16[32,3072]{1,0:T(8,128)(2,1)S(1)}, u32[]{:S(2)}, u32[]{:S(2)}) %collective-permute-start.6) | collective-permute-done | bytes 196640 | tf_op jit(solution)/shard_map/ppermute | solution.py:52
  42.6 5.5 %forward.2 = (bf16[128,1024]{1,0:T(8,128)(2,1)S(1)}, bf16[128,1024]{1,0:T(8,128)(2,1)S(1)}, f32[128,1024]{1,0:T(8,128)S(1)}, f32[128,1024]{1,0:T(8,128)S(1)}) custom-call(bf16[32,3200]{1,0:T(8,128)(2,1)S(1)} %get-tuple-element.58.refs_0_, bf16[32,3200]{1,0:T(8,128)(2,1)S(1)} %collective-permute-done.refs_1_, ...), custom_call_target="tpu_custom_call" | custom-call | flops 1610612736 | bytes 12582912 | tf_op jit(solution)/shard_map/forward/pallas_call | solution.py:213
  51.5 2.5 %collective-permute-start.10 = (bf16[128,768]{1,0:T(8,128)(2,1)S(1)}, bf16[128,768]{1,0:T(8,128)(2,1)S(1)}, u32[]{:S(2)}, u32[]{:S(2)}) collective-permute-start(bf16[128,768]{1,0:T(8,128)(2,1)S(1)} %get-tuple-element.60), channel_id=1, source_target_pairs={{0,24},{4,28},{8,16},{12,20},{16,8},{20,12},{24,0},{28,4},{1,25},{... | collective-permute-start | bytes 589832 | tf_op jit(solution)/shard_map/ppermute | solution.py:57
  54.0 7.7 %collective-permute-done.10.refs_3_ = bf16[128,768]{1,0:T(8,128)(2,1)S(1)} collective-permute-done((bf16[128,768]{1,0:T(8,128)(2,1)S(1)}, bf16[128,768]{1,0:T(8,128)(2,1)S(1)}, u32[]{:S(2)}, u32[]{:S(2)}) %collective-permute-start.10) | collective-permute-done | bytes 196640 | tf_op jit(solution)/shard_map/ppermute | solution.py:57
  63.1 3.4 %collective-permute-done.13.refs_3_ = bf16[128,1024]{1,0:T(8,128)(2,1)S(1)} collective-permute-done((bf16[128,1024]{1,0:T(8,128)(2,1)S(1)}, bf16[128,1024]{1,0:T(8,128)(2,1)S(1)}, u32[]{:S(2)}, u32[]{:S(2)}) %collective-permute-start.13) | collective-permute-done | bytes 262176 | tf_op jit(solution)/shard_map/ppermute | solution.py:57
  67.2 4.0 %backward.2 = (bf16[128,2048]{1,0:T(8,128)(2,1)S(1)}, f32[128,1]{1,0:T(8,128)S(1)}) custom-call(bf16[32,3072]{1,0:T(8,128)(2,1)S(1)} %pack_dy.1.refs_0_, bf16[32,3072]{1,0:T(8,128)(2,1)S(1)} %collective-permute-done.5.refs_1_, bf16[32,3072]{1,0:T(8,128)(2,1)S(1)} %collective-permute-done.6.refs_2_, bf16[32,3072]{1,0:T(8,128)(2,1)S(1)} %collective-permute-done.7.refs_3_, ...), custom_call_target="tpu_custom_call" | custom-call | flops 805306368 | bytes 7864320 | tf_op jit(solution)/shard_map/backward/pallas_call | solution.py:260
  71.2 1.6 collective-permute-start.15
  74.8 6.2 %token_sums.2.refs_0_ = f32[128,3072]{1,0:T(8,128)S(1)} custom-call(bf16[3072,2048]{1,0:T(8,128)(2,1)} %gate_hbm.3, bf16[3072,2048]{1,0:T(8,128)(2,1)} %up_hbm.3, bf16[128,2048]{1,0:T(8,128)(2,1)S(1)} %get-tuple-element.94.grad_ref.refs_0_), custom_call_target="tpu_custom_call" | custom-call | flops 1610612736 | bytes 12582912 | tf_op jit(solution)/shard_map/token_sums/pallas_call | solution.py:322
  81.1 8.4 %collective-permute-done.9.refs_7_ = bf16[128,1024]{1,0:T(8,128)(2,1)S(1)} collective-permute-done((bf16[128,1024]{1,0:T(8,128)(2,1)S(1)}, bf16[128,1024]{1,0:T(8,128)(2,1)S(1)}, u32[]{:S(2)}, u32[]{:S(2)}) %collective-permute-start.9) | collective-permute-done | bytes 262176 | tf_op jit(solution)/shard_map/ppermute | solution.py:57
  90.2 4.3 %backward.3 = (bf16[128,2048]{1,0:T(8,128)(2,1)S(1)}, f32[128,1]{1,0:T(8,128)S(1)}) custom-call(bf16[32,3072]{1,0:T(8,128)(2,1)S(1)} %pack_dy.1.refs_0_, bf16[32,3072]{1,0:T(8,128)(2,1)S(1)} %collective-permute-done.5.refs_1_, bf16[32,3072]{1,0:T(8,128)(2,1)S(1)} %collective-permute-done.6.refs_2_, bf16[32,3072]{1,0:T(8,128)(2,1)S(1)} %collective-permute-done.7.refs_3_, ...), custom_call_target="tpu_custom_call" | custom-call | flops 805306368 | bytes 7864320 | tf_op jit(solution)/shard_map/backward/pallas_call | solution.py:260
  94.5 1.6 collective-permute-start.22
  97.0 3.7 %all-to-all-start = ((bf16[4,128,768]{2,1,0:T(8,128)(2,1)}), bf16[4,128,768]{2,1,0:T(8,128)(2,1)S(1)}, u32[]{:S(2)}, u32[]{:S(2)}) async-start(bf16[4,128,768]{2,1,0:T(8,128)(2,1)} %columns.1), calls=%async_computation | async-start | bytes 1572864 | tf_op jit(solution)/shard_map/all_to_all | solution.py:583
  100.7 1.8 %collective-permute-start.21 = (bf16[128,2048]{1,0:T(8,128)(2,1)S(1)}, bf16[128,2048]{1,0:T(8,128)(2,1)}, u32[]{:S(2)}, u32[]{:S(2)}) collective-permute-start(bf16[128,2048]{1,0:T(8,128)(2,1)S(1)} %get-tuple-element.91.grad_ref.refs_0_), channel_id=1, source_target_pairs={{0,8},{4,12},{8,0},{12,4},{16,24},{20,28},{24,16},{28,20},{1,9},{5... | collective-permute-start | bytes 1572872 | tf_op jit(solution)/shard_map/ppermute | solution.py:57
  103.9 7.0 %token_sums.3 = (bf16[32,3200]{1,0:T(8,128)(2,1)S(1)}, bf16[32,3200]{1,0:T(8,128)(2,1)S(1)}, bf16[32,3200]{1,0:T(8,128)(2,1)}, bf16[32,3200]{1,0:T(8,128)(2,1)}) custom-call(bf16[3072,2048]{1,0:T(8,128)(2,1)} %gate_hbm.3, bf16[3072,2048]{1,0:T(8,128)(2,1)} %up_hbm.3, bf16[128,2048]{1,0:T(8,128)(2,1)S(1)} %get-tuple-element.91.grad_ref.refs_0_, ...), custom_call_target="tpu_custom_call" | custom-call | flops 1610612736 | bytes 12582912 | tf_op jit(solution)/shard_map/token_sums/pallas_call | solution.py:322
  111.7 2.1 %collective-permute-done.22.refs_2_ = bf16[128,2048]{1,0:T(8,128)(2,1)} collective-permute-done((bf16[128,2048]{1,0:T(8,128)(2,1)S(1)}, bf16[128,2048]{1,0:T(8,128)(2,1)}, u32[]{:S(2)}, u32[]{:S(2)}) %collective-permute-start.22) | collective-permute-done | bytes 524320 | tf_op jit(solution)/shard_map/ppermute | solution.py:57
  115.2 4.9 %collective-permute-start.17 = (bf16[32,3200]{1,0:T(8,128)(2,1)S(1)}, bf16[32,3200]{1,0:T(8,128)(2,1)S(1)}, u32[]{:S(2)}, u32[]{:S(2)}) collective-permute-start(bf16[32,3200]{1,0:T(8,128)(2,1)S(1)} %get-tuple-element.75), channel_id=1, source_target_pairs={{0,3},{1,0},{2,1},{3,2},{4,7},{5,4},{6,5},{7,6},{8,11},{9,8},{10,9... | collective-permute-start | bytes 614408 | tf_op jit(solution)/shard_map/ppermute | solution.py:52
  121.6 5.1 %collective-permute-done.17.refs_1_ = bf16[32,3200]{1,0:T(8,128)(2,1)S(1)} collective-permute-done((bf16[32,3200]{1,0:T(8,128)(2,1)S(1)}, bf16[32,3200]{1,0:T(8,128)(2,1)S(1)}, u32[]{:S(2)}, u32[]{:S(2)}) %collective-permute-start.17) | collective-permute-done | bytes 204832 | tf_op jit(solution)/shard_map/ppermute | solution.py:52
  126.7 2.8 %collective-permute-start.19 = (bf16[32,3200]{1,0:T(8,128)(2,1)}, bf16[32,3200]{1,0:T(8,128)(2,1)S(1)}, u32[]{:S(2)}, u32[]{:S(2)}) collective-permute-start(bf16[32,3200]{1,0:T(8,128)(2,1)} %get-tuple-element.77), channel_id=1, source_target_pairs={{0,1},{1,2},{2,3},{3,0},{4,5},{5,6},{6,7},{7,4},{8,9},{9,10},{10,1... | collective-permute-start | bytes 614408 | tf_op jit(solution)/shard_map/ppermute | solution.py:52
  131.1 3.4 %collective-permute-done.19.refs_3_ = bf16[32,3200]{1,0:T(8,128)(2,1)S(1)} collective-permute-done((bf16[32,3200]{1,0:T(8,128)(2,1)}, bf16[32,3200]{1,0:T(8,128)(2,1)S(1)}, u32[]{:S(2)}, u32[]{:S(2)}) %collective-permute-start.19) | collective-permute-done | bytes 204832 | tf_op jit(solution)/shard_map/ppermute | solution.py:52
  140.3 2.0 %theirs_sums.1 = bf16[384,2048]{1,0:T(8,128)(2,1)S(1)} custom-call(bf16[384,512]{1,0:T(8,128)(2,1)S(1)} %get-tuple-element.87.left_ref, bf16[128,1024]{1,0:T(8,128)(2,1)S(1)} %get-tuple-element.61.refs_0_, bf16[128,1024]{1,0:T(8,128)(2,1)S(1)} %collective-permute-done.11.refs_1_, bf16[128,1024]{1,0:T(8,128)(2,1)S(1)} %copy-done.1, ...), custom_call_target="tpu_custom_call" | custom-call | flops 805306368 | bytes 3670016 | tf_op jit(solution)/shard_map/theirs_sums/pallas_call | solution.py:457
  144.1 2.3 %collective-permute-done.25.other_ref = bf16[384,512]{1,0:T(8,128)(2,1)S(1)} collective-permute-done((bf16[384,512]{1,0:T(8,128)(2,1)S(1)}, bf16[384,512]{1,0:T(8,128)(2,1)S(1)}, u32[]{:S(2)}, u32[]{:S(2)}) %collective-permute-start.25) | collective-permute-done | bytes 393248 | tf_op jit(solution)/shard_map/ppermute | solution.py:57
  154.0 4.9 %pair_sums.2 = (bf16[384,2048]{1,0:T(8,128)(2,1)}, bf16[384,2048]{1,0:T(8,128)(2,1)}) custom-call(bf16[384,512]{1,0:T(8,128)(2,1)S(1)} %get-tuple-element.88.left_ref, bf16[384,512]{1,0:T(8,128)(2,1)S(1)} %collective-permute-done.25.other_ref, bf16[128,2048]{1,0:T(8,128)(2,1)S(1)} %copy-done.21, bf16[128,2048]{1,0:T(8,128)(2,1)S(1)} %copy-done.41, ...), custom_call_target="tpu_custom_call" | custom-call | flops 1610612736 | bytes 7340032 | tf_op jit(solution)/shard_map/pair_sums/pallas_call | solution.py:523
  159.0 3.2 %down_sums.1 = bf16[2048,384]{1,0:T(8,128)(2,1)} custom-call(bf16[384,512]{1,0:T(8,128)(2,1)S(1)} %get-tuple-element.83.left_ref, bf16[384,2048]{1,0:T(8,128)(2,1)S(1)} %collective-permute-done.24.got_ref, bf16[128,1024]{1,0:T(8,128)(2,1)S(1)} %get-tuple-element.61.refs_0_, bf16[128,1024]{1,0:T(8,128)(2,1)S(1)} %collective-permute-done.11.refs_1_, ...), custom_call_target="tpu_custom_call" | custom-call | flops 805306368 | bytes 5242880 | tf_op jit(solution)/shard_map/down_sums/pallas_call | solution.py:486
  162.2 4.9 %pair_sums.3 = (bf16[384,2048]{1,0:T(8,128)(2,1)}, bf16[384,2048]{1,0:T(8,128)(2,1)}) custom-call(bf16[384,512]{1,0:T(8,128)(2,1)S(1)} %get-tuple-element.88.left_ref, bf16[384,512]{1,0:T(8,128)(2,1)S(1)} %collective-permute-done.25.other_ref, ...), custom_call_target="tpu_custom_call", output_to_operand_aliasing={{0}: (10, {}), {1}: (11, {})} | custom-call | flops 1610612736 | bytes 7340032 | tf_op jit(solution)/shard_map/pair_sums/pallas_call | solution.py:523
  (143 shorter events, 39.5 us)
Async XLA Ops:
  3.5 11.1 %collective-permute-start = (bf16[32,3200]{1,0:T(8,128)(2,1)S(1)}, bf16[32,3200]{1,0:T(8,128)(2,1)S(1)}, u32[]{:S(2)}, u32[]{:S(2)}) collective-permute-start(bf16[32,3200]{1,0:T(8,128)(2,1)S(1)} %get-tuple-element.58.refs_0_), channel_id=1, source_target_pairs={{0,1},{1,2},{2,3},{3,0},{4,5},{5,6},{6,7},{7,4},{8,9},{9,10},{10,1... | collective-permute-start | bytes 614408 | tf_op jit(solution)/shard_map/ppermute | solution.py:52
  6.5 16.0 %collective-permute-start.1 = (bf16[32,3200]{1,0:T(8,128)(2,1)S(1)}, bf16[32,3200]{1,0:T(8,128)(2,1)S(1)}, u32[]{:S(2)}, u32[]{:S(2)}) collective-permute-start(bf16[32,3200]{1,0:T(8,128)(2,1)S(1)} %get-tuple-element.58.refs_0_), channel_id=1, source_target_pairs={{0,2},{1,3},{2,0},{3,1},{4,6},{5,7},{6,4},{7,5},{8,10},{9,11},{10,... | collective-permute-start | bytes 614408 | tf_op jit(solution)/shard_map/ppermute | solution.py:52
  9.1 13.4 %collective-permute-start.2 = (bf16[32,3200]{1,0:T(8,128)(2,1)S(1)}, bf16[32,3200]{1,0:T(8,128)(2,1)S(1)}, u32[]{:S(2)}, u32[]{:S(2)}) collective-permute-start(bf16[32,3200]{1,0:T(8,128)(2,1)S(1)} %get-tuple-element.58.refs_0_), channel_id=1, source_target_pairs={{0,3},{1,0},{2,1},{3,2},{4,7},{5,4},{6,5},{7,6},{8,11},{9,8},{10,9... | collective-permute-start | bytes 614408 | tf_op jit(solution)/shard_map/ppermute | solution.py:52
  22.6 16.2 %collective-permute-start.3 = (bf16[128,768]{1,0:T(8,128)(2,1)S(1)}, bf16[128,768]{1,0:T(8,128)(2,1)S(1)}, u32[]{:S(2)}, u32[]{:S(2)}) collective-permute-start(bf16[128,768]{1,0:T(8,128)(2,1)S(1)} %get-tuple-element.56), channel_id=1, source_target_pairs={{0,8},{4,12},{8,0},{12,4},{16,24},{20,28},{24,16},{28,20},{1,9},{5... | collective-permute-start | bytes 589832 | tf_op jit(solution)/shard_map/ppermute | solution.py:57
  24.4 16.2 %collective-permute-start.5 = (bf16[32,3072]{1,0:T(8,128)(2,1)S(1)}, bf16[32,3072]{1,0:T(8,128)(2,1)S(1)}, u32[]{:S(2)}, u32[]{:S(2)}) collective-permute-start(bf16[32,3072]{1,0:T(8,128)(2,1)S(1)} %pack_dy.1.refs_0_), channel_id=1, source_target_pairs={{0,1},{1,2},{2,3},{3,0},{4,5},{5,6},{6,7},{7,4},{8,9},{9,10},{10,1... | collective-permute-start | bytes 589832 | tf_op jit(solution)/shard_map/ppermute | solution.py:52
  29.3 13.3 %collective-permute-start.6 = (bf16[32,3072]{1,0:T(8,128)(2,1)S(1)}, bf16[32,3072]{1,0:T(8,128)(2,1)S(1)}, u32[]{:S(2)}, u32[]{:S(2)}) collective-permute-start(bf16[32,3072]{1,0:T(8,128)(2,1)S(1)} %pack_dy.1.refs_0_), channel_id=1, source_target_pairs={{0,2},{1,3},{2,0},{3,1},{4,6},{5,7},{6,4},{7,5},{8,10},{9,11},{10,... | collective-permute-start | bytes 589832 | tf_op jit(solution)/shard_map/ppermute | solution.py:52
  30.9 11.7 %collective-permute-start.7 = (bf16[32,3072]{1,0:T(8,128)(2,1)S(1)}, bf16[32,3072]{1,0:T(8,128)(2,1)S(1)}, u32[]{:S(2)}, u32[]{:S(2)}) collective-permute-start(bf16[32,3072]{1,0:T(8,128)(2,1)S(1)} %pack_dy.1.refs_0_), channel_id=1, source_target_pairs={{0,3},{1,0},{2,1},{3,2},{4,7},{5,4},{6,5},{7,6},{8,11},{9,8},{10,9... | collective-permute-start | bytes 589832 | tf_op jit(solution)/shard_map/ppermute | solution.py:52
  31.8 8.3 %collective-permute-start.4 = (bf16[128,768]{1,0:T(8,128)(2,1)S(1)}, bf16[128,768]{1,0:T(8,128)(2,1)S(1)}, u32[]{:S(2)}, u32[]{:S(2)}) collective-permute-start(bf16[128,768]{1,0:T(8,128)(2,1)S(1)} %get-tuple-element.57), channel_id=1, source_target_pairs={{0,16},{4,20},{8,24},{12,28},{16,0},{20,4},{24,8},{28,12},{1,17},{... | collective-permute-start | bytes 589832 | tf_op jit(solution)/shard_map/ppermute | solution.py:57
  39.5 11.5 %collective-permute-start.11 = (bf16[128,1024]{1,0:T(8,128)(2,1)S(1)}, bf16[128,1024]{1,0:T(8,128)(2,1)S(1)}, u32[]{:S(2)}, u32[]{:S(2)}) collective-permute-start(bf16[128,1024]{1,0:T(8,128)(2,1)S(1)} %get-tuple-element.61.refs_0_), channel_id=1, source_target_pairs={{0,8},{4,12},{8,0},{12,4},{16,24},{20,28},{24,16},{28,20},{1,9},{5... | collective-permute-start | bytes 786440 | tf_op jit(solution)/shard_map/ppermute | solution.py:57
  40.0 22.3 %collective-permute-start.12 = (bf16[128,1024]{1,0:T(8,128)(2,1)S(1)}, bf16[128,1024]{1,0:T(8,128)(2,1)S(1)}, u32[]{:S(2)}, u32[]{:S(2)}) collective-permute-start(bf16[128,1024]{1,0:T(8,128)(2,1)S(1)} %get-tuple-element.61.refs_0_), channel_id=1, source_target_pairs={{0,16},{4,20},{8,24},{12,28},{16,0},{20,4},{24,8},{28,12},{1,17},{... | collective-permute-start | bytes 786440 | tf_op jit(solution)/shard_map/ppermute | solution.py:57
  48.2 14.9 %collective-permute-start.14 = (bf16[128,1024]{1,0:T(8,128)(2,1)S(1)}, bf16[128,1024]{1,0:T(8,128)(2,1)S(1)}, u32[]{:S(2)}, u32[]{:S(2)}) collective-permute-start(bf16[128,1024]{1,0:T(8,128)(2,1)S(1)} %get-tuple-element.59.refs_4_), channel_id=1, source_target_pairs={{0,8},{4,12},{8,0},{12,4},{16,24},{20,28},{24,16},{28,20},{1,9},{5... | collective-permute-start | bytes 786440 | tf_op jit(solution)/shard_map/ppermute | solution.py:57
  48.8 14.3 %collective-permute-start.8 = (bf16[128,1024]{1,0:T(8,128)(2,1)S(1)}, bf16[128,1024]{1,0:T(8,128)(2,1)S(1)}, u32[]{:S(2)}, u32[]{:S(2)}) collective-permute-start(bf16[128,1024]{1,0:T(8,128)(2,1)S(1)} %get-tuple-element.59.refs_4_), channel_id=1, source_target_pairs={{0,16},{4,20},{8,24},{12,28},{16,0},{20,4},{24,8},{28,12},{1,17},{... | collective-permute-start | bytes 786440 | tf_op jit(solution)/shard_map/ppermute | solution.py:57
  51.0 15.4 %collective-permute-start.13 = (bf16[128,1024]{1,0:T(8,128)(2,1)S(1)}, bf16[128,1024]{1,0:T(8,128)(2,1)S(1)}, u32[]{:S(2)}, u32[]{:S(2)}) collective-permute-start(bf16[128,1024]{1,0:T(8,128)(2,1)S(1)} %collective-permute-done.11.refs_1_), channel_id=1, source_target_pairs={{0,16},{4,20},{8,24},{12,28},{16,0},{20,4},{24,8},{28,12},{1,17},{... | collective-permute-start | bytes 786440 | tf_op jit(solution)/shard_map/ppermute | solution.py:57
  51.5 10.1 %collective-permute-start.10 = (bf16[128,768]{1,0:T(8,128)(2,1)S(1)}, bf16[128,768]{1,0:T(8,128)(2,1)S(1)}, u32[]{:S(2)}, u32[]{:S(2)}) collective-permute-start(bf16[128,768]{1,0:T(8,128)(2,1)S(1)} %get-tuple-element.60), channel_id=1, source_target_pairs={{0,24},{4,28},{8,16},{12,20},{16,8},{20,12},{24,0},{28,4},{1,25},{... | collective-permute-start | bytes 589832 | tf_op jit(solution)/shard_map/ppermute | solution.py:57
  71.2 19.0 %collective-permute-start.15 = (bf16[128,2048]{1,0:T(8,128)(2,1)S(1)}, bf16[128,2048]{1,0:T(8,128)(2,1)S(1)}, u32[]{:S(2)}, u32[]{:S(2)}) collective-permute-start(bf16[128,2048]{1,0:T(8,128)(2,1)S(1)} %get-tuple-element.94.grad_ref.refs_0_), channel_id=1, source_target_pairs={{0,8},{4,12},{8,0},{12,4},{16,24},{20,28},{24,16},{28,20},{1,9},{5... | collective-permute-start | bytes 1572872 | tf_op jit(solution)/shard_map/ppermute | solution.py:57
  72.8 17.4 %collective-permute-start.16 = (bf16[128,2048]{1,0:T(8,128)(2,1)S(1)}, bf16[128,2048]{1,0:T(8,128)(2,1)S(1)}, u32[]{:S(2)}, u32[]{:S(2)}) collective-permute-start(bf16[128,2048]{1,0:T(8,128)(2,1)S(1)} %get-tuple-element.94.grad_ref.refs_0_), channel_id=1, source_target_pairs={{0,16},{4,20},{8,24},{12,28},{16,0},{20,4},{24,8},{28,12},{1,17},{... | collective-permute-start | bytes 1572872 | tf_op jit(solution)/shard_map/ppermute | solution.py:57
  74.3 15.2 %collective-permute-start.9 = (bf16[128,1024]{1,0:T(8,128)(2,1)S(1)}, bf16[128,1024]{1,0:T(8,128)(2,1)S(1)}, u32[]{:S(2)}, u32[]{:S(2)}) collective-permute-start(bf16[128,1024]{1,0:T(8,128)(2,1)S(1)} %collective-permute-done.8.refs_6_), channel_id=1, source_target_pairs={{0,8},{4,12},{8,0},{12,4},{16,24},{20,28},{24,16},{28,20},{1,9},{5... | collective-permute-start | bytes 786440 | tf_op jit(solution)/shard_map/ppermute | solution.py:57
  94.5 19.2 %collective-permute-start.22 = (bf16[128,2048]{1,0:T(8,128)(2,1)S(1)}, bf16[128,2048]{1,0:T(8,128)(2,1)}, u32[]{:S(2)}, u32[]{:S(2)}) collective-permute-start(bf16[128,2048]{1,0:T(8,128)(2,1)S(1)} %get-tuple-element.91.grad_ref.refs_0_), channel_id=1, source_target_pairs={{0,16},{4,20},{8,24},{12,28},{16,0},{20,4},{24,8},{28,12},{1,17},{... | collective-permute-start | bytes 1572872 | tf_op jit(solution)/shard_map/ppermute | solution.py:57
  97.0 32.5 %all-to-all-start = ((bf16[4,128,768]{2,1,0:T(8,128)(2,1)}), bf16[4,128,768]{2,1,0:T(8,128)(2,1)S(1)}, u32[]{:S(2)}, u32[]{:S(2)}) async-start(bf16[4,128,768]{2,1,0:T(8,128)(2,1)} %columns.1), calls=%async_computation | async-start | bytes 1572864 | tf_op jit(solution)/shard_map/all_to_all | solution.py:583
  100.7 33.8 %collective-permute-start.21 = (bf16[128,2048]{1,0:T(8,128)(2,1)S(1)}, bf16[128,2048]{1,0:T(8,128)(2,1)}, u32[]{:S(2)}, u32[]{:S(2)}) collective-permute-start(bf16[128,2048]{1,0:T(8,128)(2,1)S(1)} %get-tuple-element.91.grad_ref.refs_0_), channel_id=1, source_target_pairs={{0,8},{4,12},{8,0},{12,4},{16,24},{20,28},{24,16},{28,20},{1,9},{5... | collective-permute-start | bytes 1572872 | tf_op jit(solution)/shard_map/ppermute | solution.py:57
  102.5 32.0 %collective-permute-start.20 = (bf16[128,2048]{1,0:T(8,128)(2,1)}, bf16[128,2048]{1,0:T(8,128)(2,1)}, u32[]{:S(2)}, u32[]{:S(2)}) collective-permute-start(bf16[128,2048]{1,0:T(8,128)(2,1)} %copy-done.40), channel_id=1, source_target_pairs={{0,16},{4,20},{8,24},{12,28},{16,0},{20,4},{24,8},{28,12},{1,17},{... | collective-permute-start | bytes 1572872 | tf_op jit(solution)/shard_map/ppermute | solution.py:57
  113.7 20.7 %collective-permute-start.23 = (bf16[128,2048]{1,0:T(8,128)(2,1)}, bf16[128,2048]{1,0:T(8,128)(2,1)S(1)}, u32[]{:S(2)}, u32[]{:S(2)}) collective-permute-start(bf16[128,2048]{1,0:T(8,128)(2,1)} %collective-permute-done.22.refs_2_), channel_id=1, source_target_pairs={{0,8},{4,12},{8,0},{12,4},{16,24},{20,28},{24,16},{28,20},{1,9},{5... | collective-permute-start | bytes 1572872 | tf_op jit(solution)/shard_map/ppermute | solution.py:57
  115.2 11.4 %collective-permute-start.17 = (bf16[32,3200]{1,0:T(8,128)(2,1)S(1)}, bf16[32,3200]{1,0:T(8,128)(2,1)S(1)}, u32[]{:S(2)}, u32[]{:S(2)}) collective-permute-start(bf16[32,3200]{1,0:T(8,128)(2,1)S(1)} %get-tuple-element.75), channel_id=1, source_target_pairs={{0,3},{1,0},{2,1},{3,2},{4,7},{5,4},{6,5},{7,6},{8,11},{9,8},{10,9... | collective-permute-start | bytes 614408 | tf_op jit(solution)/shard_map/ppermute | solution.py:52
  120.2 10.9 %collective-permute-start.18 = (bf16[32,3200]{1,0:T(8,128)(2,1)}, bf16[32,3200]{1,0:T(8,128)(2,1)S(1)}, u32[]{:S(2)}, u32[]{:S(2)}) collective-permute-start(bf16[32,3200]{1,0:T(8,128)(2,1)} %get-tuple-element.76), channel_id=1, source_target_pairs={{0,2},{1,3},{2,0},{3,1},{4,6},{5,7},{6,4},{7,5},{8,10},{9,11},{10,... | collective-permute-start | bytes 614408 | tf_op jit(solution)/shard_map/ppermute | solution.py:52
  126.7 7.8 %collective-permute-start.19 = (bf16[32,3200]{1,0:T(8,128)(2,1)}, bf16[32,3200]{1,0:T(8,128)(2,1)S(1)}, u32[]{:S(2)}, u32[]{:S(2)}) collective-permute-start(bf16[32,3200]{1,0:T(8,128)(2,1)} %get-tuple-element.77), channel_id=1, source_target_pairs={{0,1},{1,2},{2,3},{3,0},{4,5},{5,6},{6,7},{7,4},{8,9},{9,10},{10,1... | collective-permute-start | bytes 614408 | tf_op jit(solution)/shard_map/ppermute | solution.py:52
  142.3 16.6 %collective-permute-start.24 = (bf16[384,2048]{1,0:T(8,128)(2,1)S(1)}, bf16[384,2048]{1,0:T(8,128)(2,1)S(1)}, u32[]{:S(2)}, u32[]{:S(2)}) collective-permute-start(bf16[384,2048]{1,0:T(8,128)(2,1)S(1)} %theirs_sums.1), channel_id=1, source_target_pairs={{0,4},{4,0},{8,12},{12,8},{16,20},{20,16},{24,28},{28,24},{1,5},{5... | collective-permute-start | bytes 4718600 | tf_op jit(solution)/shard_map/ppermute | solution.py:57
  143.6 4.3 %collective-permute-start.32 = (bf16[128,2048]{1,0:T(8,128)(2,1)S(1)}, bf16[128,2048]{1,0:T(8,128)(2,1)S(1)}, u32[]{:S(2)}, u32[]{:S(2)}) collective-permute-start(bf16[128,2048]{1,0:T(8,128)(2,1)S(1)} %copy-done.43), channel_id=1, source_target_pairs={{0,4},{4,0},{8,12},{12,8},{16,20},{20,16},{24,28},{28,24},{1,5},{5... | collective-permute-start | bytes 1572872 | tf_op jit(solution)/shard_map/ppermute | solution.py:57
  144.0 5.3 %collective-permute-start.30 = (bf16[128,2048]{1,0:T(8,128)(2,1)S(1)}, bf16[128,2048]{1,0:T(8,128)(2,1)S(1)}, u32[]{:S(2)}, u32[]{:S(2)}) collective-permute-start(bf16[128,2048]{1,0:T(8,128)(2,1)S(1)} %copy-done.21), channel_id=1, source_target_pairs={{0,4},{4,0},{8,12},{12,8},{16,20},{20,16},{24,28},{28,24},{1,5},{5... | collective-permute-start | bytes 1572872 | tf_op jit(solution)/shard_map/ppermute | solution.py:57
  147.1 15.1 %collective-permute-start.28 = (bf16[128,2048]{1,0:T(8,128)(2,1)}, bf16[128,2048]{1,0:T(8,128)(2,1)S(1)}, u32[]{:S(2)}, u32[]{:S(2)}) collective-permute-start(bf16[128,2048]{1,0:T(8,128)(2,1)} %collective-permute-done.22.refs_2_), channel_id=1, source_target_pairs={{0,4},{4,0},{8,12},{12,8},{16,20},{20,16},{24,28},{28,24},{1,5},{5... | collective-permute-start | bytes 1572872 | tf_op jit(solution)/shard_map/ppermute | solution.py:57
  147.9 14.3 %collective-permute-start.27 = (bf16[128,2048]{1,0:T(8,128)(2,1)}, bf16[128,2048]{1,0:T(8,128)(2,1)S(1)}, u32[]{:S(2)}, u32[]{:S(2)}) collective-permute-start(bf16[128,2048]{1,0:T(8,128)(2,1)} %collective-permute-done.21.refs_1_), channel_id=1, source_target_pairs={{0,4},{4,0},{8,12},{12,8},{16,20},{20,16},{24,28},{28,24},{1,5},{5... | collective-permute-start | bytes 1572872 | tf_op jit(solution)/shard_map/ppermute | solution.py:57
  149.4 12.8 %collective-permute-start.26 = (bf16[128,2048]{1,0:T(8,128)(2,1)S(1)}, bf16[128,2048]{1,0:T(8,128)(2,1)S(1)}, u32[]{:S(2)}, u32[]{:S(2)}) collective-permute-start(bf16[128,2048]{1,0:T(8,128)(2,1)S(1)} %get-tuple-element.91.grad_ref.refs_0_), channel_id=1, source_target_pairs={{0,4},{4,0},{8,12},{12,8},{16,20},{20,16},{24,28},{28,24},{1,5},{5... | collective-permute-start | bytes 1572872 | tf_op jit(solution)/shard_map/ppermute | solution.py:57
  149.6 12.6 %collective-permute-start.29 = (bf16[128,2048]{1,0:T(8,128)(2,1)S(1)}, bf16[128,2048]{1,0:T(8,128)(2,1)S(1)}, u32[]{:S(2)}, u32[]{:S(2)}) collective-permute-start(bf16[128,2048]{1,0:T(8,128)(2,1)S(1)} %collective-permute-done.23.refs_3_), channel_id=1, source_target_pairs={{0,4},{4,0},{8,12},{12,8},{16,20},{20,16},{24,28},{28,24},{1,5},{5... | collective-permute-start | bytes 1572872 | tf_op jit(solution)/shard_map/ppermute | solution.py:57
  (47 other events, 195.6 us)
